TPU v7x, 32 devices: a whole 2x2x4 slice. The times are simulated.
32 devices in a mesh: groups: 2 (over y), blk: 4 (over z), kv: 2 (over x), pair: 2 (over core).
Axes of the slice: x: 2, y: 2, z: 4, core: 2. Of those that a mesh axis runs over, the one named last changes fastest.
Arguments:
- queries: bfloat16 [128, 128, 128], P(('groups', 'blk'), ('kv', 'pair')), parts along dimension 0, may hold values from -15 to 15
- root_keys: bfloat16 [16384, 8, 128], P(('groups', 'blk', 'pair'), 'kv'), parts along dimension 0, may hold values from -4 to 4
- root_values: bfloat16 [16384, 8, 128], P(('groups', 'blk', 'pair'), 'kv'), parts along dimension 0, may hold values from -6 to 6
- branch_keys: bfloat16 [16, 2048, 8, 128], P(('groups', 'blk'), 'pair', 'kv'), parts along dimension 0, may hold values from -4 to 4
- branch_values: bfloat16 [16, 2048, 8, 128], P(('groups', 'blk'), 'pair', 'kv'), parts along dimension 0, may hold values from -6 to 6
- request_branch: int32 [128], P(('groups', 'blk')), parts along dimension 0, may hold values from 0 to 7, as said below
- seen_tokens: int32 [128], P(('groups', 'blk')), parts along dimension 0, may hold values from 1 to 2048, as said below
Outputs:
- attended: bfloat16 [128, 128, 128], P(('groups', 'blk'), ('kv', 'pair')), parts along dimension 0
There are 2 independent parts, one for each index of `groups`. A program takes and returns all parts, laid end to end along the dimension named above; each array names one. Nothing has to cross between parts.
Inputs may be any that keep to these rules, and one draw needn't show every extreme that they name: Within a part, request r belongs to one of the 2 branches stored on its own index of blk: request_branch[r] // 2 == r // 16, with r and the branch counted within the part. Every branch has at least one request. `seen_tokens`: on every index of blk some request sees all 2048 positions of its branch.
All inputs are finite; a program needn't handle non-finite values.
Results may differ from a plain program's by a relative error of at most 0.04.
Values may be sent and summed in bfloat16 or wider, within the bound.
No kernel may reach another device: no remote copies, remote signals or barrier semaphores. Data moves between devices by JAX's collectives and lax.ppermute only.
A program may use at most 64 MiB of HBM per device.

v0:
```python
import math

import jax
import jax.numpy as jnp
from jax import lax
from jax.sharding import PartitionSpec as P

masked_floor = -1e30


def partner(value, axis, apart):
    return lax.ppermute(value, axis, [(i, i ^ 1 << apart) for i in range(lax.axis_size(axis))])


def combine_parts(first_part, second_part):
    sums_one, maxima_one, totals_one = first_part
    sums_two, maxima_two, totals_two = second_part
    largest = jnp.maximum(maxima_one, maxima_two)
    scale_one = jnp.exp(maxima_one - largest)
    scale_two = jnp.exp(maxima_two - largest)
    merged_sums = sums_one * scale_one[..., None] + sums_two * scale_two[..., None]
    return (merged_sums, largest, totals_one * scale_one + totals_two * scale_two)


def merge_sources(partials):
    sums, maxima, totals = partials
    largest = jnp.max(maxima, axis=0)
    factor = jnp.exp(maxima - largest[None])
    return (jnp.sum(sums * factor[..., None], axis=0), largest, jnp.sum(totals * factor, axis=0))


def pick_index(array_in, index_value, dim_index):
    return lax.dynamic_index_in_dim(array_in, index_value, dim_index, keepdims=False)


def local(queries, root_keys, root_values, branch_keys, branch_values, request_branch, seen_tokens):
    local_requests, local_heads, head_width = queries.shape
    root_tokens, shared_local, _ = root_keys.shape
    local_branches, half_tokens, _, _ = branch_keys.shape
    block_devices = lax.axis_size("blk")
    pair_devices = lax.axis_size("pair")
    shared_half = shared_local // pair_devices
    group_size = local_heads // shared_half
    row_count = local_requests * local_heads
    score_scale = 1.0 / math.sqrt(head_width)
    pair_index = lax.axis_index("pair")
    other_index = 1 - pair_index
    keys_split = root_keys.reshape(root_tokens, pair_devices, shared_half, head_width)
    values_split = root_values.reshape(root_tokens, pair_devices, shared_half, head_width)
    bkeys_split = branch_keys.reshape(
        local_branches, half_tokens, pair_devices, shared_half, head_width
    )
    bvalues_split = branch_values.reshape(
        local_branches, half_tokens, pair_devices, shared_half, head_width
    )
    received = partner(
        (
            pick_index(keys_split, other_index, 1),
            pick_index(values_split, other_index, 1),
            pick_index(bkeys_split, other_index, 2),
            pick_index(bvalues_split, other_index, 2),
        ),
        "pair",
        0,
    )
    keys_mine = jnp.concatenate([pick_index(keys_split, pair_index, 1), received[0]], axis=0)
    values_mine = jnp.concatenate([pick_index(values_split, pair_index, 1), received[1]], axis=0)
    bkeys_mine = jnp.concatenate([pick_index(bkeys_split, pair_index, 2), received[2]], axis=1)
    bvalues_mine = jnp.concatenate([pick_index(bvalues_split, pair_index, 2), received[3]], axis=1)
    gathered = lax.all_gather(queries, "blk", axis=0, tiled=True)
    query_blocks = gathered.reshape(
        block_devices, local_requests, shared_half, group_size, head_width
    )

    def root_partial_mine(query_block):
        scores = (
            jnp.einsum("rkgd,tkd->krgt", query_block, keys_mine, preferred_element_type=jnp.float32)
            * score_scale
        )
        maxima = jnp.max(scores, axis=-1)
        weights = jnp.exp(scores - maxima[..., None])
        totals = jnp.sum(weights, axis=-1)
        sums = jnp.einsum(
            "krgt,tkd->rkgd",
            weights.astype(jnp.bfloat16),
            values_mine,
            preferred_element_type=jnp.float32,
        )
        return (sums, jnp.transpose(maxima, (1, 0, 2)), jnp.transpose(totals, (1, 0, 2)))

    mine_sums, mine_maxima, mine_totals = lax.map(root_partial_mine, query_blocks)
    mine_sums = mine_sums.reshape(block_devices, row_count, head_width)
    mine_maxima = mine_maxima.reshape(block_devices, row_count)
    mine_totals = mine_totals.reshape(block_devices, row_count)
    merged = merge_sources(
        (
            lax.all_to_all(mine_sums, "blk", split_axis=0, concat_axis=0, tiled=True),
            lax.all_to_all(mine_maxima, "blk", split_axis=0, concat_axis=0, tiled=True),
            lax.all_to_all(mine_totals, "blk", split_axis=0, concat_axis=0, tiled=True),
        )
    )
    full_tokens = 2 * half_tokens
    key_count = local_branches * full_tokens
    keys_flat = bkeys_mine.reshape(key_count, shared_half, head_width)
    values_flat = bvalues_mine.reshape(key_count, shared_half, head_width)
    key_slot = jnp.arange(key_count, dtype=jnp.int32)
    within = key_slot % full_tokens
    position = jnp.where(
        within < half_tokens,
        pair_index * half_tokens + within,
        other_index * half_tokens + within - half_tokens,
    )
    visible = ((request_branch % local_branches)[:, None] == (key_slot // full_tokens)[None, :]) & (
        position[None, :] < seen_tokens[:, None]
    )
    visible_mask = visible[None, :, None, :]
    own_queries = queries.reshape(local_requests, shared_half, group_size, head_width)
    scores = (
        jnp.einsum("rkgd,tkd->krgt", own_queries, keys_flat, preferred_element_type=jnp.float32)
        * score_scale
    )
    scores = jnp.where(visible_mask, scores, masked_floor)
    maxima = jnp.max(scores, axis=-1)
    weights = jnp.where(visible_mask, jnp.exp(scores - maxima[..., None]), 0.0)
    totals = jnp.sum(weights, axis=-1)
    own_sums = jnp.einsum(
        "krgt,tkd->rkgd",
        weights.astype(jnp.bfloat16),
        values_flat,
        preferred_element_type=jnp.float32,
    ).reshape(row_count, head_width)
    own_maxima = jnp.transpose(maxima, (1, 0, 2)).reshape(row_count)
    own_totals = jnp.transpose(totals, (1, 0, 2)).reshape(row_count)
    merged = combine_parts(merged, (own_sums, own_maxima, own_totals))
    final_sums, final_maxima, final_totals = merged
    attended = (final_sums / final_totals[:, None]).astype(jnp.bfloat16)
    return attended.reshape(local_requests, local_heads, head_width)


def solution(mesh):
    in_specs = (
        P(("groups", "blk"), ("kv", "pair"), None),
        P(("groups", "blk", "pair"), "kv", None),
        P(("groups", "blk", "pair"), "kv", None),
        P(("groups", "blk"), "pair", "kv", None),
        P(("groups", "blk"), "pair", "kv", None),
        P(("groups", "blk")),
        P(("groups", "blk")),
    )
    out_specs = P(("groups", "blk"), ("kv", "pair"), None)
    return jax.shard_map(local, mesh=mesh, in_specs=in_specs, out_specs=out_specs, check_vma=False)
```

profile of v0, /device:TPU:0, one launch (start us, length us, event | category | flops | bytes accessed | tf_op | source)
XLA Modules:
  0.0 95.8 jit_solution(6873006721559958175)
XLA Ops:
  0.0 4.1 %constant_dynamic-slice_fusion.6 = (bf16[1024,1,2,128]{3,2,1,0:T(2,128)(2,1)}, bf16[1024,1,2,128]{3,2,1,0:T(2,128)(2,1)S(1)}, bf16[1024,1,2,128]{3,2,1,0:T(2,128)(2,1)S(1)}, bf16[1024,1,2,128]{3,2,1,0:T(2,128)(2,1)}) fusion(bf16[1024,2,2,128]{3,2,1,0:T(2,128)(2,1)} %bitcast.128, s32[]{:T(128)S(6)} %select_n.58, s32[]{:T(128)S(6)} %select_n.59, ...), kind=kLoop, calls=%fused_computation.77 | loop fusion | bytes 4194312 | tf_op jit(solution)/shard_map/jit(dynamic_index_in_dim)/dynamic_slice | solution.py:33
  6.3 3.7 %constant_dynamic-slice_fusion.2 = (bf16[2,1024,1,2,128]{4,3,2,1,0:T(2,128)(2,1)}, bf16[2,1024,1,2,128]{4,3,2,1,0:T(2,128)(2,1)S(1)}, bf16[2,1024,1,2,128]{4,3,2...) fusion(bf16[2,1024,2,2,128]{4,3,2,1,0:T(2,128)(2,1)S(1)} %bitcast.121, s32[]{:T(128)S(6)} %select_n.58, s32[]{:T(128)S(6)} %select_n.59, ...), kind=kLoop, calls=%fused_computation.73 | loop fusion | bytes 8388616 | tf_op jit(solution)/shard_map/jit(dynamic_index_in_dim)/dynamic_slice | solution.py:33
  10.0 1.2 %copy.110 = bf16[2,1024,1,2,128]{4,1,0,3,2:T(8,128)(2,1)} copy(bf16[2,1024,1,2,128]{4,3,2,1,0:T(2,128)(2,1)S(1)} %get-tuple-element.108) | data formatting | bytes 2097152 | tf_op jit(solution)/shard_map/jit(dynamic_index_in_dim)/dynamic_slice | solution.py:33
  11.7 1.2 %copy.108 = bf16[2,1024,1,2,128]{4,1,0,3,2:T(8,128)(2,1)} copy(bf16[2,1024,1,2,128]{4,3,2,1,0:T(2,128)(2,1)S(1)} %get-tuple-element.101) | data formatting | bytes 2097152 | tf_op jit(solution)/shard_map/jit(dynamic_index_in_dim)/dynamic_slice | solution.py:33
  12.9 18.0 %all_gather.3 = bf16[64,32,128]{2,1,0:T(8,128)(2,1)} all-gather(bf16[16,32,128]{2,1,0:T(8,128)(2,1)S(1)} %copy-done.5), channel_id=1, replica_groups=mesh['groups'=2,'blk'=4,'kv'=2,'pair'=2] {'blk'}, dimensions={0}, use_global_device_ids=true | all-gather | bytes 655360 | tf_op jit(solution)/shard_map/all_gather | solution.py:70
  31.1 1.1 %pad_maximum_fusion.2 = bf16[2048,2,128]{2,0,1:T(8,128)(2,1)S(1)} fusion(bf16[1024,2,128]{2,0,1:T(8,128)(2,1)} %collective-permute-done, bf16[1024,2,128]{2,0,1:T(8,128)(2,1)S(1)} %bitcast.126), kind=kLoop, calls=%fused_computation.27 | loop fusion | flops 2097152 | bytes 2097152 | tf_op jit(solution)/shard_map/concatenate | solution.py:66
  32.2 1.1 %pad_maximum_fusion.3 = bf16[2048,2,128]{2,0,1:T(8,128)(2,1)S(1)} fusion(bf16[1024,2,128]{2,0,1:T(8,128)(2,1)} %collective-permute-done.1, bf16[1024,2,128]{2,0,1:T(8,128)(2,1)S(1)} %bitcast.125), kind=kLoop, calls=%fused_computation.28 | loop fusion | flops 2097152 | bytes 2097152 | tf_op jit(solution)/shard_map/concatenate | solution.py:67
  33.4 17.1 %while.14 = (s32[]{:T(128)}, f32[4,16,2,16,128]{4,3,2,1,0:T(8,128)}, f32[4,16,2,16]{3,2,1,0:T(2,128)S(1)}, f32[4,16,2,16]{3,2,1,0:T(2,128)S(1)}, bf16[4,16,2,16,...) while((s32[]{:T(128)}, ...), condition=%wide.region_3.4_spmd, body=%wide.region_0.3_spmd.sunk | while | flops 545258496 | bytes 15671401 | solution.py:91
  33.4 1.7 %multiply_reduce_fusion.3 = (f32[2,16,16]{2,1,0:T(8,128)S(1)}, f32[2,16,16,2048]{3,2,1,0:T(8,128)S(1)}) fusion(bf16[2048,2,128]{2,0,1:T(8,128)(2,1)S(1)} %get-tuple-element.186, bf16[4,16,2,16,128]{4,3,2,1,0:T(8,128)(2,1)} %get-tuple-element.185, s32[]{:T(128)S(6)} %copy.129), kind=kOutput, calls=%fused_computation.1.clone.1 | convolution fusion | flops 270532096 | bytes 5376004 | tf_op jit(solution)/shard_map/while/body/eval_jaxpr/rkgd,tkd->krgt/dot_general | solution.py:77
  37.7 1.7 %multiply_reduce_fusion.3 = (f32[2,16,16]{2,1,0:T(8,128)S(1)}, f32[2,16,16,2048]{3,2,1,0:T(8,128)S(1)}) fusion(bf16[2048,2,128]{2,0,1:T(8,128)(2,1)S(1)} %get-tuple-element.186, bf16[4,16,2,16,128]{4,3,2,1,0:T(8,128)(2,1)} %get-tuple-element.185, s32[]{:T(128)S(6)} %copy.129), kind=kOutput, calls=%fused_computation.1.clone.1 | convolution fusion | flops 270532096 | bytes 5376004 | tf_op jit(solution)/shard_map/while/body/eval_jaxpr/rkgd,tkd->krgt/dot_general | solution.py:77
  42.0 1.7 %multiply_reduce_fusion.3 = (f32[2,16,16]{2,1,0:T(8,128)S(1)}, f32[2,16,16,2048]{3,2,1,0:T(8,128)S(1)}) fusion(bf16[2048,2,128]{2,0,1:T(8,128)(2,1)S(1)} %get-tuple-element.186, bf16[4,16,2,16,128]{4,3,2,1,0:T(8,128)(2,1)} %get-tuple-element.185, s32[]{:T(128)S(6)} %copy.129), kind=kOutput, calls=%fused_computation.1.clone.1 | convolution fusion | flops 270532096 | bytes 5376004 | tf_op jit(solution)/shard_map/while/body/eval_jaxpr/rkgd,tkd->krgt/dot_general | solution.py:77
  46.2 1.7 %multiply_reduce_fusion.3 = (f32[2,16,16]{2,1,0:T(8,128)S(1)}, f32[2,16,16,2048]{3,2,1,0:T(8,128)S(1)}) fusion(bf16[2048,2,128]{2,0,1:T(8,128)(2,1)S(1)} %get-tuple-element.186, bf16[4,16,2,16,128]{4,3,2,1,0:T(8,128)(2,1)} %get-tuple-element.185, s32[]{:T(128)S(6)} %copy.129), kind=kOutput, calls=%fused_computation.1.clone.1 | convolution fusion | flops 270532096 | bytes 5376004 | tf_op jit(solution)/shard_map/while/body/eval_jaxpr/rkgd,tkd->krgt/dot_general | solution.py:77
  51.2 5.5 %all-to-all-start.1 = ((f32[4,1,512]{2,1,0:T(1,128)}), f32[4,1,512]{2,1,0:T(1,128)S(1)}, u32[]{:S(2)}, u32[]{:S(2)}) async-start(f32[4,1,512]{2,1,0:T(1,128)} %all_to_all.26), calls=%async_computation.1 | async-start | bytes 16384 | tf_op jit(solution)/shard_map/all_to_all | solution.py:98
  57.5 4.8 %all-to-all-done.1 = f32[4,1,512]{2,1,0:T(1,128)S(1)} async-done(((f32[4,1,512]{2,1,0:T(1,128)}), f32[4,1,512]{2,1,0:T(1,128)S(1)}, u32[]{:S(2)}, u32[]{:S(2)}) %all-to-all-start.1) | async-done | bytes 8224 | tf_op jit(solution)/shard_map/all_to_all | solution.py:98
  62.3 3.2 %all-to-all-start.2 = ((f32[4,1,512]{2,1,0:T(1,128)}), f32[4,1,512]{2,1,0:T(1,128)S(1)}, u32[]{:S(2)}, u32[]{:S(2)}) async-start(f32[4,1,512]{2,1,0:T(1,128)} %all_to_all.23), calls=%async_computation.2 | async-start | bytes 16384 | tf_op jit(solution)/shard_map/all_to_all | solution.py:99
  65.7 1.4 %copy.109 = bf16[2,1024,1,2,128]{4,1,0,3,2:T(8,128)(2,1)S(1)} copy(bf16[2,1024,1,2,128]{4,3,2,1,0:T(2,128)(2,1)} %get-tuple-element.100) | data formatting | bytes 2097152 | tf_op jit(solution)/shard_map/jit(dynamic_index_in_dim)/dynamic_slice | solution.py:33
  67.3 3.8 %all-to-all-done.2 = f32[4,1,512]{2,1,0:T(1,128)S(1)} async-done(((f32[4,1,512]{2,1,0:T(1,128)}), f32[4,1,512]{2,1,0:T(1,128)S(1)}, u32[]{:S(2)}, u32[]{:S(2)}) %all-to-all-start.2) | async-done | bytes 8224 | tf_op jit(solution)/shard_map/all_to_all | solution.py:99
  71.1 3.7 %all-to-all-start = ((f32[4,512,128]{2,1,0:T(8,128)}), f32[4,512,128]{2,1,0:T(8,128)S(1)}, u32[]{:S(2)}, u32[]{:S(2)}) async-start(f32[4,512,128]{2,1,0:T(8,128)} %bitcast.130), calls=%async_computation | async-start | bytes 2097152 | tf_op jit(solution)/shard_map/all_to_all | solution.py:97
  75.0 1.4 %pad_maximum_fusion = bf16[2,2048,2,128]{3,1,0,2:T(8,128)(2,1)S(1)} fusion(bf16[2,1024,2,128]{3,1,0,2:T(8,128)(2,1)} %collective-permute-done.2, bf16[2,1024,2,128]{3,1,0,2:T(8,128)(2,1)S(1)} %bitcast.119), kind=kLoop, calls=%fused_computation.24 | loop fusion | flops 4194304 | bytes 4194304 | tf_op jit(solution)/shard_map/concatenate | solution.py:68
  76.3 1.8 %fusion.13 = (f32[2,16,16]{2,1,0:T(8,128)S(1)}, f32[2,4096,16,16]{1,3,2,0:T(8,128)S(1)}) fusion(pred[16,4096]{1,0:T(8,128)(4,1)S(1)} %compare_and_fusion, bf16[4096,2,128,1]{2,0,3,1:T(8,128)(2,1)S(1)} %bitcast.123, bf16[16,2,16,128]{3,2,1,0:T(8,128)(2,1)S(1)} %bitcast.132), kind=kOutput, calls=%fused_computation.19 | convolution fusion | flops 543161856 | bytes 10684416 | tf_op jit(solution)/shard_map/rkgd,tkd->krgt/dot_general | solution.py:119
  78.1 2.8 %fusion.14 = f32[2,16,16]{2,1,0:T(8,128)S(1)} fusion(f32[2,4096,16,16]{1,3,2,0:T(8,128)S(1)} %get-tuple-element.107, f32[2,16,16]{2,1,0:T(8,128)S(1)} %get-tuple-element.106, pred[16,4096]{1,0:T(8,128)(4,1)S(1)} %compare_and_fusion), kind=kLoop, calls=%fused_computation.20 | loop fusion | flops 10485248 | bytes 8458240 | tf_op jit(solution)/shard_map/reduce_sum | solution.py:125
  81.4 1.4 %pad_maximum_fusion.1 = bf16[2,2048,2,128]{3,1,0,2:T(8,128)(2,1)S(1)} fusion(bf16[2,1024,2,128]{3,1,0,2:T(8,128)(2,1)} %collective-permute-done.3, bf16[2,1024,2,128]{3,1,0,2:T(8,128)(2,1)S(1)} %bitcast.118), kind=kLoop, calls=%fused_computation.25 | loop fusion | flops 4194304 | bytes 4194304 | tf_op jit(solution)/shard_map/concatenate | solution.py:69
  82.8 4.9 %fusion.19 = f32[16,2,16,128]{3,2,0,1:T(8,128)S(1)} fusion(bf16[4096,2,128,1]{2,0,3,1:T(8,128)(2,1)S(1)} %bitcast.124, f32[2,4096,16,16]{1,3,2,0:T(8,128)} %copy-done, f32[2,16,16]{2,1,0:T(8,128)S(1)} %get-tuple-element.106, pred[16,4096]{1,0:T(8,128)(4,1)S(1)} %compare_and_fusion), kind=kOutput, calls=%fused_computation.26 | convolution fusion | flops 547356672 | bytes 10815488 | tf_op jit(solution)/shard_map/krgt,tkd->rkgd/dot_general | solution.py:126
  87.8 6.7 %all-to-all-done = f32[4,512,128]{2,1,0:T(8,128)S(1)} async-done(((f32[4,512,128]{2,1,0:T(8,128)}), f32[4,512,128]{2,1,0:T(8,128)S(1)}, u32[]{:S(2)}, u32[]{:S(2)}) %all-to-all-start) | async-done | bytes 1048608 | tf_op jit(solution)/shard_map/all_to_all | solution.py:97
  (65 shorter events, 17.1 us)
Async XLA Ops:
  0.0 6.3 %copy-start.1 = (bf16[2,1024,4,128]{3,2,1,0:T(4,128)(2,1)S(1)}, bf16[2,1024,4,128]{3,2,1,0:T(4,128)(2,1)}, u32[]{:S(2)}) copy-start(bf16[2,1024,4,128]{3,2,1,0:T(4,128)(2,1)} %param.13) | copy-start | bytes 6291460
  0.0 6.3 %copy-start.2 = (bf16[2,1024,4,128]{3,2,1,0:T(4,128)(2,1)S(1)}, bf16[2,1024,4,128]{3,2,1,0:T(4,128)(2,1)}, u32[]{:S(2)}) copy-start(bf16[2,1024,4,128]{3,2,1,0:T(4,128)(2,1)} %param.12) | copy-start | bytes 6291460
  5.0 26.1 %collective-permute-start = (bf16[1024,2,128]{2,0,1:T(8,128)(2,1)}, bf16[1024,2,128]{2,0,1:T(8,128)(2,1)}, u32[]{:S(2)}, u32[]{:S(2)}) collective-permute-start(bf16[1024,2,128]{2,0,1:T(8,128)(2,1)} %bitcast.103), channel_id=1, source_target_pairs={{0,1},{1,0},{2,3},{3,2},{4,5},{5,4},{6,7},{7,6},{8,9},{9,8},{10,11... | collective-permute-start | bytes 1572872 | tf_op jit(solution)/shard_map/ppermute | solution.py:12
  6.3 26.0 %collective-permute-start.1 = (bf16[1024,2,128]{2,0,1:T(8,128)(2,1)}, bf16[1024,2,128]{2,0,1:T(8,128)(2,1)}, u32[]{:S(2)}, u32[]{:S(2)}) collective-permute-start(bf16[1024,2,128]{2,0,1:T(8,128)(2,1)} %bitcast.101), channel_id=1, source_target_pairs={{0,1},{1,0},{2,3},{3,2},{4,5},{5,4},{6,7},{7,6},{8,9},{9,8},{10,11... | collective-permute-start | bytes 1572872 | tf_op jit(solution)/shard_map/ppermute | solution.py:12
  10.0 2.9 %copy-start.5 = (bf16[16,32,128]{2,1,0:T(8,128)(2,1)S(1)}, bf16[16,32,128]{2,1,0:T(8,128)(2,1)}, u32[]{:S(2)}) copy-start(bf16[16,32,128]{2,1,0:T(8,128)(2,1)} %param.9) | copy-start | bytes 393220
  10.0 20.9 %copy-start.4 = (bf16[1024,1,2,128]{3,2,1,0:T(2,128)(2,1)S(1)}, bf16[1024,1,2,128]{3,2,1,0:T(2,128)(2,1)}, u32[]{:S(2)}) copy-start(bf16[1024,1,2,128]{3,2,1,0:T(2,128)(2,1)} %get-tuple-element.102) | copy-start | bytes 1572868
  10.0 21.0 %copy-start.3 = (bf16[1024,1,2,128]{3,2,1,0:T(2,128)(2,1)S(1)}, bf16[1024,1,2,128]{3,2,1,0:T(2,128)(2,1)}, u32[]{:S(2)}) copy-start(bf16[1024,1,2,128]{3,2,1,0:T(2,128)(2,1)} %get-tuple-element.111) | copy-start | bytes 1572868
  10.0 21.0 %copy-start.7 = (s32[16]{0:T(128)S(1)}, s32[16]{0:T(128)}, u32[]{:S(2)}) copy-start(s32[16]{0:T(128)} %param.14) | copy-start | bytes 196
  11.2 63.7 %collective-permute-start.2 = (bf16[2,1024,2,128]{3,1,0,2:T(8,128)(2,1)}, bf16[2,1024,2,128]{3,1,0,2:T(8,128)(2,1)}, u32[]{:S(2)}, u32[]{:S(2)}) collective-permute-start(bf16[2,1024,2,128]{3,1,0,2:T(8,128)(2,1)} %bitcast.99), channel_id=1, source_target_pairs={{0,1},{1,0},{2,3},{3,2},{4,5},{5,4},{6,7},{7,6},{8,9},{9,8},{10,11... | collective-permute-start | bytes 3145736 | tf_op jit(solution)/shard_map/ppermute | solution.py:12
  12.9 68.6 %collective-permute-start.3 = (bf16[2,1024,2,128]{3,1,0,2:T(8,128)(2,1)}, bf16[2,1024,2,128]{3,1,0,2:T(8,128)(2,1)}, u32[]{:S(2)}, u32[]{:S(2)}) collective-permute-start(bf16[2,1024,2,128]{3,1,0,2:T(8,128)(2,1)} %bitcast.97), channel_id=1, source_target_pairs={{0,1},{1,0},{2,3},{3,2},{4,5},{5,4},{6,7},{7,6},{8,9},{9,8},{10,11... | collective-permute-start | bytes 3145736 | tf_op jit(solution)/shard_map/ppermute | solution.py:12
  33.4 32.2 %copy-start.6 = (s32[16]{0:T(128)S(1)}, s32[16]{0:T(128)}, u32[]{:S(2)}) copy-start(s32[16]{0:T(128)} %param.15) | copy-start | bytes 196
  51.2 11.1 %all-to-all-start.1 = ((f32[4,1,512]{2,1,0:T(1,128)}), f32[4,1,512]{2,1,0:T(1,128)S(1)}, u32[]{:S(2)}, u32[]{:S(2)}) async-start(f32[4,1,512]{2,1,0:T(1,128)} %all_to_all.26), calls=%async_computation.1 | async-start | bytes 16384 | tf_op jit(solution)/shard_map/all_to_all | solution.py:98
  62.3 8.8 %all-to-all-start.2 = ((f32[4,1,512]{2,1,0:T(1,128)}), f32[4,1,512]{2,1,0:T(1,128)S(1)}, u32[]{:S(2)}, u32[]{:S(2)}) async-start(f32[4,1,512]{2,1,0:T(1,128)} %all_to_all.23), calls=%async_computation.2 | async-start | bytes 16384 | tf_op jit(solution)/shard_map/all_to_all | solution.py:99
  71.1 23.4 %all-to-all-start = ((f32[4,512,128]{2,1,0:T(8,128)}), f32[4,512,128]{2,1,0:T(8,128)S(1)}, u32[]{:S(2)}, u32[]{:S(2)}) async-start(f32[4,512,128]{2,1,0:T(8,128)} %bitcast.130), calls=%async_computation | async-start | bytes 2097152 | tf_op jit(solution)/shard_map/all_to_all | solution.py:97
  78.1 3.2 %copy-start = (f32[2,4096,16,16]{1,3,2,0:T(8,128)}, f32[2,4096,16,16]{1,3,2,0:T(8,128)S(1)}, u32[]{:S(2)}) copy-start(f32[2,4096,16,16]{1,3,2,0:T(8,128)S(1)} %get-tuple-element.107) | copy-start | bytes 25165828
where the time goes:
time: 96.4 us; the launch traced here: 95.8 us
  local copies, waits for them, and re-layouts  18.8 us (20%)
  blocking collectives  18 us (19%)
  matrix products  17.4 us (18%)
  waiting for transfers between devices  15.4 us (16%)
  starting transfers between devices  13.5 us (14%)
  other arithmetic  12.4 us (13%)
    all_gather x1, blocking collectives, local(): gathered = lax.all_gather(queries, 'blk', axis=0, tiled=True)  18 us
    dynamic_slice x6, local copies, waits for them, and re-layouts, pick_index(): lax.dynamic_index_in_dim(array_in, index_value, dim_index, keepdims=False)  11.6 us
    dot_general x4, matrix products, root_partial_mine(): jnp.einsum('rkgd,tkd->krgt', query_block, keys_mine, preferred_element_ty...  6.73 us
    all_to_all x1, waiting for transfers between devices, local(): lax.all_to_all(mine_sums, 'blk', split_axis=0, concat_axis=0, tiled=True)  6.72 us
    all_to_all x1, starting transfers between devices, local(): lax.all_to_all(mine_maxima, 'blk', split_axis=0, concat_axis=0, tiled=True)  5.49 us
    dot_general x1, matrix products, local(): jnp.einsum('krgt,tkd->rkgd', weights.astype(jnp.bfloat16), values_flat, p...  4.85 us
    all_to_all x1, waiting for transfers between devices, local(): lax.all_to_all(mine_maxima, 'blk', split_axis=0, concat_axis=0, tiled=True)  4.84 us
    dot_general x4, matrix products, root_partial_mine(): jnp.einsum('krgt,tkd->rkgd', weights.astype(jnp.bfloat16), values_mine, p...  4.06 us
  transfers between devices with their start and end apart: 7, of which 3 were waited for; matrix products, arithmetic and copies ran while one was open for 42% of the time, Pallas kernels for 0%

commit v1 on v0

v1 whole, which is shorter than its diff:
```python
import functools
import math

import jax
import jax.numpy as jnp
from jax import lax
from jax.experimental import pallas as pl
from jax.experimental.pallas import tpu as pltpu
from jax.sharding import PartitionSpec as P

masked_floor = -1e30
lowest_reference = -1e29
lane_count = 128
stat_pieces = 3
vmem_grant = 40 * 2**20


def vmem_spec():
    return pl.BlockSpec(memory_space=pltpu.VMEM)


def smem_spec():
    return pl.BlockSpec(memory_space=pltpu.SMEM)


def kernel_params():
    return pltpu.CompilerParams(vmem_limit_bytes=vmem_grant)


def exchange(value, axis, apart):
    return lax.ppermute(value, axis, [(i, i ^ apart) for i in range(lax.axis_size(axis))])


def stat_rows(rows):
    return -(-stat_pieces * (rows // lane_count) // 16) * 16


def identity_mask():
    shape = (lane_count, lane_count)
    return lax.broadcasted_iota(jnp.int32, shape, 0) == lax.broadcasted_iota(jnp.int32, shape, 1)


def column_to_rows(column, same):
    pieces = []
    for start in range(0, column.shape[0], lane_count):
        wide = jnp.broadcast_to(column[start : start + lane_count], (lane_count, lane_count))
        pieces.append(jnp.sum(jnp.where(same, wide, 0.0), axis=0, keepdims=True))
    return pieces


def rows_to_column(pieces, same):
    columns = []
    for piece in pieces:
        wide = jnp.broadcast_to(piece, (lane_count, lane_count))
        columns.append(jnp.sum(jnp.where(same, wide, 0.0), axis=1, keepdims=True))
    return jnp.concatenate(columns, axis=0)


def split_stat(value):
    pieces = []
    for _ in range(stat_pieces):
        piece = value.astype(jnp.bfloat16)
        pieces.append(piece)
        value = value - piece.astype(jnp.float32)
    return pieces


def attend(query, keys, values, scale, thresholds=None):
    scores = lax.dot_general(
        query, keys, (((1,), (1,)), ((), ())), preferred_element_type=jnp.float32
    )
    if thresholds is not None:
        slots = lax.broadcasted_iota(jnp.int32, scores.shape, 1)
        scores = jnp.where(slots < thresholds, scores, masked_floor)
    largest = jnp.max(scores, axis=1, keepdims=True)
    if thresholds is not None:
        largest = jnp.maximum(largest, lowest_reference)
    weights = jnp.exp2((scores - largest) * scale)
    totals = jnp.sum(weights, axis=1, keepdims=True)
    sums = jnp.dot(weights.astype(jnp.bfloat16), values, preferred_element_type=jnp.float32)
    return sums, largest * scale, totals


def normalised(sums, largest, totals):
    some = totals > 0.0
    safe = jnp.where(some, totals, 1.0)
    level = jnp.where(some, largest + jnp.log2(safe), masked_floor)
    return sums * (1.0 / safe), level


def store_packed(out_ref, heads, requests, group_size, outs, levels, same):
    rows = requests * heads * group_size
    per_head = requests * group_size
    all_rows = []
    for h in range(heads):
        block = outs[h].astype(jnp.bfloat16).reshape(requests, group_size, lane_count)
        for r in range(requests):
            out_ref[pl.ds((r * heads + h) * group_size, group_size), :] = block[r]
        all_rows += column_to_rows(levels[h], same)
    stats = jnp.concatenate(all_rows, axis=0)
    pieces = [piece.astype(jnp.float32) for piece in split_stat(stats)]
    spare = stat_rows(rows) - stat_pieces * stats.shape[0]
    if spare:
        pieces.append(jnp.zeros((spare, lane_count), jnp.float32))
    out_ref[pl.ds(rows, stat_rows(rows)), :] = jnp.concatenate(pieces, axis=0).astype(jnp.bfloat16)


def load_packed(in_ref, heads, requests, group_size, same):
    rows = requests * heads * group_size
    lines = rows // lane_count
    per_head = lines // heads
    stats = in_ref[pl.ds(rows, stat_rows(rows)), :].astype(jnp.float32)
    joined = stats[:lines]
    for piece in range(1, stat_pieces):
        joined = joined + stats[piece * lines : (piece + 1) * lines]
    outs, levels = [], []
    for h in range(heads):
        parts = [
            in_ref[pl.ds((r * heads + h) * group_size, group_size), :] for r in range(requests)
        ]
        outs.append(jnp.concatenate(parts, axis=0).astype(jnp.float32))
        lines_here = [joined[h * per_head + i : h * per_head + i + 1] for i in range(per_head)]
        levels.append(rows_to_column(lines_here, same))
    return outs, levels


def head_queries(query_ref, head, group_size):
    block = query_ref[:, head * group_size : (head + 1) * group_size, :]
    return block.reshape(block.shape[0] * group_size, block.shape[2])


def split_heads(source_ref, target_ref, first, heads, base, chunk):
    tokens = source_ref.shape[0]

    @pl.loop(0, tokens // chunk)
    def _(step):
        block = source_ref[pl.ds(step * chunk, chunk)]
        block = jnp.swapaxes(block[:, first : first + heads, :], 0, 1)
        target_ref[:, pl.ds(base + step * chunk, chunk), :] = block


def prepare_kernel(pair_ref, ko_ref, vo_ref, kp_ref, vp_ref, k_ref, v_ref):
    tokens, shared, _ = ko_ref.shape
    heads = k_ref.shape[0]
    for choice in range(shared // heads):

        @pl.when(pair_ref[0] == choice)
        def _():
            for base, keys, values in ((0, ko_ref, vo_ref), (tokens, kp_ref, vp_ref)):
                split_heads(keys, k_ref, choice * heads, heads, base, 64)
                split_heads(values, v_ref, choice * heads, heads, base, 64)


def prepare(pair_index, keys, values, other_keys, other_values, heads):
    tokens, _, width = keys.shape
    shape = jax.ShapeDtypeStruct((heads, 2 * tokens, width), keys.dtype)
    return pl.pallas_call(
        prepare_kernel,
        out_shape=(shape, shape),
        in_specs=[smem_spec()] + [vmem_spec()] * 4,
        out_specs=(vmem_spec(), vmem_spec()),
        compiler_params=kernel_params(),
        cost_estimate=pl.CostEstimate(flops=0, bytes_accessed=8 * 2**20, transcendentals=0),
        name="root_prepare",
    )(pair_index, keys, values, other_keys, other_values)


def root_kernel(scale, group_size, query_ref, k_ref, v_ref, out_ref):
    heads = k_ref.shape[0]
    requests = query_ref.shape[0]
    same = identity_mask()
    outs, levels = [], []
    for h in range(heads):
        query = head_queries(query_ref, h, group_size)
        out, level = normalised(*attend(query, k_ref[h], v_ref[h], scale))
        outs.append(out)
        levels.append(level)
    store_packed(out_ref, heads, requests, group_size, outs, levels, same)


def root_block(query, keys, values, scale):
    requests, local_heads, width = query.shape
    heads, tokens, _ = keys.shape
    rows = requests * local_heads
    return pl.pallas_call(
        functools.partial(root_kernel, scale, local_heads // heads),
        out_shape=jax.ShapeDtypeStruct((rows + stat_rows(rows), width), query.dtype),
        in_specs=[vmem_spec()] * 3,
        out_specs=vmem_spec(),
        compiler_params=kernel_params(),
        cost_estimate=pl.CostEstimate(
            flops=4 * rows * tokens * width, bytes_accessed=6 * 2**20, transcendentals=rows * tokens
        ),
        name="root_block",
    )(query, keys, values)


def branch_kernel(
    scale, group_size, pair_ref, branch_ref, seen_ref, mine_ref, theirs_ref, bk_ref, bv_ref,
    mine_out, theirs_out, k_ref, v_ref, limit_ref,
):
    requests, local_heads, _ = mine_ref.shape
    branches, tokens, shared, _ = bk_ref.shape
    heads = local_heads // group_size
    pair = pair_ref[0]
    same = identity_mask()
    for b in range(branches):
        split_heads(bk_ref.at[b], k_ref.at[b], 0, shared, 0, 64)
        split_heads(bv_ref.at[b], v_ref.at[b], 0, shared, 0, 64)
        for r in range(requests):
            here = branch_ref[r] % branches == b
            limit = jnp.where(here, seen_ref[r] - pair * tokens, 0)
            limit_ref[b, pl.ds(r * group_size, group_size), :] = jnp.full(
                (group_size, lane_count), limit, jnp.int32
            )
    for query_ref, out_ref, owner in ((mine_ref, mine_out, pair), (theirs_ref, theirs_out, 1 - pair)):
        outs, levels = [], []
        for h in range(heads):
            query = head_queries(query_ref, h, group_size)
            parts = []
            for b in range(branches):
                keys = k_ref[b, owner * heads + h]
                values = v_ref[b, owner * heads + h]
                parts.append(attend(query, keys, values, scale, limit_ref[b][:, :1]))
            sums, largest, totals = parts[0]
            for other_sums, other_largest, other_totals in parts[1:]:
                top = jnp.maximum(largest, other_largest)
                one, two = jnp.exp2(largest - top), jnp.exp2(other_largest - top)
                sums = sums * one + other_sums * two
                totals = totals * one + other_totals * two
                largest = top
            out, level = normalised(sums, largest, totals)
            outs.append(out)
            levels.append(level)
        store_packed(out_ref, heads, requests, group_size, outs, levels, same)


def branch_block(pair_index, branch, seen, mine, theirs, keys, values, scale, heads):
    requests, local_heads, width = mine.shape
    branches, tokens, shared, _ = keys.shape
    rows = requests * local_heads
    group_size = local_heads // heads
    shape = jax.ShapeDtypeStruct((rows + stat_rows(rows), width), mine.dtype)
    held = pltpu.VMEM((branches, shared, tokens, width), keys.dtype)
    count = 2 * rows * branches * tokens
    return pl.pallas_call(
        functools.partial(branch_kernel, scale, group_size),
        out_shape=(shape, shape),
        in_specs=[smem_spec()] * 3 + [vmem_spec()] * 4,
        out_specs=(vmem_spec(), vmem_spec()),
        scratch_shapes=[
            held,
            held,
            pltpu.VMEM((branches, requests * group_size, lane_count), jnp.int32),
        ],
        compiler_params=kernel_params(),
        cost_estimate=pl.CostEstimate(
            flops=4 * count * width, bytes_accessed=12 * 2**20, transcendentals=count
        ),
        name="branch_block",
    )(pair_index, branch, seen, mine, theirs, keys, values)


def merge_kernel(last, heads, requests, group_size, *refs):
    ins, out_ref = refs[:-1], refs[-1]
    same = identity_mask()
    loaded = [load_packed(ref, heads, requests, group_size, same) for ref in ins]
    outs, levels = [], []
    for h in range(heads):
        top = loaded[0][1][h]
        for _, level in loaded[1:]:
            top = jnp.maximum(top, level[h])
        sums = totals = 0.0
        for out, level in loaded:
            weight = jnp.exp2(level[h] - top)
            sums = sums + out[h] * weight
            totals = totals + weight
        outs.append(sums * (1.0 / totals))
        levels.append(top + jnp.log2(totals))
    if last:
        for h in range(heads):
            block = outs[h].astype(out_ref.dtype).reshape(requests, group_size, lane_count)
            out_ref[:, h * group_size : (h + 1) * group_size, :] = block
    else:
        store_packed(out_ref, heads, requests, group_size, outs, levels, same)


def merge(parts, last, heads, requests, group_size):
    if last:
        shape = (requests, heads * group_size, lane_count)
    else:
        shape = parts[0].shape
    return pl.pallas_call(
        functools.partial(merge_kernel, last, heads, requests, group_size),
        out_shape=jax.ShapeDtypeStruct(shape, parts[0].dtype),
        in_specs=[vmem_spec()] * len(parts),
        out_specs=vmem_spec(),
        compiler_params=kernel_params(),
        cost_estimate=pl.CostEstimate(flops=0, bytes_accessed=2**20, transcendentals=0),
        name="merge_last" if last else "merge_some",
    )(*parts)


def local(queries, root_keys, root_values, branch_keys, branch_values, request_branch, seen_tokens):
    requests, local_heads, width = queries.shape
    shared = root_keys.shape[1]
    blocks = lax.axis_size("blk")
    heads = shared // lax.axis_size("pair")
    group_size = local_heads // heads
    scale = math.log2(math.e) / math.sqrt(width)
    pair_index = lax.axis_index("pair").astype(jnp.int32).reshape(1)

    other_keys = exchange(root_keys, "pair", 1)
    other_values = exchange(root_values, "pair", 1)
    other_queries = exchange(queries, "pair", 1)
    arrived = {}
    for apart in range(blocks - 1, 0, -2):
        arrived[apart] = exchange(queries, "blk", apart)
    for apart in range(blocks - 1, 2, -2):
        arrived[apart ^ 1] = exchange(arrived[apart], "blk", 1)

    keys, values = prepare(pair_index, root_keys, root_values, other_keys, other_values, heads)
    near = [root_block(queries, keys, values, scale)]
    returned = {}
    for apart in arrived:
        returned[apart] = exchange(root_block(arrived[apart], keys, values, scale), "blk", apart)
    mine, theirs = branch_block(
        pair_index, request_branch, seen_tokens, queries, other_queries,
        branch_keys, branch_values, scale, heads,
    )
    near += [mine, exchange(theirs, "pair", 1)]
    order = list(returned)
    near += [returned[apart] for apart in order[:-1]]
    most = merge(near, False, heads, requests, group_size)
    return merge([most, returned[order[-1]]], True, heads, requests, group_size)


def solution(mesh):
    in_specs = (
        P(("groups", "blk"), ("kv", "pair"), None),
        P(("groups", "blk", "pair"), "kv", None),
        P(("groups", "blk", "pair"), "kv", None),
        P(("groups", "blk"), "pair", "kv", None),
        P(("groups", "blk"), "pair", "kv", None),
        P(("groups", "blk")),
        P(("groups", "blk")),
    )
    out_specs = P(("groups", "blk"), ("kv", "pair"), None)
    return jax.shard_map(local, mesh=mesh, in_specs=in_specs, out_specs=out_specs, check_vma=False)
```

time: 96.4 us -> 47.5 us (0.49)
  Pallas kernels: 0 us -> 19.6 us
  blocking collectives: 18 us -> 0 us
  matrix products: 17.4 us -> 0 us
  local copies, waits for them, and re-layouts: 18.8 us -> 5.41 us
  other arithmetic: 12.4 us -> 0 us
  waiting for transfers between devices: 15.4 us -> 10 us
  starting transfers between devices: 13.5 us -> 12.1 us
    pallas_call x0 -> x8, Pallas kernels: none -> 19.6 us  [the longest x1 8 us: branch_block(): pl.pallas_call(functools.partial(branch_kernel, scale, group_size), out_s...]
    all_gather x1 -> x0, blocking collectives: 18 us -> none  [local(): gathered = lax.all_gather(queries, 'blk', axis=0, tiled=True)]
    dot_general x10 -> x0, matrix products: 17.4 us -> none  [the longest x4 6.73 us: root_partial_mine(): jnp.einsum('rkgd,tkd->krgt', query_block, keys_mine, preferred_element_ty...]
    all_to_all x3 -> x0, waiting for transfers between devices: 15.4 us -> none  [the longest x1 6.72 us: local(): lax.all_to_all(mine_sums, 'blk', split_axis=0, concat_axis=0, tiled=True)]
    all_to_all x3 -> x0, starting transfers between devices: 12.4 us -> none  [the longest x1 5.49 us: local(): lax.all_to_all(mine_maxima, 'blk', split_axis=0, concat_axis=0, tiled=True)]
    dynamic_slice x6 -> x0, local copies, waits for them, and re-layouts: 11.6 us -> none  [pick_index(): lax.dynamic_index_in_dim(array_in, index_value, dim_index, keepdims=False)]
    ppermute x4 -> x10, starting transfers between devices: 1.02 us -> 12.1 us  [exchange(): lax.ppermute(value, axis, [(i, i ^ apart) for i in range(lax.axis_size(ax...]
    ppermute x4 -> x10, waiting for transfers between devices: 0.01 us -> 10 us  [exchange(): lax.ppermute(value, axis, [(i, i ^ apart) for i in range(lax.axis_size(ax...]
  transfers between devices with their start and end apart: 7 -> 10, of which waited for: 3 -> 3; matrix products, arithmetic and copies ran while one was open for 42% -> 0% of each run, Pallas kernels for 0% -> 39%
where the time goes in v1:
time: 47.5 us; the launch traced here: 47.3 us
  Pallas kernels  19.6 us (41%)
  starting transfers between devices  12.1 us (25%)
  waiting for transfers between devices  10 us (21%)
  local copies, waits for them, and re-layouts  5.41 us (11%)
    ppermute x10, starting transfers between devices, exchange(): lax.ppermute(value, axis, [(i, i ^ apart) for i in range(lax.axis_size(ax...  12.1 us
    ppermute x10, waiting for transfers between devices, exchange(): lax.ppermute(value, axis, [(i, i ^ apart) for i in range(lax.axis_size(ax...  10 us
    pallas_call x1, Pallas kernels, branch_block(): pl.pallas_call(functools.partial(branch_kernel, scale, group_size), out_s...  8 us
    pallas_call x4, Pallas kernels, root_block(): pl.pallas_call(functools.partial(root_kernel, scale, local_heads // heads...  7.58 us
    unnamed x16, local copies, waits for them, and re-layouts  5.41 us
    pallas_call x2, Pallas kernels, merge(): pl.pallas_call(functools.partial(merge_kernel, last, heads, requests, gro...  2.15 us
    pallas_call x1, Pallas kernels, prepare(): pl.pallas_call(prepare_kernel, out_shape=(shape, shape), in_specs=[smem_s...  1.91 us
  transfers between devices with their start and end apart: 10, of which 3 were waited for; matrix products, arithmetic and copies ran while one was open for 0% of the time, Pallas kernels for 39%

profile of v1, /device:TPU:0, one launch (start us, length us, event | category | flops | bytes accessed | tf_op | source)
XLA Modules:
  0.0 47.3 jit_solution(3401818156572289917)
XLA Ops:
  0.0 0.5 collective-permute-start
  0.5 0.1 collective-permute-start.1
  0.5 5.0 %collective-permute-start.4 = (bf16[16,32,128]{2,1,0:T(8,128)(2,1)}, bf16[16,32,128]{2,1,0:T(8,128)(2,1)S(1)}, u32[]{:S(2)}, u32[]{:S(2)}) collective-permute-start(bf16[16,32,128]{2,1,0:T(8,128)(2,1)} %mine_ref.1), channel_id=1, source_target_pairs={{0,12},{4,8},{8,4},{12,0},{1,13},{5,9},{9,5},{13,1},{2,14},{6,10},... | collective-permute-start | bytes 393224 | tf_op jit(solution)/shard_map/ppermute | solution.py:31
  5.6 4.6 %collective-permute-done.4.query_ref = bf16[16,32,128]{2,1,0:T(8,128)(2,1)S(1)} collective-permute-done((bf16[16,32,128]{2,1,0:T(8,128)(2,1)}, bf16[16,32,128]{2,1,0:T(8,128)(2,1)S(1)}, u32[]{:S(2)}, u32[]{:S(2)}) %collective-permute-start.4) | collective-permute-done | bytes 131104 | tf_op jit(solution)/shard_map/ppermute | solution.py:31
  10.1 1.8 %collective-permute-start.8 = (bf16[16,32,128]{2,1,0:T(8,128)(2,1)S(1)}, bf16[16,32,128]{2,1,0:T(8,128)(2,1)S(1)}, u32[]{:S(2)}, u32[]{:S(2)}) collective-permute-start(bf16[16,32,128]{2,1,0:T(8,128)(2,1)S(1)} %collective-permute-done.4.query_ref), channel_id=1, source_target_pairs={{0,4},{4,0},{8,12},{12,8},{1,5},{5,1},{9,13},{13,9},{2,6},{6,2},{1... | collective-permute-start | bytes 393224 | tf_op jit(solution)/shard_map/ppermute | solution.py:31
  12.0 1.6 %copy-done = bf16[2,1024,4,128]{3,2,1,0:T(4,128)(2,1)S(1)} copy-done((bf16[2,1024,4,128]{3,2,1,0:T(4,128)(2,1)S(1)}, bf16[2,1024,4,128]{3,2,1,0:T(4,128)(2,1)}, u32[]{:S(2)}) %copy-start) | copy-done | bytes 2097176
  13.6 1.6 %copy-done.1 = bf16[2,1024,4,128]{3,2,1,0:T(4,128)(2,1)S(1)} copy-done((bf16[2,1024,4,128]{3,2,1,0:T(4,128)(2,1)S(1)}, bf16[2,1024,4,128]{3,2,1,0:T(4,128)(2,1)}, u32[]{:S(2)}) %copy-start.1) | copy-done | bytes 2097176
  15.2 0.9 %copy-done.4 = bf16[16,32,128]{2,1,0:T(8,128)(2,1)S(1)} copy-done((bf16[16,32,128]{2,1,0:T(8,128)(2,1)S(1)}, bf16[16,32,128]{2,1,0:T(8,128)(2,1)}, u32[]{:S(2)}) %copy-start.4) | copy-done | bytes 131096
  16.1 0.7 %copy-done.6 = s32[16]{0:T(128)S(1)} copy-done((s32[16]{0:T(128)S(1)}, s32[16]{0:T(128)}, u32[]{:S(2)}) %copy-start.6) | copy-done | bytes 88
  16.7 0.7 %copy-done.7 = s32[16]{0:T(128)S(1)} copy-done((s32[16]{0:T(128)S(1)}, s32[16]{0:T(128)}, u32[]{:S(2)}) %copy-start.7) | copy-done | bytes 88
  17.4 8.0 %branch_block.1 = (bf16[528,128]{1,0:T(8,128)(2,1)S(1)}, bf16[528,128]{1,0:T(8,128)(2,1)S(1)}) custom-call(s32[1]{0:T(128)} %bitcast.pair_ref, s32[16]{0:T(128)S(1)} %copy-done.6, s32[16]{0:T(128)S(1)} %copy-done.7, bf16[16,32,128]{2,1,0:T(8,128)(2,1)S(1)} %copy-done.4, bf16[16,32,128]{2,1,0:T(8,128)(2,1)S(1)} %collective-permute-done.2.theirs_ref, ...), custom_call_target="tpu_custom_call" | custom-call | flops 1073741824 | bytes 12582912 | tf_op jit(solution)/shard_map/branch_block/pallas_call | solution.py:246
  25.4 0.1 collective-permute-start.3
  25.5 1.9 %root_prepare.1 = (bf16[2,2048,128]{2,1,0:T(8,128)(2,1)S(1)}, bf16[2,2048,128]{2,1,0:T(8,128)(2,1)S(1)}) custom-call(s32[1]{0:T(128)} %bitcast.pair_ref, bf16[1024,4,128]{2,1,0:T(4,128)(2,1)S(1)} %copy-done.2, bf16[1024,4,128]{2,1,0:T(4,128)(2,1)S(1)} %copy-done.3, bf16[1024,4,128]{2,1,0:T(4,128)(2,1)S(1)} %collective-permute-done.kp_ref, ...), custom_call_target="tpu_custom_call" | custom-call | bytes 8388608 | tf_op jit(solution)/shard_map/root_prepare/pallas_call | solution.py:157
  27.4 1.9 %root_block.5 = bf16[528,128]{1,0:T(8,128)(2,1)S(1)} custom-call(bf16[16,32,128]{2,1,0:T(8,128)(2,1)S(1)} %collective-permute-done.4.query_ref, bf16[2,2048,128]{2,1,0:T(8,128)(2,1)S(1)} %get-tuple-element.9.k_ref, bf16[2,2048,128]{2,1,0:T(8,128)(2,1)S(1)} %get-tuple-element.10.v_ref), custom_call_target="tpu_custom_call" | custom-call | flops 536870912 | bytes 6291456 | tf_op jit(solution)/shard_map/root_block/pallas_call | solution.py:185
  29.3 2.4 %collective-permute-start.5 = (bf16[528,128]{1,0:T(8,128)(2,1)S(1)}, bf16[528,128]{1,0:T(8,128)(2,1)S(1)}, u32[]{:S(2)}, u32[]{:S(2)}) collective-permute-start(bf16[528,128]{1,0:T(8,128)(2,1)S(1)} %root_block.5), channel_id=1, source_target_pairs={{0,12},{4,8},{8,4},{12,0},{1,13},{5,9},{9,5},{13,1},{2,14},{6,10},... | collective-permute-start | bytes 405512 | tf_op jit(solution)/shard_map/ppermute | solution.py:31
  31.8 1.9 %root_block.6 = bf16[528,128]{1,0:T(8,128)(2,1)S(1)} custom-call(bf16[16,32,128]{2,1,0:T(8,128)(2,1)S(1)} %collective-permute-done.6.query_ref, bf16[2,2048,128]{2,1,0:T(8,128)(2,1)S(1)} %get-tuple-element.9.k_ref, bf16[2,2048,128]{2,1,0:T(8,128)(2,1)S(1)} %get-tuple-element.10.v_ref), custom_call_target="tpu_custom_call" | custom-call | flops 536870912 | bytes 6291456 | tf_op jit(solution)/shard_map/root_block/pallas_call | solution.py:185
  33.7 0.8 %collective-permute-start.7 = (bf16[528,128]{1,0:T(8,128)(2,1)S(1)}, bf16[528,128]{1,0:T(8,128)(2,1)S(1)}, u32[]{:S(2)}, u32[]{:S(2)}) collective-permute-start(bf16[528,128]{1,0:T(8,128)(2,1)S(1)} %root_block.6), channel_id=1, source_target_pairs={{0,4},{4,0},{8,12},{12,8},{1,5},{5,1},{9,13},{13,9},{2,6},{6,2},{1... | collective-permute-start | bytes 405512 | tf_op jit(solution)/shard_map/ppermute | solution.py:31
  34.5 1.9 %root_block.7 = bf16[528,128]{1,0:T(8,128)(2,1)S(1)} custom-call(bf16[16,32,128]{2,1,0:T(8,128)(2,1)S(1)} %collective-permute-done.8.query_ref, bf16[2,2048,128]{2,1,0:T(8,128)(2,1)S(1)} %get-tuple-element.9.k_ref, bf16[2,2048,128]{2,1,0:T(8,128)(2,1)S(1)} %get-tuple-element.10.v_ref), custom_call_target="tpu_custom_call" | custom-call | flops 536870912 | bytes 6291456 | tf_op jit(solution)/shard_map/root_block/pallas_call | solution.py:185
  36.4 1.3 %collective-permute-start.9 = (bf16[528,128]{1,0:T(8,128)(2,1)S(1)}, bf16[528,128]{1,0:T(8,128)(2,1)S(1)}, u32[]{:S(2)}, u32[]{:S(2)}) collective-permute-start(bf16[528,128]{1,0:T(8,128)(2,1)S(1)} %root_block.7), channel_id=1, source_target_pairs={{0,8},{4,12},{8,0},{12,4},{1,9},{5,13},{9,1},{13,5},{2,10},{6,14},... | collective-permute-start | bytes 405512 | tf_op jit(solution)/shard_map/ppermute | solution.py:31
  37.7 1.9 %root_block.4.refs_0_ = bf16[528,128]{1,0:T(8,128)(2,1)S(1)} custom-call(bf16[16,32,128]{2,1,0:T(8,128)(2,1)S(1)} %copy-done.5, bf16[2,2048,128]{2,1,0:T(8,128)(2,1)S(1)} %get-tuple-element.9.k_ref, bf16[2,2048,128]{2,1,0:T(8,128)(2,1)S(1)} %get-tuple-element.10.v_ref), custom_call_target="tpu_custom_call" | custom-call | flops 536870912 | bytes 6291456 | tf_op jit(solution)/shard_map/root_block/pallas_call | solution.py:185
  39.6 1.7 %collective-permute-done.7.refs_4_ = bf16[528,128]{1,0:T(8,128)(2,1)S(1)} collective-permute-done((bf16[528,128]{1,0:T(8,128)(2,1)S(1)}, bf16[528,128]{1,0:T(8,128)(2,1)S(1)}, u32[]{:S(2)}, u32[]{:S(2)}) %collective-permute-start.7) | collective-permute-done | bytes 135200 | tf_op jit(solution)/shard_map/ppermute | solution.py:31
  41.4 1.0 %merge_some.1.refs_0_ = bf16[528,128]{1,0:T(8,128)(2,1)S(1)} custom-call(bf16[528,128]{1,0:T(8,128)(2,1)S(1)} %root_block.4.refs_0_, bf16[528,128]{1,0:T(8,128)(2,1)S(1)} %get-tuple-element.11.refs_1_, bf16[528,128]{1,0:T(8,128)(2,1)S(1)} %collective-permute-done.3.refs_2_, bf16[528,128]{1,0:T(8,128)(2,1)S(1)} %collective-permute-done.5.refs_3_, ...), custom_call_target="tpu_custom_call" | custom-call | bytes 1048576 | tf_op jit(solution)/shard_map/merge_some/pallas_call | solution.py:293
  42.4 3.7 %collective-permute-done.9.refs_1_ = bf16[528,128]{1,0:T(8,128)(2,1)S(1)} collective-permute-done((bf16[528,128]{1,0:T(8,128)(2,1)S(1)}, bf16[528,128]{1,0:T(8,128)(2,1)S(1)}, u32[]{:S(2)}, u32[]{:S(2)}) %collective-permute-start.9) | collective-permute-done | bytes 135200 | tf_op jit(solution)/shard_map/ppermute | solution.py:31
  46.1 1.1 %merge_last.1 = bf16[16,32,128]{2,1,0:T(8,128)(2,1)} custom-call(bf16[528,128]{1,0:T(8,128)(2,1)S(1)} %merge_some.1.refs_0_, bf16[528,128]{1,0:T(8,128)(2,1)S(1)} %collective-permute-done.9.refs_1_), custom_call_target="tpu_custom_call" | custom-call | bytes 1048576 | tf_op jit(solution)/shard_map/merge_last/pallas_call | solution.py:293
  (20 shorter events, 0.0 us)
Async XLA Ops:
  0.0 25.5 %collective-permute-start = (bf16[1024,4,128]{2,1,0:T(4,128)(2,1)}, bf16[1024,4,128]{2,1,0:T(4,128)(2,1)S(1)}, u32[]{:S(2)}, u32[]{:S(2)}) collective-permute-start(bf16[1024,4,128]{2,1,0:T(4,128)(2,1)} %ko_ref.1), channel_id=1, source_target_pairs={{0,1},{1,0},{2,3},{3,2},{4,5},{5,4},{6,7},{7,6},{8,9},{9,8},{10,11... | collective-permute-start | bytes 3145736 | tf_op jit(solution)/shard_map/ppermute | solution.py:31
  0.5 25.0 %collective-permute-start.1 = (bf16[1024,4,128]{2,1,0:T(4,128)(2,1)}, bf16[1024,4,128]{2,1,0:T(4,128)(2,1)S(1)}, u32[]{:S(2)}, u32[]{:S(2)}) collective-permute-start(bf16[1024,4,128]{2,1,0:T(4,128)(2,1)} %vo_ref.1), channel_id=1, source_target_pairs={{0,1},{1,0},{2,3},{3,2},{4,5},{5,4},{6,7},{7,6},{8,9},{9,8},{10,11... | collective-permute-start | bytes 3145736 | tf_op jit(solution)/shard_map/ppermute | solution.py:31
  0.5 9.6 %collective-permute-start.4 = (bf16[16,32,128]{2,1,0:T(8,128)(2,1)}, bf16[16,32,128]{2,1,0:T(8,128)(2,1)S(1)}, u32[]{:S(2)}, u32[]{:S(2)}) collective-permute-start(bf16[16,32,128]{2,1,0:T(8,128)(2,1)} %mine_ref.1), channel_id=1, source_target_pairs={{0,12},{4,8},{8,4},{12,0},{1,13},{5,9},{9,5},{13,1},{2,14},{6,10},... | collective-permute-start | bytes 393224 | tf_op jit(solution)/shard_map/ppermute | solution.py:31
  5.6 6.4 %collective-permute-start.2 = (bf16[16,32,128]{2,1,0:T(8,128)(2,1)}, bf16[16,32,128]{2,1,0:T(8,128)(2,1)S(1)}, u32[]{:S(2)}, u32[]{:S(2)}) collective-permute-start(bf16[16,32,128]{2,1,0:T(8,128)(2,1)} %mine_ref.1), channel_id=1, source_target_pairs={{0,1},{1,0},{2,3},{3,2},{4,5},{5,4},{6,7},{7,6},{8,9},{9,8},{10,11... | collective-permute-start | bytes 393224 | tf_op jit(solution)/shard_map/ppermute | solution.py:31
  5.6 26.2 %collective-permute-start.6 = (bf16[16,32,128]{2,1,0:T(8,128)(2,1)}, bf16[16,32,128]{2,1,0:T(8,128)(2,1)S(1)}, u32[]{:S(2)}, u32[]{:S(2)}) collective-permute-start(bf16[16,32,128]{2,1,0:T(8,128)(2,1)} %mine_ref.1), channel_id=1, source_target_pairs={{0,4},{4,0},{8,12},{12,8},{1,5},{5,1},{9,13},{13,9},{2,6},{6,2},{1... | collective-permute-start | bytes 393224 | tf_op jit(solution)/shard_map/ppermute | solution.py:31
  10.1 24.4 %collective-permute-start.8 = (bf16[16,32,128]{2,1,0:T(8,128)(2,1)S(1)}, bf16[16,32,128]{2,1,0:T(8,128)(2,1)S(1)}, u32[]{:S(2)}, u32[]{:S(2)}) collective-permute-start(bf16[16,32,128]{2,1,0:T(8,128)(2,1)S(1)} %collective-permute-done.4.query_ref), channel_id=1, source_target_pairs={{0,4},{4,0},{8,12},{12,8},{1,5},{5,1},{9,13},{13,9},{2,6},{6,2},{1... | collective-permute-start | bytes 393224 | tf_op jit(solution)/shard_map/ppermute | solution.py:31
  12.0 1.6 %copy-start = (bf16[2,1024,4,128]{3,2,1,0:T(4,128)(2,1)S(1)}, bf16[2,1024,4,128]{3,2,1,0:T(4,128)(2,1)}, u32[]{:S(2)}) copy-start(bf16[2,1024,4,128]{3,2,1,0:T(4,128)(2,1)} %bk_ref.1) | copy-start | bytes 6291460
  13.6 1.6 %copy-start.1 = (bf16[2,1024,4,128]{3,2,1,0:T(4,128)(2,1)S(1)}, bf16[2,1024,4,128]{3,2,1,0:T(4,128)(2,1)}, u32[]{:S(2)}) copy-start(bf16[2,1024,4,128]{3,2,1,0:T(4,128)(2,1)} %bv_ref.1) | copy-start | bytes 6291460
  15.1 0.9 %copy-start.4 = (bf16[16,32,128]{2,1,0:T(8,128)(2,1)S(1)}, bf16[16,32,128]{2,1,0:T(8,128)(2,1)}, u32[]{:S(2)}) copy-start(bf16[16,32,128]{2,1,0:T(8,128)(2,1)} %mine_ref.1) | copy-start | bytes 393220
  16.1 0.7 %copy-start.6 = (s32[16]{0:T(128)S(1)}, s32[16]{0:T(128)}, u32[]{:S(2)}) copy-start(s32[16]{0:T(128)} %branch_ref.1) | copy-start | bytes 196
  16.7 0.7 %copy-start.7 = (s32[16]{0:T(128)S(1)}, s32[16]{0:T(128)}, u32[]{:S(2)}) copy-start(s32[16]{0:T(128)} %seen_ref.1) | copy-start | bytes 196
  17.4 8.1 %copy-start.2 = (bf16[1024,4,128]{2,1,0:T(4,128)(2,1)S(1)}, bf16[1024,4,128]{2,1,0:T(4,128)(2,1)}, u32[]{:S(2)}) copy-start(bf16[1024,4,128]{2,1,0:T(4,128)(2,1)} %ko_ref.1) | copy-start | bytes 3145732
  17.4 8.1 %copy-start.3 = (bf16[1024,4,128]{2,1,0:T(4,128)(2,1)S(1)}, bf16[1024,4,128]{2,1,0:T(4,128)(2,1)}, u32[]{:S(2)}) copy-start(bf16[1024,4,128]{2,1,0:T(4,128)(2,1)} %vo_ref.1) | copy-start | bytes 3145732
  25.4 14.3 %collective-permute-start.3 = (bf16[528,128]{1,0:T(8,128)(2,1)S(1)}, bf16[528,128]{1,0:T(8,128)(2,1)S(1)}, u32[]{:S(2)}, u32[]{:S(2)}) collective-permute-start(bf16[528,128]{1,0:T(8,128)(2,1)S(1)} %get-tuple-element.12), channel_id=1, source_target_pairs={{0,1},{1,0},{2,3},{3,2},{4,5},{5,4},{6,7},{7,6},{8,9},{9,8},{10,11... | collective-permute-start | bytes 405512 | tf_op jit(solution)/shard_map/ppermute | solution.py:31
  29.3 8.4 %copy-start.5 = (bf16[16,32,128]{2,1,0:T(8,128)(2,1)S(1)}, bf16[16,32,128]{2,1,0:T(8,128)(2,1)}, u32[]{:S(2)}) copy-start(bf16[16,32,128]{2,1,0:T(8,128)(2,1)} %mine_ref.1) | copy-start | bytes 393220
  29.3 10.3 %collective-permute-start.5 = (bf16[528,128]{1,0:T(8,128)(2,1)S(1)}, bf16[528,128]{1,0:T(8,128)(2,1)S(1)}, u32[]{:S(2)}, u32[]{:S(2)}) collective-permute-start(bf16[528,128]{1,0:T(8,128)(2,1)S(1)} %root_block.5), channel_id=1, source_target_pairs={{0,12},{4,8},{8,4},{12,0},{1,13},{5,9},{9,5},{13,1},{2,14},{6,10},... | collective-permute-start | bytes 405512 | tf_op jit(solution)/shard_map/ppermute | solution.py:31
  33.7 7.7 %collective-permute-start.7 = (bf16[528,128]{1,0:T(8,128)(2,1)S(1)}, bf16[528,128]{1,0:T(8,128)(2,1)S(1)}, u32[]{:S(2)}, u32[]{:S(2)}) collective-permute-start(bf16[528,128]{1,0:T(8,128)(2,1)S(1)} %root_block.6), channel_id=1, source_target_pairs={{0,4},{4,0},{8,12},{12,8},{1,5},{5,1},{9,13},{13,9},{2,6},{6,2},{1... | collective-permute-start | bytes 405512 | tf_op jit(solution)/shard_map/ppermute | solution.py:31
  36.4 9.7 %collective-permute-start.9 = (bf16[528,128]{1,0:T(8,128)(2,1)S(1)}, bf16[528,128]{1,0:T(8,128)(2,1)S(1)}, u32[]{:S(2)}, u32[]{:S(2)}) collective-permute-start(bf16[528,128]{1,0:T(8,128)(2,1)S(1)} %root_block.7), channel_id=1, source_target_pairs={{0,8},{4,12},{8,0},{12,4},{1,9},{5,13},{9,1},{13,5},{2,10},{6,14},... | collective-permute-start | bytes 405512 | tf_op jit(solution)/shard_map/ppermute | solution.py:31

commit v2 on v1

--- a/solution.py
+++ b/solution.py
@@ -13,6 +13,8 @@
 lane_count = 128
 stat_pieces = 3
 vmem_grant = 40 * 2**20
+branch_grant = 58 * 2**20
+chunk_tokens = 256
 
 
 def vmem_spec():
@@ -23,8 +25,20 @@
     return pl.BlockSpec(memory_space=pltpu.SMEM)
 
 
-def kernel_params():
-    return pltpu.CompilerParams(vmem_limit_bytes=vmem_grant)
+def any_specs(operands):
+    return [pl.BlockSpec(memory_space=pl.ANY)] * len(operands)
+
+
+def ordered(kernel, after):
+    return lambda *refs: kernel(*refs[len(after) :])
+
+
+def light_cost():
+    return pl.CostEstimate(flops=1, bytes_accessed=1, transcendentals=0)
+
+
+def kernel_params(grant=vmem_grant):
+    return pltpu.CompilerParams(vmem_limit_bytes=grant)
 
 
 def exchange(value, axis, apart):
@@ -129,40 +143,46 @@
     return block.reshape(block.shape[0] * group_size, block.shape[2])
 
 
-def split_heads(source_ref, target_ref, first, heads, base, chunk):
-    tokens = source_ref.shape[0]
+def split_heads(source_ref, target_ref, wide_ref, shared, first, heads, base):
+    tokens = source_ref.shape[0] // shared
+    chunk = wide_ref.shape[0] // shared
 
     @pl.loop(0, tokens // chunk)
     def _(step):
-        block = source_ref[pl.ds(step * chunk, chunk)]
-        block = jnp.swapaxes(block[:, first : first + heads, :], 0, 1)
-        target_ref[:, pl.ds(base + step * chunk, chunk), :] = block
-
-
-def prepare_kernel(pair_ref, ko_ref, vo_ref, kp_ref, vp_ref, k_ref, v_ref):
-    tokens, shared, _ = ko_ref.shape
-    heads = k_ref.shape[0]
-    for choice in range(shared // heads):
-
-        @pl.when(pair_ref[0] == choice)
-        def _():
-            for base, keys, values in ((0, ko_ref, vo_ref), (tokens, kp_ref, vp_ref)):
-                split_heads(keys, k_ref, choice * heads, heads, base, 64)
-                split_heads(values, v_ref, choice * heads, heads, base, 64)
-
-
-def prepare(pair_index, keys, values, other_keys, other_values, heads):
-    tokens, _, width = keys.shape
+        start = pl.multiple_of(step * chunk, chunk)
+        rows = pl.multiple_of(step * (chunk * shared), chunk * shared)
+        wide_ref[...] = source_ref[pl.ds(rows, chunk * shared), :].astype(jnp.float32)
+        for h in range(heads):
+            picked = wide_ref[pl.ds(first + h, chunk, stride=shared), :]
+            target_ref[h, pl.ds(base + start, chunk), :] = picked.astype(target_ref.dtype)
+
+
+def prepare_kernel(shared, pair_ref, ko_ref, vo_ref, kp_ref, vp_ref, k_ref, v_ref, wide_ref):
+    heads, both, _ = k_ref.shape
+    first = pair_ref[0] * heads
+    for base, keys, values in ((0, ko_ref, vo_ref), (both // 2, kp_ref, vp_ref)):
+        split_heads(keys, k_ref, wide_ref, shared, first, heads, base)
+        split_heads(values, v_ref, wide_ref, shared, first, heads, base)
+
+
+def flat(cache):
+    *lead, tokens, shared, width = cache.shape
+    return cache.reshape(*lead, tokens * shared, width)
+
+
+def prepare(pair_index, keys, values, other_keys, other_values, heads, after):
+    tokens, shared, width = keys.shape
     shape = jax.ShapeDtypeStruct((heads, 2 * tokens, width), keys.dtype)
     return pl.pallas_call(
-        prepare_kernel,
+        ordered(functools.partial(prepare_kernel, shared), after),
         out_shape=(shape, shape),
-        in_specs=[smem_spec()] + [vmem_spec()] * 4,
+        in_specs=any_specs(after) + [smem_spec()] + [vmem_spec()] * 4,
         out_specs=(vmem_spec(), vmem_spec()),
+        scratch_shapes=[pltpu.VMEM((chunk_tokens * shared, width), jnp.float32)],
         compiler_params=kernel_params(),
-        cost_estimate=pl.CostEstimate(flops=0, bytes_accessed=8 * 2**20, transcendentals=0),
+        cost_estimate=light_cost(),
         name="root_prepare",
-    )(pair_index, keys, values, other_keys, other_values)
+    )(*after, pair_index, flat(keys), flat(values), flat(other_keys), flat(other_values))
 
 
 def root_kernel(scale, group_size, query_ref, k_ref, v_ref, out_ref):
@@ -178,41 +198,59 @@
     store_packed(out_ref, heads, requests, group_size, outs, levels, same)
 
 
-def root_block(query, keys, values, scale):
+def root_block(query, keys, values, scale, after):
     requests, local_heads, width = query.shape
     heads, tokens, _ = keys.shape
     rows = requests * local_heads
     return pl.pallas_call(
-        functools.partial(root_kernel, scale, local_heads // heads),
+        ordered(functools.partial(root_kernel, scale, local_heads // heads), after),
         out_shape=jax.ShapeDtypeStruct((rows + stat_rows(rows), width), query.dtype),
-        in_specs=[vmem_spec()] * 3,
+        in_specs=any_specs(after) + [vmem_spec()] * 3,
         out_specs=vmem_spec(),
         compiler_params=kernel_params(),
-        cost_estimate=pl.CostEstimate(
-            flops=4 * rows * tokens * width, bytes_accessed=6 * 2**20, transcendentals=rows * tokens
-        ),
+        cost_estimate=light_cost(),
         name="root_block",
-    )(query, keys, values)
+    )(*after, query, keys, values)
 
 
 def branch_kernel(
-    scale, group_size, pair_ref, branch_ref, seen_ref, mine_ref, theirs_ref, bk_ref, bv_ref,
-    mine_out, theirs_out, k_ref, v_ref, limit_ref,
+    scale, group_size, pair_ref, mine_ref, theirs_ref, branch_hbm, seen_hbm, bk_hbm, bv_hbm,
+    mine_out, theirs_out, branch_ref, seen_ref, bk_ref, bv_ref, k_ref, v_ref, limit_ref,
+    wide_ref, small_sems, large_sems,
 ):
     requests, local_heads, _ = mine_ref.shape
-    branches, tokens, shared, _ = bk_ref.shape
+    branches, shared, tokens, _ = k_ref.shape
     heads = local_heads // group_size
+    small = [
+        pltpu.make_async_copy(source, target, small_sems.at[i])
+        for i, (source, target) in enumerate(
+            ((branch_hbm, branch_ref), (seen_hbm, seen_ref))
+        )
+    ]
+    large = [
+        [
+            pltpu.make_async_copy(source.at[b], target.at[b], large_sems.at[b, i])
+            for i, (source, target) in enumerate(((bk_hbm, bk_ref), (bv_hbm, bv_ref)))
+        ]
+        for b in range(branches)
+    ]
+    for copy in small + sum(large, []):
+        copy.start()
+    for copy in small:
+        copy.wait()
     pair = pair_ref[0]
     same = identity_mask()
     for b in range(branches):
-        split_heads(bk_ref.at[b], k_ref.at[b], 0, shared, 0, 64)
-        split_heads(bv_ref.at[b], v_ref.at[b], 0, shared, 0, 64)
         for r in range(requests):
             here = branch_ref[r] % branches == b
             limit = jnp.where(here, seen_ref[r] - pair * tokens, 0)
             limit_ref[b, pl.ds(r * group_size, group_size), :] = jnp.full(
                 (group_size, lane_count), limit, jnp.int32
             )
+    for b in range(branches):
+        for copy, source, target in zip(large[b], (bk_ref, bv_ref), (k_ref, v_ref)):
+            copy.wait()
+            split_heads(source.at[b], target.at[b], wide_ref, shared, 0, shared, 0)
     for query_ref, out_ref, owner in ((mine_ref, mine_out, pair), (theirs_ref, theirs_out, 1 - pair)):
         outs, levels = [], []
         for h in range(heads):
@@ -241,24 +279,30 @@
     rows = requests * local_heads
     group_size = local_heads // heads
     shape = jax.ShapeDtypeStruct((rows + stat_rows(rows), width), mine.dtype)
+    raw = pltpu.VMEM((branches, tokens * shared, width), keys.dtype)
     held = pltpu.VMEM((branches, shared, tokens, width), keys.dtype)
-    count = 2 * rows * branches * tokens
+    from_hbm = (branch, seen, flat(keys), flat(values))
     return pl.pallas_call(
         functools.partial(branch_kernel, scale, group_size),
         out_shape=(shape, shape),
-        in_specs=[smem_spec()] * 3 + [vmem_spec()] * 4,
+        in_specs=[smem_spec(), vmem_spec(), vmem_spec()] + [pl.BlockSpec(memory_space=pltpu.HBM)] * len(from_hbm),
         out_specs=(vmem_spec(), vmem_spec()),
         scratch_shapes=[
+            pltpu.SMEM(branch.shape, branch.dtype),
+            pltpu.SMEM(seen.shape, seen.dtype),
+            raw,
+            raw,
             held,
             held,
             pltpu.VMEM((branches, requests * group_size, lane_count), jnp.int32),
+            pltpu.VMEM((chunk_tokens * shared, width), jnp.float32),
+            pltpu.SemaphoreType.DMA((2,)),
+            pltpu.SemaphoreType.DMA((branches, 2)),
         ],
-        compiler_params=kernel_params(),
-        cost_estimate=pl.CostEstimate(
-            flops=4 * count * width, bytes_accessed=12 * 2**20, transcendentals=count
-        ),
+        compiler_params=kernel_params(branch_grant),
+        cost_estimate=light_cost(),
         name="branch_block",
-    )(pair_index, branch, seen, mine, theirs, keys, values)
+    )(pair_index, mine, theirs, *from_hbm)
 
 
 def merge_kernel(last, heads, requests, group_size, *refs):
@@ -285,20 +329,20 @@
         store_packed(out_ref, heads, requests, group_size, outs, levels, same)
 
 
-def merge(parts, last, heads, requests, group_size):
+def merge(parts, last, heads, requests, group_size, after=()):
     if last:
         shape = (requests, heads * group_size, lane_count)
     else:
         shape = parts[0].shape
     return pl.pallas_call(
-        functools.partial(merge_kernel, last, heads, requests, group_size),
+        ordered(functools.partial(merge_kernel, last, heads, requests, group_size), after),
         out_shape=jax.ShapeDtypeStruct(shape, parts[0].dtype),
-        in_specs=[vmem_spec()] * len(parts),
+        in_specs=any_specs(after) + [vmem_spec()] * len(parts),
         out_specs=vmem_spec(),
         compiler_params=kernel_params(),
-        cost_estimate=pl.CostEstimate(flops=0, bytes_accessed=2**20, transcendentals=0),
+        cost_estimate=light_cost(),
         name="merge_last" if last else "merge_some",
-    )(*parts)
+    )(*after, *parts)
 
 
 def local(queries, root_keys, root_values, branch_keys, branch_values, request_branch, seen_tokens):
@@ -316,23 +360,31 @@
     arrived = {}
     for apart in range(blocks - 1, 0, -2):
         arrived[apart] = exchange(queries, "blk", apart)
-    for apart in range(blocks - 1, 2, -2):
-        arrived[apart ^ 1] = exchange(arrived[apart], "blk", 1)
-
-    keys, values = prepare(pair_index, root_keys, root_values, other_keys, other_values, heads)
-    near = [root_block(queries, keys, values, scale)]
-    returned = {}
-    for apart in arrived:
-        returned[apart] = exchange(root_block(arrived[apart], keys, values, scale), "blk", apart)
+
     mine, theirs = branch_block(
         pair_index, request_branch, seen_tokens, queries, other_queries,
         branch_keys, branch_values, scale, heads,
     )
-    near += [mine, exchange(theirs, "pair", 1)]
-    order = list(returned)
-    near += [returned[apart] for apart in order[:-1]]
-    most = merge(near, False, heads, requests, group_size)
-    return merge([most, returned[order[-1]]], True, heads, requests, group_size)
+    from_partner = exchange(theirs, "pair", 1)
+    direct = list(arrived)
+    *held, mine = lax.optimization_barrier((*arrived.values(), mine))
+    arrived = dict(zip(direct, held))
+    for apart in range(blocks - 1, 2, -2):
+        arrived[apart ^ 1] = exchange(arrived[apart], "blk", 1)
+    keys, values = prepare(
+        pair_index, root_keys, root_values, other_keys, other_values, heads, (mine,)
+    )
+    partials, previous = {}, ()
+    for apart in sorted(arrived, key=lambda a: (a == 1, -a)):
+        partials[apart] = root_block(arrived[apart], keys, values, scale, previous)
+        previous = (partials[apart],)
+    returned = {apart: exchange(partials[apart], "blk", apart) for apart in sorted(partials)}
+    own = root_block(queries, keys, values, scale, previous)
+    late = [returned.pop(apart) for apart in (2, 1) if apart in returned]
+    most = merge([own, mine, from_partner, *returned.values()], False, heads, requests, group_size)
+    for part in late[:-1]:
+        most = merge([most, part], False, heads, requests, group_size)
+    return merge([most, late[-1]], True, heads, requests, group_size)
 
 
 def solution(mesh):

time: 47.5 us -> 38.8 us (0.82)
  waiting for transfers between devices: 10 us -> 4.43 us
  local copies, waits for them, and re-layouts: 5.41 us -> 1.57 us
  Pallas kernels: 19.6 us -> 20.3 us
    ppermute x10, waiting for transfers between devices: 10 us -> 4.43 us  [exchange(): lax.ppermute(value, axis, [(i, i ^ apart) for i in range(lax.axis_size(ax...]
    unnamed x16 -> x10, local copies, waits for them, and re-layouts: 5.41 us -> 1.57 us
    pallas_call x1, Pallas kernels: 8 us -> 9.08 us  [branch_block(): pl.pallas_call(functools.partial(branch_kernel, scale, group_size), out_s...]
    pallas_call x7 -> x8, Pallas kernels: 11.6 us -> 11.2 us  [the longest x4 7.57 us: root_block(): pl.pallas_call(ordered(functools.partial(root_kernel, scale, local_heads...]
  transfers between devices with their start and end apart: 10 -> 10, of which waited for: 3 -> 1; matrix products, arithmetic and copies ran while one was open for 0% -> 0% of each run, Pallas kernels for 39% -> 50%
where the time goes in v2:
time: 38.8 us; the launch traced here: 38.6 us
  Pallas kernels  20.3 us (52%)
  starting transfers between devices  12.2 us (31%)
  waiting for transfers between devices  4.43 us (11%)
  local copies, waits for them, and re-layouts  1.57 us (4%)
    ppermute x10, starting transfers between devices, exchange(): lax.ppermute(value, axis, [(i, i ^ apart) for i in range(lax.axis_size(ax...  12.2 us
    pallas_call x1, Pallas kernels, branch_block(): pl.pallas_call(functools.partial(branch_kernel, scale, group_size), out_s...  9.08 us
    pallas_call x4, Pallas kernels, root_block(): pl.pallas_call(ordered(functools.partial(root_kernel, scale, local_heads...  7.57 us
    ppermute x10, waiting for transfers between devices, exchange(): lax.ppermute(value, axis, [(i, i ^ apart) for i in range(lax.axis_size(ax...  4.43 us
    pallas_call x3, Pallas kernels, merge(): pl.pallas_call(ordered(functools.partial(merge_kernel, last, heads, reque...  2.55 us
    unnamed x10, local copies, waits for them, and re-layouts  1.57 us
    pallas_call x1, Pallas kernels, prepare(): pl.pallas_call(ordered(functools.partial(prepare_kernel, shared), after),...  1.09 us
  transfers between devices with their start and end apart: 10, of which 1 were waited for; matrix products, arithmetic and copies ran while one was open for 0% of the time, Pallas kernels for 50%

profile of v2, /device:TPU:0, one launch (start us, length us, event | category | flops | bytes accessed | tf_op | source)
XLA Modules:
  0.0 38.6 jit_solution(2334823379566113381)
XLA Ops:
  0.0 0.5 %collective-permute-start.3 = (bf16[1024,4,128]{2,1,0:T(4,128)(2,1)}, bf16[1024,4,128]{2,1,0:T(4,128)(2,1)S(1)}, u32[]{:S(2)}, u32[]{:S(2)}) collective-permute-start(bf16[1024,4,128]{2,1,0:T(4,128)(2,1)} %param.8), channel_id=1, source_target_pairs={{0,1},{1,0},{2,3},{3,2},{4,5},{5,4},{6,7},{7,6},{8,9},{9,8},{10,11... | collective-permute-start | bytes 3145736 | tf_op jit(solution)/shard_map/ppermute | solution.py:45
  0.5 0.1 collective-permute-start.4
  0.5 0.5 %collective-permute-start.2 = (bf16[16,32,128]{2,1,0:T(8,128)(2,1)}, bf16[16,32,128]{2,1,0:T(8,128)(2,1)S(1)}, u32[]{:S(2)}, u32[]{:S(2)}) collective-permute-start(bf16[16,32,128]{2,1,0:T(8,128)(2,1)} %refs_1_.1), channel_id=1, source_target_pairs={{0,1},{1,0},{2,3},{3,2},{4,5},{5,4},{6,7},{7,6},{8,9},{9,8},{10,11... | collective-permute-start | bytes 393224 | tf_op jit(solution)/shard_map/ppermute | solution.py:45
  1.0 4.6 %collective-permute-start = (bf16[16,32,128]{2,1,0:T(8,128)(2,1)}, bf16[16,32,128]{2,1,0:T(8,128)(2,1)S(1)}, u32[]{:S(2)}, u32[]{:S(2)}) collective-permute-start(bf16[16,32,128]{2,1,0:T(8,128)(2,1)} %refs_1_.1), channel_id=1, source_target_pairs={{0,12},{4,8},{8,4},{12,0},{1,13},{5,9},{9,5},{13,1},{2,14},{6,10},... | collective-permute-start | bytes 393224 | tf_op jit(solution)/shard_map/ppermute | solution.py:45
  5.6 0.0 collective-permute-start.1
  5.6 0.0 collective-permute-done.2.theirs_ref
  5.6 0.7 %copy-done.4 = bf16[16,32,128]{2,1,0:T(8,128)(2,1)} copy-done((bf16[16,32,128]{2,1,0:T(8,128)(2,1)}, bf16[16,32,128]{2,1,0:T(8,128)(2,1)S(1)}, u32[]{:S(2)}) %copy-start.4) | copy-done | bytes 131096
  6.2 9.1 %branch_block.1 = (bf16[528,128]{1,0:T(8,128)(2,1)}, bf16[528,128]{1,0:T(8,128)(2,1)}) custom-call(s32[1]{0:T(128)} %bitcast.pair_ref.refs_1_, bf16[16,32,128]{2,1,0:T(8,128)(2,1)} %refs_1_.1, bf16[16,32,128]{2,1,0:T(8,128)(2,1)} %copy-done.4, s32[16]{0:T(128)} %branch_hbm.1, s32[16]{0:T(128)} %seen_hbm.1, bf16[2,4096,128]{2,1,0:T(8,128)(2,1)} %bitcast.11, ...), custom_call_target="tpu_custom_call" | custom-call | flops 1 | bytes 1 | tf_op jit(solution)/shard_map/branch_block/pallas_call | solution.py:285
  15.3 0.0 collective-permute-done.1.refs_1_
  15.3 2.1 %collective-permute-start.5 = (bf16[16,32,128]{2,1,0:T(8,128)(2,1)S(1)}, bf16[16,32,128]{2,1,0:T(8,128)(2,1)S(1)}, u32[]{:S(2)}, u32[]{:S(2)}) collective-permute-start(bf16[16,32,128]{2,1,0:T(8,128)(2,1)S(1)} %collective-permute-done.refs_0_), channel_id=1, source_target_pairs={{0,4},{4,0},{8,12},{12,8},{1,5},{5,1},{9,13},{13,9},{2,6},{6,2},{1... | collective-permute-start | bytes 393224 | tf_op jit(solution)/shard_map/ppermute | solution.py:45
  17.5 0.9 %copy-done.2 = bf16[528,128]{1,0:T(8,128)(2,1)S(1)} copy-done((bf16[528,128]{1,0:T(8,128)(2,1)S(1)}, bf16[528,128]{1,0:T(8,128)(2,1)}, u32[]{:S(2)}) %copy-start.2) | copy-done | bytes 135192
  18.4 1.1 %root_prepare.1 = (bf16[2,2048,128]{2,1,0:T(8,128)(2,1)S(1)}, bf16[2,2048,128]{2,1,0:T(8,128)(2,1)S(1)}) custom-call(bf16[528,128]{1,0:T(8,128)(2,1)S(1)} %copy-done.2, s32[1]{0:T(128)} %bitcast.pair_ref.refs_1_, bf16[4096,128]{1,0:T(8,128)(2,1)S(1)} %bitcast.7, bf16[4096,128]{1,0:T(8,128)(2,1)S(1)} %bitcast.8, bf16[4096,128]{1,0:T(8,128)(2,1)S(1)} %bitcast.9, ...), custom_call_target="tpu_custom_call" | custom-call | flops 1 | bytes 1 | tf_op jit(solution)/shard_map/root_prepare/pallas_call | solution.py:176
  19.5 1.9 %root_block.4.refs_0_ = bf16[528,128]{1,0:T(8,128)(2,1)S(1)} custom-call(bf16[16,32,128]{2,1,0:T(8,128)(2,1)S(1)} %collective-permute-done.refs_0_, bf16[2,2048,128]{2,1,0:T(8,128)(2,1)S(1)} %get-tuple-element.15.refs_1_.refs_2_, bf16[2,2048,128]{2,1,0:T(8,128)(2,1)S(1)} %get-tuple-element.16.refs_2_.refs_3_), custom_call_target="tpu_custom_call" | custom-call | flops 1 | bytes 1 | tf_op jit(solution)/shard_map/root_block/pallas_call | solution.py:205
  21.4 0.0 copy-start.3
  21.4 2.5 %collective-permute-start.7 = (bf16[528,128]{1,0:T(8,128)(2,1)S(1)}, bf16[528,128]{1,0:T(8,128)(2,1)S(1)}, u32[]{:S(2)}, u32[]{:S(2)}) collective-permute-start(bf16[528,128]{1,0:T(8,128)(2,1)S(1)} %root_block.4.refs_0_), channel_id=1, source_target_pairs={{0,12},{4,8},{8,4},{12,0},{1,13},{5,9},{9,5},{13,1},{2,14},{6,10},... | collective-permute-start | bytes 405512 | tf_op jit(solution)/shard_map/ppermute | solution.py:45
  23.9 1.9 %root_block.5.refs_0_ = bf16[528,128]{1,0:T(8,128)(2,1)S(1)} custom-call(bf16[528,128]{1,0:T(8,128)(2,1)S(1)} %root_block.4.refs_0_, bf16[16,32,128]{2,1,0:T(8,128)(2,1)S(1)} %collective-permute-done.5.refs_1_, bf16[2,2048,128]{2,1,0:T(8,128)(2,1)S(1)} %get-tuple-element.15.refs_1_.refs_2_, bf16[2,2048,128]{2,1,0:T(8,128)(2,1)S(1)} %get-tuple-element.16.refs_2_.refs_3_), custom_call_target="tpu_custom_call" | custom-call | flops 1 | bytes 1 | tf_op jit(solution)/shard_map/root_block/pallas_call | solution.py:205
  25.8 0.2 collective-permute-start.8
  26.0 1.9 %root_block.6.refs_0_ = bf16[528,128]{1,0:T(8,128)(2,1)S(1)} custom-call(bf16[528,128]{1,0:T(8,128)(2,1)S(1)} %root_block.5.refs_0_, bf16[16,32,128]{2,1,0:T(8,128)(2,1)S(1)} %collective-permute-done.1.refs_1_, bf16[2,2048,128]{2,1,0:T(8,128)(2,1)S(1)} %get-tuple-element.15.refs_1_.refs_2_, bf16[2,2048,128]{2,1,0:T(8,128)(2,1)S(1)} %get-tuple-element.16.refs_2_.refs_3_), custom_call_target="tpu_custom_call" | custom-call | flops 1 | bytes 1 | tf_op jit(solution)/shard_map/root_block/pallas_call | solution.py:205
  27.9 1.9 %collective-permute-start.9 = (bf16[528,128]{1,0:T(8,128)(2,1)S(1)}, bf16[528,128]{1,0:T(8,128)(2,1)S(1)}, u32[]{:S(2)}, u32[]{:S(2)}) collective-permute-start(bf16[528,128]{1,0:T(8,128)(2,1)S(1)} %root_block.6.refs_0_), channel_id=1, source_target_pairs={{0,4},{4,0},{8,12},{12,8},{1,5},{5,1},{9,13},{13,9},{2,6},{6,2},{1... | collective-permute-start | bytes 405512 | tf_op jit(solution)/shard_map/ppermute | solution.py:45
  29.8 1.9 %root_block.7.refs_0_ = bf16[528,128]{1,0:T(8,128)(2,1)S(1)} custom-call(bf16[528,128]{1,0:T(8,128)(2,1)S(1)} %root_block.6.refs_0_, bf16[16,32,128]{2,1,0:T(8,128)(2,1)S(1)} %copy-done.3, bf16[2,2048,128]{2,1,0:T(8,128)(2,1)S(1)} %get-tuple-element.15.refs_1_.refs_2_, bf16[2,2048,128]{2,1,0:T(8,128)(2,1)S(1)} %get-tuple-element.16.refs_2_.refs_3_), custom_call_target="tpu_custom_call" | custom-call | flops 1 | bytes 1 | tf_op jit(solution)/shard_map/root_block/pallas_call | solution.py:205
  31.7 0.9 %merge_some.2.refs_0_ = bf16[528,128]{1,0:T(8,128)(2,1)S(1)} custom-call(bf16[528,128]{1,0:T(8,128)(2,1)S(1)} %root_block.7.refs_0_, bf16[528,128]{1,0:T(8,128)(2,1)S(1)} %copy-done.2, bf16[528,128]{1,0:T(8,128)(2,1)S(1)} %collective-permute-done.6.refs_2_, bf16[528,128]{1,0:T(8,128)(2,1)S(1)} %collective-permute-done.7.refs_3_), custom_call_target="tpu_custom_call" | custom-call | flops 1 | bytes 1 | tf_op jit(solution)/shard_map/merge_some/pallas_call | solution.py:337
  32.5 4.4 %collective-permute-done.8.refs_1_ = bf16[528,128]{1,0:T(8,128)(2,1)S(1)} collective-permute-done((bf16[528,128]{1,0:T(8,128)(2,1)S(1)}, bf16[528,128]{1,0:T(8,128)(2,1)S(1)}, u32[]{:S(2)}, u32[]{:S(2)}) %collective-permute-start.8) | collective-permute-done | bytes 135200 | tf_op jit(solution)/shard_map/ppermute | solution.py:45
  37.0 0.6 %merge_some.3.refs_0_ = bf16[528,128]{1,0:T(8,128)(2,1)S(1)} custom-call(bf16[528,128]{1,0:T(8,128)(2,1)S(1)} %merge_some.2.refs_0_, bf16[528,128]{1,0:T(8,128)(2,1)S(1)} %collective-permute-done.8.refs_1_), custom_call_target="tpu_custom_call" | custom-call | flops 1 | bytes 1 | tf_op jit(solution)/shard_map/merge_some/pallas_call | solution.py:337
  37.5 1.1 %merge_last.1 = bf16[16,32,128]{2,1,0:T(8,128)(2,1)} custom-call(bf16[528,128]{1,0:T(8,128)(2,1)S(1)} %merge_some.3.refs_0_, bf16[528,128]{1,0:T(8,128)(2,1)S(1)} %collective-permute-done.9.refs_1_), custom_call_target="tpu_custom_call" | custom-call | flops 1 | bytes 1 | tf_op jit(solution)/shard_map/merge_last/pallas_call | solution.py:337
  (15 shorter events, 0.0 us)
Async XLA Ops:
  0.0 17.4 %collective-permute-start.3 = (bf16[1024,4,128]{2,1,0:T(4,128)(2,1)}, bf16[1024,4,128]{2,1,0:T(4,128)(2,1)S(1)}, u32[]{:S(2)}, u32[]{:S(2)}) collective-permute-start(bf16[1024,4,128]{2,1,0:T(4,128)(2,1)} %param.8), channel_id=1, source_target_pairs={{0,1},{1,0},{2,3},{3,2},{4,5},{5,4},{6,7},{7,6},{8,9},{9,8},{10,11... | collective-permute-start | bytes 3145736 | tf_op jit(solution)/shard_map/ppermute | solution.py:45
  0.5 17.0 %collective-permute-start.4 = (bf16[1024,4,128]{2,1,0:T(4,128)(2,1)}, bf16[1024,4,128]{2,1,0:T(4,128)(2,1)S(1)}, u32[]{:S(2)}, u32[]{:S(2)}) collective-permute-start(bf16[1024,4,128]{2,1,0:T(4,128)(2,1)} %param.9), channel_id=1, source_target_pairs={{0,1},{1,0},{2,3},{3,2},{4,5},{5,4},{6,7},{7,6},{8,9},{9,8},{10,11... | collective-permute-start | bytes 3145736 | tf_op jit(solution)/shard_map/ppermute | solution.py:45
  0.5 5.1 %collective-permute-start.2 = (bf16[16,32,128]{2,1,0:T(8,128)(2,1)}, bf16[16,32,128]{2,1,0:T(8,128)(2,1)S(1)}, u32[]{:S(2)}, u32[]{:S(2)}) collective-permute-start(bf16[16,32,128]{2,1,0:T(8,128)(2,1)} %refs_1_.1), channel_id=1, source_target_pairs={{0,1},{1,0},{2,3},{3,2},{4,5},{5,4},{6,7},{7,6},{8,9},{9,8},{10,11... | collective-permute-start | bytes 393224 | tf_op jit(solution)/shard_map/ppermute | solution.py:45
  1.0 14.4 %collective-permute-start = (bf16[16,32,128]{2,1,0:T(8,128)(2,1)}, bf16[16,32,128]{2,1,0:T(8,128)(2,1)S(1)}, u32[]{:S(2)}, u32[]{:S(2)}) collective-permute-start(bf16[16,32,128]{2,1,0:T(8,128)(2,1)} %refs_1_.1), channel_id=1, source_target_pairs={{0,12},{4,8},{8,4},{12,0},{1,13},{5,9},{9,5},{13,1},{2,14},{6,10},... | collective-permute-start | bytes 393224 | tf_op jit(solution)/shard_map/ppermute | solution.py:45
  5.6 9.8 %collective-permute-start.1 = (bf16[16,32,128]{2,1,0:T(8,128)(2,1)}, bf16[16,32,128]{2,1,0:T(8,128)(2,1)S(1)}, u32[]{:S(2)}, u32[]{:S(2)}) collective-permute-start(bf16[16,32,128]{2,1,0:T(8,128)(2,1)} %refs_1_.1), channel_id=1, source_target_pairs={{0,4},{4,0},{8,12},{12,8},{1,5},{5,1},{9,13},{13,9},{2,6},{6,2},{1... | collective-permute-start | bytes 393224 | tf_op jit(solution)/shard_map/ppermute | solution.py:45
  5.6 0.7 %copy-start.4 = (bf16[16,32,128]{2,1,0:T(8,128)(2,1)}, bf16[16,32,128]{2,1,0:T(8,128)(2,1)S(1)}, u32[]{:S(2)}) copy-start(bf16[16,32,128]{2,1,0:T(8,128)(2,1)S(1)} %collective-permute-done.2.theirs_ref) | copy-start | bytes 393220
  6.2 11.2 %copy-start = (bf16[1024,4,128]{2,1,0:T(4,128)(2,1)S(1)}, bf16[1024,4,128]{2,1,0:T(4,128)(2,1)}, u32[]{:S(2)}) copy-start(bf16[1024,4,128]{2,1,0:T(4,128)(2,1)} %param.8) | copy-start | bytes 3145732
  6.2 11.2 %copy-start.1 = (bf16[1024,4,128]{2,1,0:T(4,128)(2,1)S(1)}, bf16[1024,4,128]{2,1,0:T(4,128)(2,1)}, u32[]{:S(2)}) copy-start(bf16[1024,4,128]{2,1,0:T(4,128)(2,1)} %param.9) | copy-start | bytes 3145732
  15.3 8.6 %collective-permute-start.5 = (bf16[16,32,128]{2,1,0:T(8,128)(2,1)S(1)}, bf16[16,32,128]{2,1,0:T(8,128)(2,1)S(1)}, u32[]{:S(2)}, u32[]{:S(2)}) collective-permute-start(bf16[16,32,128]{2,1,0:T(8,128)(2,1)S(1)} %collective-permute-done.refs_0_), channel_id=1, source_target_pairs={{0,4},{4,0},{8,12},{12,8},{1,5},{5,1},{9,13},{13,9},{2,6},{6,2},{1... | collective-permute-start | bytes 393224 | tf_op jit(solution)/shard_map/ppermute | solution.py:45
  17.4 14.2 %collective-permute-start.6 = (bf16[528,128]{1,0:T(8,128)(2,1)}, bf16[528,128]{1,0:T(8,128)(2,1)S(1)}, u32[]{:S(2)}, u32[]{:S(2)}) collective-permute-start(bf16[528,128]{1,0:T(8,128)(2,1)} %get-tuple-element.18), channel_id=1, source_target_pairs={{0,1},{1,0},{2,3},{3,2},{4,5},{5,4},{6,7},{7,6},{8,9},{9,8},{10,11... | collective-permute-start | bytes 405512 | tf_op jit(solution)/shard_map/ppermute | solution.py:45
  17.5 0.9 %copy-start.2 = (bf16[528,128]{1,0:T(8,128)(2,1)S(1)}, bf16[528,128]{1,0:T(8,128)(2,1)}, u32[]{:S(2)}) copy-start(bf16[528,128]{1,0:T(8,128)(2,1)} %get-tuple-element.14.refs_0_.refs_1_) | copy-start | bytes 405508
  21.4 8.4 %copy-start.3 = (bf16[16,32,128]{2,1,0:T(8,128)(2,1)S(1)}, bf16[16,32,128]{2,1,0:T(8,128)(2,1)}, u32[]{:S(2)}) copy-start(bf16[16,32,128]{2,1,0:T(8,128)(2,1)} %refs_1_.1) | copy-start | bytes 393220
  21.4 10.3 %collective-permute-start.7 = (bf16[528,128]{1,0:T(8,128)(2,1)S(1)}, bf16[528,128]{1,0:T(8,128)(2,1)S(1)}, u32[]{:S(2)}, u32[]{:S(2)}) collective-permute-start(bf16[528,128]{1,0:T(8,128)(2,1)S(1)} %root_block.4.refs_0_), channel_id=1, source_target_pairs={{0,12},{4,8},{8,4},{12,0},{1,13},{5,9},{9,5},{13,1},{2,14},{6,10},... | collective-permute-start | bytes 405512 | tf_op jit(solution)/shard_map/ppermute | solution.py:45
  25.8 11.1 %collective-permute-start.8 = (bf16[528,128]{1,0:T(8,128)(2,1)S(1)}, bf16[528,128]{1,0:T(8,128)(2,1)S(1)}, u32[]{:S(2)}, u32[]{:S(2)}) collective-permute-start(bf16[528,128]{1,0:T(8,128)(2,1)S(1)} %root_block.5.refs_0_), channel_id=1, source_target_pairs={{0,8},{4,12},{8,0},{12,4},{1,9},{5,13},{9,1},{13,5},{2,10},{6,14},... | collective-permute-start | bytes 405512 | tf_op jit(solution)/shard_map/ppermute | solution.py:45
  27.9 9.6 %collective-permute-start.9 = (bf16[528,128]{1,0:T(8,128)(2,1)S(1)}, bf16[528,128]{1,0:T(8,128)(2,1)S(1)}, u32[]{:S(2)}, u32[]{:S(2)}) collective-permute-start(bf16[528,128]{1,0:T(8,128)(2,1)S(1)} %root_block.6.refs_0_), channel_id=1, source_target_pairs={{0,4},{4,0},{8,12},{12,8},{1,5},{5,1},{9,13},{13,9},{2,6},{6,2},{1... | collective-permute-start | bytes 405512 | tf_op jit(solution)/shard_map/ppermute | solution.py:45

commit v3 on v2

v3 whole, which is shorter than its diff:
```python
import functools
import math

import jax
import jax.numpy as jnp
from jax import lax
from jax.experimental import pallas as pl
from jax.experimental.pallas import tpu as pltpu
from jax.sharding import PartitionSpec as P

masked_floor = -1e30
lowest_reference = -1e29
lane_count = 128
stat_pieces = 3
vmem_grant = 24 * 2**20
chunk_tokens = 256
least_total = 2.0**-60
most_total = 2.0**100


def vmem_spec():
    return pl.BlockSpec(memory_space=pltpu.VMEM)


def smem_spec():
    return pl.BlockSpec(memory_space=pltpu.SMEM)


def any_specs(operands):
    return [pl.BlockSpec(memory_space=pl.ANY)] * len(operands)


def ordered(kernel, after):
    return lambda *refs: kernel(*refs[len(after) :])


def light_cost():
    return pl.CostEstimate(flops=1, bytes_accessed=1, transcendentals=0)


def kernel_params(grant=vmem_grant):
    return pltpu.CompilerParams(vmem_limit_bytes=grant)


def exchange(value, axis, apart):
    return lax.ppermute(value, axis, [(i, i ^ apart) for i in range(lax.axis_size(axis))])


def stat_rows(rows):
    return -(-stat_pieces * (rows // lane_count) // 16) * 16


def identity_mask():
    shape = (lane_count, lane_count)
    return lax.broadcasted_iota(jnp.int32, shape, 0) == lax.broadcasted_iota(jnp.int32, shape, 1)


def column_to_rows(column, same):
    pieces = []
    for start in range(0, column.shape[0], lane_count):
        wide = jnp.broadcast_to(column[start : start + lane_count], (lane_count, lane_count))
        pieces.append(jnp.sum(jnp.where(same, wide, 0.0), axis=0, keepdims=True))
    return pieces


def rows_to_column(pieces, same):
    columns = []
    for piece in pieces:
        wide = jnp.broadcast_to(piece, (lane_count, lane_count))
        columns.append(jnp.sum(jnp.where(same, wide, 0.0), axis=1, keepdims=True))
    return jnp.concatenate(columns, axis=0)


def split_stat(value):
    pieces = []
    for _ in range(stat_pieces):
        piece = value.astype(jnp.bfloat16)
        pieces.append(piece)
        value = value - piece.astype(jnp.float32)
    return pieces


def evaluate(pieces, scale, exact):
    state = None
    visible = None
    for query, keys, values, limits in pieces:
        scores = lax.dot_general(
            query, keys, (((1,), (1,)), ((), ())), preferred_element_type=jnp.float32
        )
        seen = None
        if limits is not None:
            seen = lax.broadcasted_iota(jnp.int32, scores.shape, 1) < limits
            some = limits > 0
            visible = some if visible is None else visible | some
        if exact:
            if seen is not None:
                scores = jnp.where(seen, scores, masked_floor)
            largest = jnp.max(scores, axis=1, keepdims=True)
            if seen is not None:
                largest = jnp.maximum(largest, lowest_reference)
            weights = jnp.exp2((scores - largest) * scale)
            largest = largest * scale
        else:
            weights = jnp.exp2(scores * scale)
            if seen is not None:
                weights = jnp.where(seen, weights, 0.0)
        totals = jnp.sum(weights, axis=1, keepdims=True)
        sums = jnp.dot(weights.astype(jnp.bfloat16), values, preferred_element_type=jnp.float32)
        if state is None:
            state = (sums, totals, largest if exact else None)
        elif exact:
            top = jnp.maximum(state[2], largest)
            one, two = jnp.exp2(state[2] - top), jnp.exp2(largest - top)
            state = (state[0] * one + sums * two, state[1] * one + totals * two, top)
        else:
            state = (state[0] + sums, state[1] + totals, None)
    sums, totals, largest = state
    sound = (totals > least_total) & (totals < most_total)
    safe = totals
    if visible is not None:
        sound = sound | jnp.logical_not(visible)
        safe = jnp.where(visible, totals, 1.0)
    level = jnp.log2(safe)
    if exact:
        level = level + largest
    if visible is not None:
        level = jnp.where(visible, level, masked_floor)
    return sums * (1.0 / safe), level, sound


def write_partials(jobs, scale, heads, requests, group_size):
    same = identity_mask()

    def run(exact):
        least = 1.0
        for out_ref, pieces_of in jobs:
            outs, levels = [], []
            for h in range(heads):
                out, level, sound = evaluate(pieces_of(h), scale, exact)
                outs.append(out)
                levels.append(level)
                least = jnp.minimum(least, jnp.where(sound, 1.0, 0.0))
            store_packed(out_ref, heads, requests, group_size, outs, levels, same)
        return jnp.min(least)

    least = run(False)

    @pl.when(least < 0.5)
    def _():
        run(True)


def store_packed(out_ref, heads, requests, group_size, outs, levels, same):
    rows = requests * heads * group_size
    per_head = requests * group_size
    all_rows = []
    for h in range(heads):
        block = outs[h].astype(jnp.bfloat16).reshape(requests, group_size, lane_count)
        for r in range(requests):
            out_ref[pl.ds((r * heads + h) * group_size, group_size), :] = block[r]
        all_rows += column_to_rows(levels[h], same)
    stats = jnp.concatenate(all_rows, axis=0)
    pieces = [piece.astype(jnp.float32) for piece in split_stat(stats)]
    spare = stat_rows(rows) - stat_pieces * stats.shape[0]
    if spare:
        pieces.append(jnp.zeros((spare, lane_count), jnp.float32))
    out_ref[pl.ds(rows, stat_rows(rows)), :] = jnp.concatenate(pieces, axis=0).astype(jnp.bfloat16)


def load_packed(in_ref, heads, requests, group_size, same):
    rows = requests * heads * group_size
    lines = rows // lane_count
    per_head = lines // heads
    stats = in_ref[pl.ds(rows, stat_rows(rows)), :].astype(jnp.float32)
    joined = stats[:lines]
    for piece in range(1, stat_pieces):
        joined = joined + stats[piece * lines : (piece + 1) * lines]
    outs, levels = [], []
    for h in range(heads):
        parts = [
            in_ref[pl.ds((r * heads + h) * group_size, group_size), :] for r in range(requests)
        ]
        outs.append(jnp.concatenate(parts, axis=0).astype(jnp.float32))
        lines_here = [joined[h * per_head + i : h * per_head + i + 1] for i in range(per_head)]
        levels.append(rows_to_column(lines_here, same))
    return outs, levels


def head_queries(query_ref, head, group_size):
    block = query_ref[:, head * group_size : (head + 1) * group_size, :]
    return block.reshape(block.shape[0] * group_size, block.shape[2])


def split_heads(source_ref, target_ref, wide_ref, shared, first, heads, base):
    tokens = source_ref.shape[0] // shared
    chunk = wide_ref.shape[0] // shared

    @pl.loop(0, tokens // chunk)
    def _(step):
        start = pl.multiple_of(step * chunk, chunk)
        rows = pl.multiple_of(step * (chunk * shared), chunk * shared)
        wide_ref[...] = source_ref[pl.ds(rows, chunk * shared), :].astype(jnp.float32)
        for h in range(heads):
            picked = wide_ref[pl.ds(first + h, chunk, stride=shared), :]
            target_ref[h, pl.ds(base + start, chunk), :] = picked.astype(target_ref.dtype)


def flat(cache):
    *lead, tokens, shared, width = cache.shape
    return cache.reshape(*lead, tokens * shared, width)


def packed_shape(query):
    requests, local_heads, width = query.shape
    rows = requests * local_heads
    return jax.ShapeDtypeStruct((rows + stat_rows(rows), width), query.dtype)


def root_pieces(query_ref, k_ref, v_ref, group_size):
    return lambda h: [(head_queries(query_ref, h, group_size), k_ref[h], v_ref[h], None)]


def first_kernel(
    scale, shared, pair_ref, query_ref, ko_ref, vo_ref, kp_ref, vp_ref, k_ref, v_ref, out_ref, wide_ref
):
    heads, both, _ = k_ref.shape
    first = pair_ref[0] * heads
    for base, keys, values in ((0, ko_ref, vo_ref), (both // 2, kp_ref, vp_ref)):
        split_heads(keys, k_ref, wide_ref, shared, first, heads, base)
        split_heads(values, v_ref, wide_ref, shared, first, heads, base)
    requests, local_heads, _ = query_ref.shape
    group_size = local_heads // heads
    pieces = root_pieces(query_ref, k_ref, v_ref, group_size)
    write_partials([(out_ref, pieces)], scale, heads, requests, group_size)


def first_block(pair_index, query, keys, values, other_keys, other_values, scale, heads):
    tokens, shared, width = keys.shape
    shape = jax.ShapeDtypeStruct((heads, 2 * tokens, width), keys.dtype)
    return pl.pallas_call(
        functools.partial(first_kernel, scale, shared),
        out_shape=(shape, shape, packed_shape(query)),
        in_specs=[smem_spec()] + [vmem_spec()] * 5,
        out_specs=(vmem_spec(),) * 3,
        scratch_shapes=[pltpu.VMEM((chunk_tokens * shared, width), jnp.float32)],
        compiler_params=kernel_params(),
        cost_estimate=light_cost(),
        name="first_block",
    )(pair_index, query, flat(keys), flat(values), flat(other_keys), flat(other_values))


def place_kernel(in_ref, out_ref):
    out_ref[0] = in_ref[0]


def place(pair_index):
    return pl.pallas_call(
        place_kernel,
        out_shape=jax.ShapeDtypeStruct(pair_index.shape, pair_index.dtype),
        in_specs=[smem_spec()],
        out_specs=smem_spec(),
        compiler_params=kernel_params(2**20),
        cost_estimate=pl.CostEstimate(flops=10**10, bytes_accessed=1, transcendentals=0),
        name="place",
    )(pair_index)


def root_kernel(scale, count, k_ref, v_ref, *refs):
    heads = k_ref.shape[0]
    requests, local_heads, _ = refs[0].shape
    group_size = local_heads // heads
    jobs = [
        (out_ref, root_pieces(query_ref, k_ref, v_ref, group_size))
        for query_ref, out_ref in zip(refs[:count], refs[count:])
    ]
    write_partials(jobs, scale, heads, requests, group_size)


def root_blocks(queries, keys, values, scale, after):
    return pl.pallas_call(
        ordered(functools.partial(root_kernel, scale, len(queries)), after),
        out_shape=[packed_shape(query) for query in queries],
        in_specs=any_specs(after) + [vmem_spec()] * (2 + len(queries)),
        out_specs=[vmem_spec()] * len(queries),
        compiler_params=kernel_params(),
        cost_estimate=light_cost(),
        name="root_blocks",
    )(*after, keys, values, *queries)


def branch_kernel(
    scale, shared, pair_ref, branch_ref, seen_ref, query_ref, ko_ref, vo_ref, kp_ref, vp_ref,
    out_ref, k_ref, v_ref, limit_ref, wide_ref,
):
    requests, local_heads, _ = query_ref.shape
    branches, heads, both, _ = k_ref.shape
    group_size = local_heads // heads
    pair = pair_ref[0]
    first = pair * heads
    half = both // 2
    for b in range(branches):
        for owner, keys, values in ((pair, ko_ref, vo_ref), (1 - pair, kp_ref, vp_ref)):
            base = pl.multiple_of(owner * half, half)
            split_heads(keys.at[b], k_ref.at[b], wide_ref, shared, first, heads, base)
            split_heads(values.at[b], v_ref.at[b], wide_ref, shared, first, heads, base)
        for r in range(requests):
            limit = jnp.where(branch_ref[r] % branches == b, seen_ref[r], 0)
            limit_ref[b, pl.ds(r * group_size, group_size), :] = jnp.full(
                (group_size, lane_count), limit, jnp.int32
            )

    def pieces(h):
        query = head_queries(query_ref, h, group_size)
        return [
            (query, k_ref[b, h], v_ref[b, h], limit_ref[b][:, :1]) for b in range(branches)
        ]

    write_partials([(out_ref, pieces)], scale, heads, requests, group_size)


def branch_block(pair_index, branch, seen, query, caches, scale, heads, after):
    branches, tokens, shared, width = caches[0].shape
    requests, local_heads, _ = query.shape
    rows = requests * local_heads // heads
    held = pltpu.VMEM((branches, heads, 2 * tokens, width), caches[0].dtype)
    return pl.pallas_call(
        ordered(functools.partial(branch_kernel, scale, shared), after),
        out_shape=packed_shape(query),
        in_specs=any_specs(after) + [smem_spec()] * 3 + [vmem_spec()] * 5,
        out_specs=vmem_spec(),
        scratch_shapes=[
            held,
            held,
            pltpu.VMEM((branches, rows, lane_count), jnp.int32),
            pltpu.VMEM((chunk_tokens * shared, width), jnp.float32),
        ],
        compiler_params=kernel_params(),
        cost_estimate=light_cost(),
        name="branch_block",
    )(*after, pair_index, branch, seen, query, *map(flat, caches))


def merge_kernel(last, heads, requests, group_size, *refs):
    ins, out_ref = refs[:-1], refs[-1]
    same = identity_mask()
    loaded = [load_packed(ref, heads, requests, group_size, same) for ref in ins]
    outs, levels = [], []
    for h in range(heads):
        top = loaded[0][1][h]
        for _, level in loaded[1:]:
            top = jnp.maximum(top, level[h])
        sums = totals = 0.0
        for out, level in loaded:
            weight = jnp.exp2(level[h] - top)
            sums = sums + out[h] * weight
            totals = totals + weight
        outs.append(sums * (1.0 / totals))
        levels.append(top + jnp.log2(totals))
    if last:
        for h in range(heads):
            block = outs[h].astype(out_ref.dtype).reshape(requests, group_size, lane_count)
            out_ref[:, h * group_size : (h + 1) * group_size, :] = block
    else:
        store_packed(out_ref, heads, requests, group_size, outs, levels, same)


def merge(parts, last, heads, requests, group_size, after=()):
    if last:
        shape = (requests, heads * group_size, lane_count)
    else:
        shape = parts[0].shape
    return pl.pallas_call(
        ordered(functools.partial(merge_kernel, last, heads, requests, group_size), after),
        out_shape=jax.ShapeDtypeStruct(shape, parts[0].dtype),
        in_specs=any_specs(after) + [vmem_spec()] * len(parts),
        out_specs=vmem_spec(),
        compiler_params=kernel_params(),
        cost_estimate=light_cost(),
        name="merge_last" if last else "merge_some",
    )(*after, *parts)


def local(queries, root_keys, root_values, branch_keys, branch_values, request_branch, seen_tokens):
    requests, local_heads, width = queries.shape
    shared = root_keys.shape[1]
    blocks = lax.axis_size("blk")
    heads = shared // lax.axis_size("pair")
    group_size = local_heads // heads
    scale = math.log2(math.e) / math.sqrt(width)
    pair_index = place(lax.axis_index("pair").astype(jnp.int32).reshape(1))

    other_keys = exchange(root_keys, "pair", 1)
    other_values = exchange(root_values, "pair", 1)
    direct = range(blocks - 1, 0, -2)
    arrived = [exchange(queries, "blk", apart) for apart in direct]

    keys, values, own = first_block(
        pair_index, queries, root_keys, root_values, other_keys, other_values, scale, heads
    )
    *arrived, own, far_keys, far_values = lax.optimization_barrier(
        (*arrived, own, branch_keys, branch_values)
    )
    other_branch_keys = exchange(far_keys, "pair", 1)
    other_branch_values = exchange(far_values, "pair", 1)
    arrived = dict(zip(direct, arrived))
    for apart in range(blocks - 1, 2, -2):
        arrived[apart ^ 1] = exchange(arrived[apart], "blk", 1)

    groups = [(apart,) for apart in arrived if apart > 2] + [
        tuple(apart for apart in (2, 1) if apart in arrived)
    ]
    returned, previous = {}, ()
    for group in groups:
        partials = root_blocks([arrived[apart] for apart in group], keys, values, scale, previous)
        previous = (partials[0],)
        for apart, partial in zip(group, partials):
            returned[apart] = exchange(partial, "blk", apart)
    branch = branch_block(
        pair_index, request_branch, seen_tokens, queries,
        (branch_keys, branch_values, other_branch_keys, other_branch_values),
        scale, heads, previous,
    )
    last = returned.pop(max(groups[-1]))
    most = merge([own, branch, *returned.values()], False, heads, requests, group_size)
    return merge([most, last], True, heads, requests, group_size)


def solution(mesh):
    in_specs = (
        P(("groups", "blk"), ("kv", "pair"), None),
        P(("groups", "blk", "pair"), "kv", None),
        P(("groups", "blk", "pair"), "kv", None),
        P(("groups", "blk"), "pair", "kv", None),
        P(("groups", "blk"), "pair", "kv", None),
        P(("groups", "blk")),
        P(("groups", "blk")),
    )
    out_specs = P(("groups", "blk"), ("kv", "pair"), None)
    return jax.shard_map(local, mesh=mesh, in_specs=in_specs, out_specs=out_specs, check_vma=False)
```

time: 38.8 us -> 41.3 us (1.064)
  Pallas kernels: 20.3 us -> 27.4 us
  waiting for transfers between devices: 4.43 us -> 0.31 us
  local copies, waits for them, and re-layouts: 1.57 us -> 1.01 us
    pallas_call x6 -> x5, Pallas kernels: 17.7 us -> 25.4 us  [the longest x1 10.7 us: branch_block(): pl.pallas_call(ordered(functools.partial(branch_kernel, scale, shared), a...]
    ppermute x10, waiting for transfers between devices: 4.43 us -> 0.31 us  [exchange(): lax.ppermute(value, axis, [(i, i ^ apart) for i in range(lax.axis_size(ax...]
    unnamed x10 -> x14, local copies, waits for them, and re-layouts: 1.57 us -> 1.01 us
    pallas_call x3 -> x2, Pallas kernels: 2.55 us -> 2 us  [merge(): pl.pallas_call(ordered(functools.partial(merge_kernel, last, heads, reque...]
  transfers between devices with their start and end apart: 10 -> 10, of which waited for: 1 -> 1; matrix products, arithmetic and copies ran while one was open for 0% -> 0% of each run, Pallas kernels for 50% -> 64%
where the time goes in v3:
time: 41.3 us; the launch traced here: 41.2 us
  Pallas kernels  27.4 us (66%)
  starting transfers between devices  12.4 us (30%)
  local copies, waits for them, and re-layouts  1.01 us (2%)
    ppermute x10, starting transfers between devices, exchange(): lax.ppermute(value, axis, [(i, i ^ apart) for i in range(lax.axis_size(ax...  12.4 us
    pallas_call x1, Pallas kernels, branch_block(): pl.pallas_call(ordered(functools.partial(branch_kernel, scale, shared), a...  10.7 us
    pallas_call x2, Pallas kernels, root_blocks(): pl.pallas_call(ordered(functools.partial(root_kernel, scale, len(queries)...  9.2 us
    pallas_call x1, Pallas kernels, first_block(): pl.pallas_call(functools.partial(first_kernel, scale, shared), out_shape=...  4.93 us
    pallas_call x2, Pallas kernels, merge(): pl.pallas_call(ordered(functools.partial(merge_kernel, last, heads, reque...  2 us
    unnamed x14, local copies, waits for them, and re-layouts  1.01 us
  transfers between devices with their start and end apart: 10, of which 1 were waited for; matrix products, arithmetic and copies ran while one was open for 0% of the time, Pallas kernels for 64%

profile of v3, /device:TPU:0, one launch (start us, length us, event | category | flops | bytes accessed | tf_op | source)
XLA Modules:
  0.0 41.2 jit_solution(17978991360290989846)
XLA Ops:
  0.0 0.5 %collective-permute-start.2 = (bf16[1024,4,128]{2,1,0:T(4,128)(2,1)}, bf16[1024,4,128]{2,1,0:T(4,128)(2,1)S(1)}, u32[]{:S(2)}, u32[]{:S(2)}) collective-permute-start(bf16[1024,4,128]{2,1,0:T(4,128)(2,1)} %param.8), channel_id=1, source_target_pairs={{0,1},{1,0},{2,3},{3,2},{4,5},{5,4},{6,7},{7,6},{8,9},{9,8},{10,11... | collective-permute-start | bytes 3145736 | tf_op jit(solution)/shard_map/ppermute | solution.py:46
  0.5 0.1 collective-permute-start.3
  0.5 5.0 %collective-permute-start = (bf16[16,32,128]{2,1,0:T(8,128)(2,1)}, bf16[16,32,128]{2,1,0:T(8,128)(2,1)S(1)}, u32[]{:S(2)}, u32[]{:S(2)}) collective-permute-start(bf16[16,32,128]{2,1,0:T(8,128)(2,1)} %refs_4_.1), channel_id=1, source_target_pairs={{0,12},{4,8},{8,4},{12,0},{1,13},{5,9},{9,5},{13,1},{2,14},{6,10},... | collective-permute-start | bytes 393224 | tf_op jit(solution)/shard_map/ppermute | solution.py:46
  5.6 0.0 collective-permute-start.1
  5.6 0.5 %place.1.pair_ref.refs_1_ = s32[1]{0:T(128)} custom-call(s32[1]{0:T(128)} %bitcast.in_ref), custom_call_target="tpu_custom_call" | custom-call | flops 10000000000 | bytes 1 | tf_op jit(solution)/shard_map/place/pallas_call | solution.py:257
  6.1 0.0 collective-permute-done.2
  6.1 0.7 %copy-done.2 = bf16[1024,4,128]{2,1,0:T(4,128)(2,1)S(1)} copy-done((bf16[1024,4,128]{2,1,0:T(4,128)(2,1)S(1)}, bf16[1024,4,128]{2,1,0:T(4,128)(2,1)}, u32[]{:S(2)}) %copy-start.2) | copy-done | bytes 1048600
  6.8 0.3 copy-done.3
  7.1 4.9 %first_block.1 = (bf16[2,2048,128]{2,1,0:T(8,128)(2,1)S(1)}, bf16[2,2048,128]{2,1,0:T(8,128)(2,1)S(1)}, bf16[528,128]{1,0:T(8,128)(2,1)S(1)}) custom-call(s32[1]{0:T(128)} %place.1.pair_ref.refs_1_, bf16[16,32,128]{2,1,0:T(8,128)(2,1)S(1)} %copy-done.4, bf16[4096,128]{1,0:T(8,128)(2,1)S(1)} %bitcast.13, bf16[4096,128]{1,0:T(8,128)(2,1)S(1)} %bitcast.14, ...), custom_call_target="tpu_custom_call" | custom-call | flops 1 | bytes 1 | tf_op jit(solution)/shard_map/first_block/pallas_call | solution.py:240
  12.0 0.0 collective-permute-done.refs_2_
  12.1 0.3 collective-permute-done.1.refs_4_
  12.3 0.0 collective-permute-start.5
  12.4 0.5 %collective-permute-start.6 = (bf16[2,1024,4,128]{3,2,1,0:T(4,128)(2,1)S(1)}, bf16[2,1024,4,128]{3,2,1,0:T(4,128)(2,1)S(1)}, u32[]{:S(2)}, u32[]{:S(2)}) collective-permute-start(bf16[2,1024,4,128]{3,2,1,0:T(4,128)(2,1)S(1)} %copy-done.1), channel_id=1, source_target_pairs={{0,1},{1,0},{2,3},{3,2},{4,5},{5,4},{6,7},{7,6},{8,9},{9,8},{10,11... | collective-permute-start | bytes 6291464 | tf_op jit(solution)/shard_map/ppermute | solution.py:46
  12.9 1.8 %collective-permute-start.4 = (bf16[16,32,128]{2,1,0:T(8,128)(2,1)S(1)}, bf16[16,32,128]{2,1,0:T(8,128)(2,1)S(1)}, u32[]{:S(2)}, u32[]{:S(2)}) collective-permute-start(bf16[16,32,128]{2,1,0:T(8,128)(2,1)S(1)} %collective-permute-done.refs_2_), channel_id=1, source_target_pairs={{0,4},{4,0},{8,12},{12,8},{1,5},{5,1},{9,13},{13,9},{2,6},{6,2},{1... | collective-permute-start | bytes 393224 | tf_op jit(solution)/shard_map/ppermute | solution.py:46
  14.7 3.2 %root_blocks.2.refs_0_ = bf16[528,128]{1,0:T(8,128)(2,1)S(1)} custom-call(bf16[2,2048,128]{2,1,0:T(8,128)(2,1)S(1)} %get-tuple-element.17.refs_0_.refs_1_, bf16[2,2048,128]{2,1,0:T(8,128)(2,1)S(1)} %get-tuple-element.18.refs_1_.refs_2_, bf16[16,32,128]{2,1,0:T(8,128)(2,1)S(1)} %collective-permute-done.refs_2_), custom_call_target="tpu_custom_call" | custom-call | flops 1 | bytes 1 | tf_op jit(solution)/shard_map/root_blocks/pallas_call | solution.py:280
  17.9 0.8 %collective-permute-start.7 = (bf16[528,128]{1,0:T(8,128)(2,1)S(1)}, bf16[528,128]{1,0:T(8,128)(2,1)S(1)}, u32[]{:S(2)}, u32[]{:S(2)}) collective-permute-start(bf16[528,128]{1,0:T(8,128)(2,1)S(1)} %root_blocks.2.refs_0_), channel_id=1, source_target_pairs={{0,12},{4,8},{8,4},{12,0},{1,13},{5,9},{9,5},{13,1},{2,14},{6,10},... | collective-permute-start | bytes 405512 | tf_op jit(solution)/shard_map/ppermute | solution.py:46
  18.7 6.0 %root_blocks.3 = (bf16[528,128]{1,0:T(8,128)(2,1)S(1)}, bf16[528,128]{1,0:T(8,128)(2,1)S(1)}) custom-call(bf16[528,128]{1,0:T(8,128)(2,1)S(1)} %root_blocks.2.refs_0_, bf16[2,2048,128]{2,1,0:T(8,128)(2,1)S(1)} %get-tuple-element.17.refs_0_.refs_1_, bf16[2,2048,128]{2,1,0:T(8,128)(2,1)S(1)} %get-tuple-element.18.refs_1_.refs_2_, ...), custom_call_target="tpu_custom_call" | custom-call | flops 1 | bytes 1 | tf_op jit(solution)/shard_map/root_blocks/pallas_call | solution.py:280
  24.7 1.5 %collective-permute-start.8 = (bf16[528,128]{1,0:T(8,128)(2,1)S(1)}, bf16[528,128]{1,0:T(8,128)(2,1)S(1)}, u32[]{:S(2)}, u32[]{:S(2)}) collective-permute-start(bf16[528,128]{1,0:T(8,128)(2,1)S(1)} %get-tuple-element.24), channel_id=1, source_target_pairs={{0,4},{4,0},{8,12},{12,8},{1,5},{5,1},{9,13},{13,9},{2,6},{6,2},{1... | collective-permute-start | bytes 405512 | tf_op jit(solution)/shard_map/ppermute | solution.py:46
  26.3 2.1 %collective-permute-start.9 = (bf16[528,128]{1,0:T(8,128)(2,1)S(1)}, bf16[528,128]{1,0:T(8,128)(2,1)S(1)}, u32[]{:S(2)}, u32[]{:S(2)}) collective-permute-start(bf16[528,128]{1,0:T(8,128)(2,1)S(1)} %get-tuple-element.21.refs_0_), channel_id=1, source_target_pairs={{0,8},{4,12},{8,0},{12,4},{1,9},{5,13},{9,1},{13,5},{2,10},{6,14},... | collective-permute-start | bytes 405512 | tf_op jit(solution)/shard_map/ppermute | solution.py:46
  28.4 0.0 collective-permute-done.5
  28.4 0.0 collective-permute-done.6
  28.4 10.7 %branch_block.1.refs_1_ = bf16[528,128]{1,0:T(8,128)(2,1)S(1)} custom-call(bf16[528,128]{1,0:T(8,128)(2,1)S(1)} %get-tuple-element.21.refs_0_, s32[1]{0:T(128)} %place.1.pair_ref.refs_1_, s32[16]{0:T(128)S(1)} %copy-done.5, s32[16]{0:T(128)S(1)} %copy-done.6, bf16[16,32,128]{2,1,0:T(8,128)(2,1)S(1)} %copy-done.4, bf16[2,4096,128]{2,1,0:T(8,128)(2,1)S(1)} %bitcast.9, ...), custom_call_target="tpu_custom_call" | custom-call | flops 1 | bytes 1 | tf_op jit(solution)/shard_map/branch_block/pallas_call | solution.py:326
  39.2 0.9 %merge_some.1.refs_0_ = bf16[528,128]{1,0:T(8,128)(2,1)S(1)} custom-call(bf16[528,128]{1,0:T(8,128)(2,1)S(1)} %get-tuple-element.16.refs_0_, bf16[528,128]{1,0:T(8,128)(2,1)S(1)} %branch_block.1.refs_1_, bf16[528,128]{1,0:T(8,128)(2,1)S(1)} %collective-permute-done.7.refs_2_, bf16[528,128]{1,0:T(8,128)(2,1)S(1)} %collective-permute-done.8.refs_3_), custom_call_target="tpu_custom_call" | custom-call | flops 1 | bytes 1 | tf_op jit(solution)/shard_map/merge_some/pallas_call | solution.py:372
  40.1 1.1 %merge_last.1 = bf16[16,32,128]{2,1,0:T(8,128)(2,1)} custom-call(bf16[528,128]{1,0:T(8,128)(2,1)S(1)} %merge_some.1.refs_0_, bf16[528,128]{1,0:T(8,128)(2,1)S(1)} %collective-permute-done.9.refs_1_), custom_call_target="tpu_custom_call" | custom-call | flops 1 | bytes 1 | tf_op jit(solution)/shard_map/merge_last/pallas_call | solution.py:372
  (17 shorter events, 0.0 us)
Async XLA Ops:
  0.0 6.1 %collective-permute-start.2 = (bf16[1024,4,128]{2,1,0:T(4,128)(2,1)}, bf16[1024,4,128]{2,1,0:T(4,128)(2,1)S(1)}, u32[]{:S(2)}, u32[]{:S(2)}) collective-permute-start(bf16[1024,4,128]{2,1,0:T(4,128)(2,1)} %param.8), channel_id=1, source_target_pairs={{0,1},{1,0},{2,3},{3,2},{4,5},{5,4},{6,7},{7,6},{8,9},{9,8},{10,11... | collective-permute-start | bytes 3145736 | tf_op jit(solution)/shard_map/ppermute | solution.py:46
  0.5 5.7 %collective-permute-start.3 = (bf16[1024,4,128]{2,1,0:T(4,128)(2,1)}, bf16[1024,4,128]{2,1,0:T(4,128)(2,1)S(1)}, u32[]{:S(2)}, u32[]{:S(2)}) collective-permute-start(bf16[1024,4,128]{2,1,0:T(4,128)(2,1)} %param.9), channel_id=1, source_target_pairs={{0,1},{1,0},{2,3},{3,2},{4,5},{5,4},{6,7},{7,6},{8,9},{9,8},{10,11... | collective-permute-start | bytes 3145736 | tf_op jit(solution)/shard_map/ppermute | solution.py:46
  0.5 11.5 %collective-permute-start = (bf16[16,32,128]{2,1,0:T(8,128)(2,1)}, bf16[16,32,128]{2,1,0:T(8,128)(2,1)S(1)}, u32[]{:S(2)}, u32[]{:S(2)}) collective-permute-start(bf16[16,32,128]{2,1,0:T(8,128)(2,1)} %refs_4_.1), channel_id=1, source_target_pairs={{0,12},{4,8},{8,4},{12,0},{1,13},{5,9},{9,5},{13,1},{2,14},{6,10},... | collective-permute-start | bytes 393224 | tf_op jit(solution)/shard_map/ppermute | solution.py:46
  5.6 6.8 %collective-permute-start.1 = (bf16[16,32,128]{2,1,0:T(8,128)(2,1)}, bf16[16,32,128]{2,1,0:T(8,128)(2,1)S(1)}, u32[]{:S(2)}, u32[]{:S(2)}) collective-permute-start(bf16[16,32,128]{2,1,0:T(8,128)(2,1)} %refs_4_.1), channel_id=1, source_target_pairs={{0,4},{4,0},{8,12},{12,8},{1,5},{5,1},{9,13},{13,9},{2,6},{6,2},{1... | collective-permute-start | bytes 393224 | tf_op jit(solution)/shard_map/ppermute | solution.py:46
  5.6 1.2 %copy-start.2 = (bf16[1024,4,128]{2,1,0:T(4,128)(2,1)S(1)}, bf16[1024,4,128]{2,1,0:T(4,128)(2,1)}, u32[]{:S(2)}) copy-start(bf16[1024,4,128]{2,1,0:T(4,128)(2,1)} %param.8) | copy-start | bytes 3145732
  5.6 1.5 %copy-start.3 = (bf16[1024,4,128]{2,1,0:T(4,128)(2,1)S(1)}, bf16[1024,4,128]{2,1,0:T(4,128)(2,1)}, u32[]{:S(2)}) copy-start(bf16[1024,4,128]{2,1,0:T(4,128)(2,1)} %param.9) | copy-start | bytes 3145732
  5.6 1.5 %copy-start.4 = (bf16[16,32,128]{2,1,0:T(8,128)(2,1)S(1)}, bf16[16,32,128]{2,1,0:T(8,128)(2,1)}, u32[]{:S(2)}) copy-start(bf16[16,32,128]{2,1,0:T(8,128)(2,1)} %refs_4_.1) | copy-start | bytes 393220
  7.1 5.2 %copy-start = (bf16[2,1024,4,128]{3,2,1,0:T(4,128)(2,1)S(1)}, bf16[2,1024,4,128]{3,2,1,0:T(4,128)(2,1)}, u32[]{:S(2)}) copy-start(bf16[2,1024,4,128]{3,2,1,0:T(4,128)(2,1)} %param.10) | copy-start | bytes 6291460
  7.1 5.2 %copy-start.1 = (bf16[2,1024,4,128]{3,2,1,0:T(4,128)(2,1)S(1)}, bf16[2,1024,4,128]{3,2,1,0:T(4,128)(2,1)}, u32[]{:S(2)}) copy-start(bf16[2,1024,4,128]{3,2,1,0:T(4,128)(2,1)} %param.11) | copy-start | bytes 6291460
  12.3 16.1 %collective-permute-start.5 = (bf16[2,1024,4,128]{3,2,1,0:T(4,128)(2,1)S(1)}, bf16[2,1024,4,128]{3,2,1,0:T(4,128)(2,1)S(1)}, u32[]{:S(2)}, u32[]{:S(2)}) collective-permute-start(bf16[2,1024,4,128]{3,2,1,0:T(4,128)(2,1)S(1)} %copy-done), channel_id=1, source_target_pairs={{0,1},{1,0},{2,3},{3,2},{4,5},{5,4},{6,7},{7,6},{8,9},{9,8},{10,11... | collective-permute-start | bytes 6291464 | tf_op jit(solution)/shard_map/ppermute | solution.py:46
  12.4 16.1 %collective-permute-start.6 = (bf16[2,1024,4,128]{3,2,1,0:T(4,128)(2,1)S(1)}, bf16[2,1024,4,128]{3,2,1,0:T(4,128)(2,1)S(1)}, u32[]{:S(2)}, u32[]{:S(2)}) collective-permute-start(bf16[2,1024,4,128]{3,2,1,0:T(4,128)(2,1)S(1)} %copy-done.1), channel_id=1, source_target_pairs={{0,1},{1,0},{2,3},{3,2},{4,5},{5,4},{6,7},{7,6},{8,9},{9,8},{10,11... | collective-permute-start | bytes 6291464 | tf_op jit(solution)/shard_map/ppermute | solution.py:46
  12.9 5.8 %collective-permute-start.4 = (bf16[16,32,128]{2,1,0:T(8,128)(2,1)S(1)}, bf16[16,32,128]{2,1,0:T(8,128)(2,1)S(1)}, u32[]{:S(2)}, u32[]{:S(2)}) collective-permute-start(bf16[16,32,128]{2,1,0:T(8,128)(2,1)S(1)} %collective-permute-done.refs_2_), channel_id=1, source_target_pairs={{0,4},{4,0},{8,12},{12,8},{1,5},{5,1},{9,13},{13,9},{2,6},{6,2},{1... | collective-permute-start | bytes 393224 | tf_op jit(solution)/shard_map/ppermute | solution.py:46
  14.7 13.7 %copy-start.5 = (s32[16]{0:T(128)S(1)}, s32[16]{0:T(128)}, u32[]{:S(2)}) copy-start(s32[16]{0:T(128)} %refs_2_.1) | copy-start | bytes 196
  14.7 13.7 %copy-start.6 = (s32[16]{0:T(128)S(1)}, s32[16]{0:T(128)}, u32[]{:S(2)}) copy-start(s32[16]{0:T(128)} %refs_3_.1) | copy-start | bytes 196
  17.9 21.3 %collective-permute-start.7 = (bf16[528,128]{1,0:T(8,128)(2,1)S(1)}, bf16[528,128]{1,0:T(8,128)(2,1)S(1)}, u32[]{:S(2)}, u32[]{:S(2)}) collective-permute-start(bf16[528,128]{1,0:T(8,128)(2,1)S(1)} %root_blocks.2.refs_0_), channel_id=1, source_target_pairs={{0,12},{4,8},{8,4},{12,0},{1,13},{5,9},{9,5},{13,1},{2,14},{6,10},... | collective-permute-start | bytes 405512 | tf_op jit(solution)/shard_map/ppermute | solution.py:46
  24.7 14.4 %collective-permute-start.8 = (bf16[528,128]{1,0:T(8,128)(2,1)S(1)}, bf16[528,128]{1,0:T(8,128)(2,1)S(1)}, u32[]{:S(2)}, u32[]{:S(2)}) collective-permute-start(bf16[528,128]{1,0:T(8,128)(2,1)S(1)} %get-tuple-element.24), channel_id=1, source_target_pairs={{0,4},{4,0},{8,12},{12,8},{1,5},{5,1},{9,13},{13,9},{2,6},{6,2},{1... | collective-permute-start | bytes 405512 | tf_op jit(solution)/shard_map/ppermute | solution.py:46
  26.3 13.8 %collective-permute-start.9 = (bf16[528,128]{1,0:T(8,128)(2,1)S(1)}, bf16[528,128]{1,0:T(8,128)(2,1)S(1)}, u32[]{:S(2)}, u32[]{:S(2)}) collective-permute-start(bf16[528,128]{1,0:T(8,128)(2,1)S(1)} %get-tuple-element.21.refs_0_), channel_id=1, source_target_pairs={{0,8},{4,12},{8,0},{12,4},{1,9},{5,13},{9,1},{13,5},{2,10},{6,14},... | collective-permute-start | bytes 405512 | tf_op jit(solution)/shard_map/ppermute | solution.py:46

commit v4 on v3

--- a/solution.py
+++ b/solution.py
@@ -128,8 +128,22 @@
     return sums * (1.0 / safe), level, sound
 
 
-def write_partials(jobs, scale, heads, requests, group_size):
+def combine(parts):
+    top = parts[0][1]
+    for _, level in parts[1:]:
+        top = jnp.maximum(top, level)
+    sums = totals = 0.0
+    for out, level in parts:
+        weight = jnp.exp2(level - top)
+        sums = sums + out * weight
+        totals = totals + weight
+    return sums * (1.0 / totals), top + jnp.log2(totals)
+
+
+def write_partials(jobs, scale, heads, requests, group_size, others=()):
     same = identity_mask()
+
+    loaded = [load_packed(ref, heads, requests, group_size, same) for ref in others]
 
     def run(exact):
         least = 1.0
@@ -137,6 +151,9 @@
             outs, levels = [], []
             for h in range(heads):
                 out, level, sound = evaluate(pieces_of(h), scale, exact)
+                if others:
+                    added = [(o[h], l[h]) for o, l in loaded]
+                    out, level = combine([(out, level), *added])
                 outs.append(out)
                 levels.append(level)
                 least = jnp.minimum(least, jnp.where(sound, 1.0, 0.0))
@@ -288,56 +305,74 @@
     )(*after, keys, values, *queries)
 
 
-def branch_kernel(
-    scale, shared, pair_ref, branch_ref, seen_ref, query_ref, ko_ref, vo_ref, kp_ref, vp_ref,
+def branch_pieces(query_ref, k_ref, v_ref, limit_ref, owner, heads, group_size):
+    def pieces(h):
+        query = head_queries(query_ref, h, group_size)
+        at = owner * heads + h
+        return [
+            (query, k_ref[b, at], v_ref[b, at], limit_ref[b][:, :1]) for b in range(k_ref.shape[0])
+        ]
+
+    return pieces
+
+
+def theirs_kernel(
+    scale, heads, pair_ref, branch_ref, seen_ref, query_ref, bk_ref, bv_ref,
     out_ref, k_ref, v_ref, limit_ref, wide_ref,
 ):
     requests, local_heads, _ = query_ref.shape
-    branches, heads, both, _ = k_ref.shape
+    branches, shared, tokens, _ = k_ref.shape
     group_size = local_heads // heads
-    pair = pair_ref[0]
-    first = pair * heads
-    half = both // 2
     for b in range(branches):
-        for owner, keys, values in ((pair, ko_ref, vo_ref), (1 - pair, kp_ref, vp_ref)):
-            base = pl.multiple_of(owner * half, half)
-            split_heads(keys.at[b], k_ref.at[b], wide_ref, shared, first, heads, base)
-            split_heads(values.at[b], v_ref.at[b], wide_ref, shared, first, heads, base)
+        split_heads(bk_ref.at[b], k_ref.at[b], wide_ref, shared, 0, shared, 0)
+        split_heads(bv_ref.at[b], v_ref.at[b], wide_ref, shared, 0, shared, 0)
         for r in range(requests):
-            limit = jnp.where(branch_ref[r] % branches == b, seen_ref[r], 0)
+            here = branch_ref[r] % branches == b
+            limit = jnp.where(here, seen_ref[r] - pair_ref[0] * tokens, 0)
             limit_ref[b, pl.ds(r * group_size, group_size), :] = jnp.full(
                 (group_size, lane_count), limit, jnp.int32
             )
-
-    def pieces(h):
-        query = head_queries(query_ref, h, group_size)
-        return [
-            (query, k_ref[b, h], v_ref[b, h], limit_ref[b][:, :1]) for b in range(branches)
-        ]
-
+    owner = 1 - pair_ref[0]
+    pieces = branch_pieces(query_ref, k_ref, v_ref, limit_ref, owner, heads, group_size)
     write_partials([(out_ref, pieces)], scale, heads, requests, group_size)
 
 
-def branch_block(pair_index, branch, seen, query, caches, scale, heads, after):
-    branches, tokens, shared, width = caches[0].shape
+def mine_kernel(scale, heads, pair_ref, query_ref, k_ref, v_ref, limit_ref, *refs):
+    *others, out_ref = refs
+    requests, local_heads, _ = query_ref.shape
+    group_size = local_heads // heads
+    pieces = branch_pieces(query_ref, k_ref, v_ref, limit_ref, pair_ref[0], heads, group_size)
+    write_partials([(out_ref, pieces)], scale, heads, requests, group_size, others)
+
+
+def theirs_block(pair_index, branch, seen, query, keys, values, scale, heads, after):
+    branches, tokens, shared, width = keys.shape
     requests, local_heads, _ = query.shape
     rows = requests * local_heads // heads
-    held = pltpu.VMEM((branches, heads, 2 * tokens, width), caches[0].dtype)
-    return pl.pallas_call(
-        ordered(functools.partial(branch_kernel, scale, shared), after),
-        out_shape=packed_shape(query),
-        in_specs=any_specs(after) + [smem_spec()] * 3 + [vmem_spec()] * 5,
-        out_specs=vmem_spec(),
-        scratch_shapes=[
-            held,
-            held,
-            pltpu.VMEM((branches, rows, lane_count), jnp.int32),
-            pltpu.VMEM((chunk_tokens * shared, width), jnp.float32),
-        ],
+    held = jax.ShapeDtypeStruct((branches, shared, tokens, width), keys.dtype)
+    limits = jax.ShapeDtypeStruct((branches, rows, lane_count), jnp.int32)
+    return pl.pallas_call(
+        ordered(functools.partial(theirs_kernel, scale, heads), after),
+        out_shape=(packed_shape(query), held, held, limits),
+        in_specs=any_specs(after) + [smem_spec()] * 3 + [vmem_spec()] * 3,
+        out_specs=(vmem_spec(),) * 4,
+        scratch_shapes=[pltpu.VMEM((chunk_tokens * shared, width), jnp.float32)],
         compiler_params=kernel_params(),
         cost_estimate=light_cost(),
-        name="branch_block",
-    )(*after, pair_index, branch, seen, query, *map(flat, caches))
+        name="theirs_block",
+    )(*after, pair_index, branch, seen, query, flat(keys), flat(values))
+
+
+def mine_block(pair_index, query, keys, values, limits, others, scale, heads):
+    return pl.pallas_call(
+        functools.partial(mine_kernel, scale, heads),
+        out_shape=packed_shape(query),
+        in_specs=[smem_spec()] + [vmem_spec()] * (4 + len(others)),
+        out_specs=vmem_spec(),
+        compiler_params=kernel_params(),
+        cost_estimate=light_cost(),
+        name="mine_block",
+    )(pair_index, query, keys, values, limits, *others)
 
 
 def merge_kernel(last, heads, requests, group_size, *refs):
@@ -346,16 +381,9 @@
     loaded = [load_packed(ref, heads, requests, group_size, same) for ref in ins]
     outs, levels = [], []
     for h in range(heads):
-        top = loaded[0][1][h]
-        for _, level in loaded[1:]:
-            top = jnp.maximum(top, level[h])
-        sums = totals = 0.0
-        for out, level in loaded:
-            weight = jnp.exp2(level[h] - top)
-            sums = sums + out[h] * weight
-            totals = totals + weight
-        outs.append(sums * (1.0 / totals))
-        levels.append(top + jnp.log2(totals))
+        out, level = combine([(o[h], l[h]) for o, l in loaded])
+        outs.append(out)
+        levels.append(level)
     if last:
         for h in range(heads):
             block = outs[h].astype(out_ref.dtype).reshape(requests, group_size, lane_count)
@@ -391,38 +419,31 @@
 
     other_keys = exchange(root_keys, "pair", 1)
     other_values = exchange(root_values, "pair", 1)
+    other_queries = exchange(queries, "pair", 1)
     direct = range(blocks - 1, 0, -2)
-    arrived = [exchange(queries, "blk", apart) for apart in direct]
+    arrived = {apart: exchange(queries, "blk", apart) for apart in direct}
 
     keys, values, own = first_block(
         pair_index, queries, root_keys, root_values, other_keys, other_values, scale, heads
     )
-    *arrived, own, far_keys, far_values = lax.optimization_barrier(
-        (*arrived, own, branch_keys, branch_values)
-    )
-    other_branch_keys = exchange(far_keys, "pair", 1)
-    other_branch_values = exchange(far_values, "pair", 1)
-    arrived = dict(zip(direct, arrived))
-    for apart in range(blocks - 1, 2, -2):
-        arrived[apart ^ 1] = exchange(arrived[apart], "blk", 1)
-
-    groups = [(apart,) for apart in arrived if apart > 2] + [
-        tuple(apart for apart in (2, 1) if apart in arrived)
-    ]
+    groups = [(apart, apart ^ 1) for apart in direct if apart > 1]
+    for far, near in groups:
+        arrived[far], own = lax.optimization_barrier((arrived[far], own))
+        arrived[near] = exchange(arrived[far], "blk", 1)
+    order = sorted(arrived, key=lambda apart: (apart % 2 == 0, -apart))
     returned, previous = {}, ()
-    for group in groups:
-        partials = root_blocks([arrived[apart] for apart in group], keys, values, scale, previous)
-        previous = (partials[0],)
-        for apart, partial in zip(group, partials):
-            returned[apart] = exchange(partial, "blk", apart)
-    branch = branch_block(
-        pair_index, request_branch, seen_tokens, queries,
-        (branch_keys, branch_values, other_branch_keys, other_branch_values),
+    for apart in order:
+        previous = root_blocks([arrived[apart]], keys, values, scale, previous)
+        returned[apart] = exchange(previous[0], "blk", apart)
+    theirs, held_keys, held_values, limits = theirs_block(
+        pair_index, request_branch, seen_tokens, other_queries, branch_keys, branch_values,
         scale, heads, previous,
     )
-    last = returned.pop(max(groups[-1]))
-    most = merge([own, branch, *returned.values()], False, heads, requests, group_size)
-    return merge([most, last], True, heads, requests, group_size)
+    from_partner = exchange(theirs, "pair", 1)
+    early = [own] + [returned.pop(apart) for apart in order if apart > 2 and apart % 2]
+    most = mine_block(pair_index, queries, held_keys, held_values, limits, early, scale, heads)
+    most = merge([most, *returned.values()], False, heads, requests, group_size)
+    return merge([most, from_partner], True, heads, requests, group_size)
 
 
 def solution(mesh):

time: 41.3 us -> 42.6 us (1.031)
  Pallas kernels: 27.4 us -> 28.8 us
    pallas_call x1 -> x2, Pallas kernels: 10.7 us -> 12 us  [the longest x1 6.61 us: theirs_block(): pl.pallas_call(ordered(functools.partial(theirs_kernel, scale, heads), af...]
    pallas_call x2 -> x3, Pallas kernels: 9.2 us -> 9.68 us  [root_blocks(): pl.pallas_call(ordered(functools.partial(root_kernel, scale, len(queries)...]
  transfers between devices with their start and end apart: 10 -> 10, of which waited for: 1 -> 0; matrix products, arithmetic and copies ran while one was open for 0% -> 0% of each run, Pallas kernels for 64% -> 65%
where the time goes in v4:
time: 42.6 us; the launch traced here: 42.4 us
  Pallas kernels  28.8 us (68%)
  starting transfers between devices  12.3 us (29%)
  local copies, waits for them, and re-layouts  1.02 us (2%)
    ppermute x10, starting transfers between devices, exchange(): lax.ppermute(value, axis, [(i, i ^ apart) for i in range(lax.axis_size(ax...  12.3 us
    pallas_call x3, Pallas kernels, root_blocks(): pl.pallas_call(ordered(functools.partial(root_kernel, scale, len(queries)...  9.68 us
    pallas_call x1, Pallas kernels, theirs_block(): pl.pallas_call(ordered(functools.partial(theirs_kernel, scale, heads), af...  6.61 us
    pallas_call x1, Pallas kernels, mine_block(): pl.pallas_call(functools.partial(mine_kernel, scale, heads), out_shape=pa...  5.43 us
    pallas_call x1, Pallas kernels, first_block(): pl.pallas_call(functools.partial(first_kernel, scale, shared), out_shape=...  4.78 us
    pallas_call x2, Pallas kernels, merge(): pl.pallas_call(ordered(functools.partial(merge_kernel, last, heads, reque...  1.83 us
    unnamed x14, local copies, waits for them, and re-layouts  1.02 us
  transfers between devices with their start and end apart: 10, of which 0 were waited for; matrix products, arithmetic and copies ran while one was open for 0% of the time, Pallas kernels for 65%

profile of v4, /device:TPU:0, one launch (start us, length us, event | category | flops | bytes accessed | tf_op | source)
XLA Modules:
  0.0 42.4 jit_solution(6297930066634728424)
XLA Ops:
  0.0 0.5 %collective-permute-start = (bf16[1024,4,128]{2,1,0:T(4,128)(2,1)}, bf16[1024,4,128]{2,1,0:T(4,128)(2,1)S(1)}, u32[]{:S(2)}, u32[]{:S(2)}) collective-permute-start(bf16[1024,4,128]{2,1,0:T(4,128)(2,1)} %param.8), channel_id=1, source_target_pairs={{0,1},{1,0},{2,3},{3,2},{4,5},{5,4},{6,7},{7,6},{8,9},{9,8},{10,11... | collective-permute-start | bytes 3145736 | tf_op jit(solution)/shard_map/ppermute | solution.py:46
  0.5 0.1 collective-permute-start.1
  0.5 5.0 %collective-permute-start.2 = (bf16[16,32,128]{2,1,0:T(8,128)(2,1)}, bf16[16,32,128]{2,1,0:T(8,128)(2,1)S(1)}, u32[]{:S(2)}, u32[]{:S(2)}) collective-permute-start(bf16[16,32,128]{2,1,0:T(8,128)(2,1)} %query_ref.3), channel_id=1, source_target_pairs={{0,12},{4,8},{8,4},{12,0},{1,13},{5,9},{9,5},{13,1},{2,14},{6,10},... | collective-permute-start | bytes 393224 | tf_op jit(solution)/shard_map/ppermute | solution.py:46
  5.6 0.0 collective-permute-start.3
  5.6 0.5 %place.1.pair_ref.refs_1_ = s32[1]{0:T(128)} custom-call(s32[1]{0:T(128)} %bitcast.in_ref), custom_call_target="tpu_custom_call" | custom-call | flops 10000000000 | bytes 1 | tf_op jit(solution)/shard_map/place/pallas_call | solution.py:274
  6.1 0.7 %copy-done.2 = bf16[1024,4,128]{2,1,0:T(4,128)(2,1)S(1)} copy-done((bf16[1024,4,128]{2,1,0:T(4,128)(2,1)S(1)}, bf16[1024,4,128]{2,1,0:T(4,128)(2,1)}, u32[]{:S(2)}) %copy-start.2) | copy-done | bytes 1048600
  6.8 0.3 copy-done.3
  7.1 4.8 %first_block.1 = (bf16[2,2048,128]{2,1,0:T(8,128)(2,1)S(1)}, bf16[2,2048,128]{2,1,0:T(8,128)(2,1)S(1)}, bf16[528,128]{1,0:T(8,128)(2,1)S(1)}) custom-call(s32[1]{0:T(128)} %place.1.pair_ref.refs_1_, bf16[16,32,128]{2,1,0:T(8,128)(2,1)S(1)} %copy-done.4, bf16[4096,128]{1,0:T(8,128)(2,1)S(1)} %bitcast.9, bf16[4096,128]{1,0:T(8,128)(2,1)S(1)} %bitcast.10, ...), custom_call_target="tpu_custom_call" | custom-call | flops 1 | bytes 1 | tf_op jit(solution)/shard_map/first_block/pallas_call | solution.py:257
  11.9 2.1 %collective-permute-start.4 = (bf16[16,32,128]{2,1,0:T(8,128)(2,1)S(1)}, bf16[16,32,128]{2,1,0:T(8,128)(2,1)S(1)}, u32[]{:S(2)}, u32[]{:S(2)}) collective-permute-start(bf16[16,32,128]{2,1,0:T(8,128)(2,1)S(1)} %collective-permute-done.2.refs_2_), channel_id=1, source_target_pairs={{0,4},{4,0},{8,12},{12,8},{1,5},{5,1},{9,13},{13,9},{2,6},{6,2},{1... | collective-permute-start | bytes 393224 | tf_op jit(solution)/shard_map/ppermute | solution.py:46
  14.0 3.2 %root_blocks.3.refs_0_ = bf16[528,128]{1,0:T(8,128)(2,1)S(1)} custom-call(bf16[2,2048,128]{2,1,0:T(8,128)(2,1)S(1)} %get-tuple-element.14.refs_0_.refs_1_, bf16[2,2048,128]{2,1,0:T(8,128)(2,1)S(1)} %get-tuple-element.15.refs_1_.refs_2_, bf16[16,32,128]{2,1,0:T(8,128)(2,1)S(1)} %collective-permute-done.2.refs_2_), custom_call_target="tpu_custom_call" | custom-call | flops 1 | bytes 1 | tf_op jit(solution)/shard_map/root_blocks/pallas_call | solution.py:297
  17.2 0.0 copy-start
  17.2 0.0 copy-start.1
  17.2 0.0 copy-start.5
  17.2 0.0 copy-start.6
  17.2 0.8 %collective-permute-start.6 = (bf16[528,128]{1,0:T(8,128)(2,1)S(1)}, bf16[528,128]{1,0:T(8,128)(2,1)S(1)}, u32[]{:S(2)}, u32[]{:S(2)}) collective-permute-start(bf16[528,128]{1,0:T(8,128)(2,1)S(1)} %root_blocks.3.refs_0_), channel_id=1, source_target_pairs={{0,12},{4,8},{8,4},{12,0},{1,13},{5,9},{9,5},{13,1},{2,14},{6,10},... | collective-permute-start | bytes 405512 | tf_op jit(solution)/shard_map/ppermute | solution.py:46
  18.0 3.2 %root_blocks.4.refs_0_ = bf16[528,128]{1,0:T(8,128)(2,1)S(1)} custom-call(bf16[528,128]{1,0:T(8,128)(2,1)S(1)} %root_blocks.3.refs_0_, bf16[2,2048,128]{2,1,0:T(8,128)(2,1)S(1)} %get-tuple-element.14.refs_0_.refs_1_, bf16[2,2048,128]{2,1,0:T(8,128)(2,1)S(1)} %get-tuple-element.15.refs_1_.refs_2_, bf16[16,32,128]{2,1,0:T(8,128)(2,1)S(1)} %collective-permute-done.3.refs_3_), custom_call_target="tpu_custom_call" | custom-call | flops 1 | bytes 1 | tf_op jit(solution)/shard_map/root_blocks/pallas_call | solution.py:297
  21.2 0.7 %collective-permute-start.7 = (bf16[528,128]{1,0:T(8,128)(2,1)S(1)}, bf16[528,128]{1,0:T(8,128)(2,1)S(1)}, u32[]{:S(2)}, u32[]{:S(2)}) collective-permute-start(bf16[528,128]{1,0:T(8,128)(2,1)S(1)} %root_blocks.4.refs_0_), channel_id=1, source_target_pairs={{0,4},{4,0},{8,12},{12,8},{1,5},{5,1},{9,13},{13,9},{2,6},{6,2},{1... | collective-permute-start | bytes 405512 | tf_op jit(solution)/shard_map/ppermute | solution.py:46
  22.0 3.3 %root_blocks.5.refs_0_ = bf16[528,128]{1,0:T(8,128)(2,1)S(1)} custom-call(bf16[528,128]{1,0:T(8,128)(2,1)S(1)} %root_blocks.4.refs_0_, bf16[2,2048,128]{2,1,0:T(8,128)(2,1)S(1)} %get-tuple-element.14.refs_0_.refs_1_, bf16[2,2048,128]{2,1,0:T(8,128)(2,1)S(1)} %get-tuple-element.15.refs_1_.refs_2_, bf16[16,32,128]{2,1,0:T(8,128)(2,1)S(1)} %collective-permute-done.4.refs_3_), custom_call_target="tpu_custom_call" | custom-call | flops 1 | bytes 1 | tf_op jit(solution)/shard_map/root_blocks/pallas_call | solution.py:297
  25.3 3.0 %collective-permute-start.8 = (bf16[528,128]{1,0:T(8,128)(2,1)S(1)}, bf16[528,128]{1,0:T(8,128)(2,1)S(1)}, u32[]{:S(2)}, u32[]{:S(2)}) collective-permute-start(bf16[528,128]{1,0:T(8,128)(2,1)S(1)} %root_blocks.5.refs_0_), channel_id=1, source_target_pairs={{0,8},{4,12},{8,0},{12,4},{1,9},{5,13},{9,1},{13,5},{2,10},{6,14},... | collective-permute-start | bytes 405512 | tf_op jit(solution)/shard_map/ppermute | solution.py:46
  28.4 6.6 %theirs_block.1 = (bf16[528,128]{1,0:T(8,128)(2,1)S(1)}, bf16[2,4,1024,128]{3,2,1,0:T(8,128)(2,1)S(1)}, bf16[2,4,1024,128]{3,2,1,0:T(8,128)(2,1)S(1)}, s32[2,256,128]{2,1,0:T(8,128)S(1)}) custom-call(bf16[528,128]{1,0:T(8,128)(2,1)S(1)} %root_blocks.5.refs_0_, s32[1]{0:T(128)} %place.1.pair_ref.refs_1_, s32[16]{0:T(128)S(1)} %copy-done.5, s32[16]{0:T(128)S(1)} %copy-done.6, ...), custom_call_target="tpu_custom_call" | custom-call | flops 1 | bytes 1 | tf_op jit(solution)/shard_map/theirs_block/pallas_call | solution.py:354
  35.0 0.1 collective-permute-start.9
  35.1 5.4 %mine_block.1.refs_0_ = bf16[528,128]{1,0:T(8,128)(2,1)S(1)} custom-call(s32[1]{0:T(128)} %place.1.pair_ref.refs_1_, bf16[16,32,128]{2,1,0:T(8,128)(2,1)S(1)} %copy-done.4, bf16[2,4,1024,128]{3,2,1,0:T(8,128)(2,1)S(1)} %get-tuple-element.18.k_ref, bf16[2,4,1024,128]{3,2,1,0:T(8,128)(2,1)S(1)} %get-tuple-element.19.v_ref, ...), custom_call_target="tpu_custom_call" | custom-call | flops 1 | bytes 1 | tf_op jit(solution)/shard_map/mine_block/pallas_call | solution.py:367
  40.5 0.7 %merge_some.1.refs_0_ = bf16[528,128]{1,0:T(8,128)(2,1)S(1)} custom-call(bf16[528,128]{1,0:T(8,128)(2,1)S(1)} %mine_block.1.refs_0_, bf16[528,128]{1,0:T(8,128)(2,1)S(1)} %collective-permute-done.7.refs_1_, bf16[528,128]{1,0:T(8,128)(2,1)S(1)} %collective-permute-done.8.refs_2_), custom_call_target="tpu_custom_call" | custom-call | flops 1 | bytes 1 | tf_op jit(solution)/shard_map/merge_some/pallas_call | solution.py:400
  41.2 1.1 %merge_last.1 = bf16[16,32,128]{2,1,0:T(8,128)(2,1)} custom-call(bf16[528,128]{1,0:T(8,128)(2,1)S(1)} %merge_some.1.refs_0_, bf16[528,128]{1,0:T(8,128)(2,1)S(1)} %collective-permute-done.9.refs_1_), custom_call_target="tpu_custom_call" | custom-call | flops 1 | bytes 1 | tf_op jit(solution)/shard_map/merge_last/pallas_call | solution.py:400
  (19 shorter events, 0.0 us)
Async XLA Ops:
  0.0 6.1 %collective-permute-start = (bf16[1024,4,128]{2,1,0:T(4,128)(2,1)}, bf16[1024,4,128]{2,1,0:T(4,128)(2,1)S(1)}, u32[]{:S(2)}, u32[]{:S(2)}) collective-permute-start(bf16[1024,4,128]{2,1,0:T(4,128)(2,1)} %param.8), channel_id=1, source_target_pairs={{0,1},{1,0},{2,3},{3,2},{4,5},{5,4},{6,7},{7,6},{8,9},{9,8},{10,11... | collective-permute-start | bytes 3145736 | tf_op jit(solution)/shard_map/ppermute | solution.py:46
  0.5 5.7 %collective-permute-start.1 = (bf16[1024,4,128]{2,1,0:T(4,128)(2,1)}, bf16[1024,4,128]{2,1,0:T(4,128)(2,1)S(1)}, u32[]{:S(2)}, u32[]{:S(2)}) collective-permute-start(bf16[1024,4,128]{2,1,0:T(4,128)(2,1)} %param.9), channel_id=1, source_target_pairs={{0,1},{1,0},{2,3},{3,2},{4,5},{5,4},{6,7},{7,6},{8,9},{9,8},{10,11... | collective-permute-start | bytes 3145736 | tf_op jit(solution)/shard_map/ppermute | solution.py:46
  0.5 11.4 %collective-permute-start.2 = (bf16[16,32,128]{2,1,0:T(8,128)(2,1)}, bf16[16,32,128]{2,1,0:T(8,128)(2,1)S(1)}, u32[]{:S(2)}, u32[]{:S(2)}) collective-permute-start(bf16[16,32,128]{2,1,0:T(8,128)(2,1)} %query_ref.3), channel_id=1, source_target_pairs={{0,12},{4,8},{8,4},{12,0},{1,13},{5,9},{9,5},{13,1},{2,14},{6,10},... | collective-permute-start | bytes 393224 | tf_op jit(solution)/shard_map/ppermute | solution.py:46
  5.6 12.5 %collective-permute-start.3 = (bf16[16,32,128]{2,1,0:T(8,128)(2,1)}, bf16[16,32,128]{2,1,0:T(8,128)(2,1)S(1)}, u32[]{:S(2)}, u32[]{:S(2)}) collective-permute-start(bf16[16,32,128]{2,1,0:T(8,128)(2,1)} %query_ref.3), channel_id=1, source_target_pairs={{0,4},{4,0},{8,12},{12,8},{1,5},{5,1},{9,13},{13,9},{2,6},{6,2},{1... | collective-permute-start | bytes 393224 | tf_op jit(solution)/shard_map/ppermute | solution.py:46
  5.6 1.2 %copy-start.2 = (bf16[1024,4,128]{2,1,0:T(4,128)(2,1)S(1)}, bf16[1024,4,128]{2,1,0:T(4,128)(2,1)}, u32[]{:S(2)}) copy-start(bf16[1024,4,128]{2,1,0:T(4,128)(2,1)} %param.8) | copy-start | bytes 3145732
  5.6 1.5 %copy-start.3 = (bf16[1024,4,128]{2,1,0:T(4,128)(2,1)S(1)}, bf16[1024,4,128]{2,1,0:T(4,128)(2,1)}, u32[]{:S(2)}) copy-start(bf16[1024,4,128]{2,1,0:T(4,128)(2,1)} %param.9) | copy-start | bytes 3145732
  5.6 1.5 %copy-start.4 = (bf16[16,32,128]{2,1,0:T(8,128)(2,1)S(1)}, bf16[16,32,128]{2,1,0:T(8,128)(2,1)}, u32[]{:S(2)}) copy-start(bf16[16,32,128]{2,1,0:T(8,128)(2,1)} %query_ref.3) | copy-start | bytes 393220
  11.9 10.1 %collective-permute-start.4 = (bf16[16,32,128]{2,1,0:T(8,128)(2,1)S(1)}, bf16[16,32,128]{2,1,0:T(8,128)(2,1)S(1)}, u32[]{:S(2)}, u32[]{:S(2)}) collective-permute-start(bf16[16,32,128]{2,1,0:T(8,128)(2,1)S(1)} %collective-permute-done.2.refs_2_), channel_id=1, source_target_pairs={{0,4},{4,0},{8,12},{12,8},{1,5},{5,1},{9,13},{13,9},{2,6},{6,2},{1... | collective-permute-start | bytes 393224 | tf_op jit(solution)/shard_map/ppermute | solution.py:46
  14.0 14.3 %collective-permute-start.5 = (bf16[16,32,128]{2,1,0:T(8,128)(2,1)S(1)}, bf16[16,32,128]{2,1,0:T(8,128)(2,1)S(1)}, u32[]{:S(2)}, u32[]{:S(2)}) collective-permute-start(bf16[16,32,128]{2,1,0:T(8,128)(2,1)S(1)} %copy-done.4), channel_id=1, source_target_pairs={{0,1},{1,0},{2,3},{3,2},{4,5},{5,4},{6,7},{7,6},{8,9},{9,8},{10,11... | collective-permute-start | bytes 393224 | tf_op jit(solution)/shard_map/ppermute | solution.py:46
  17.2 11.2 %copy-start = (bf16[2,1024,4,128]{3,2,1,0:T(4,128)(2,1)S(1)}, bf16[2,1024,4,128]{3,2,1,0:T(4,128)(2,1)}, u32[]{:S(2)}) copy-start(bf16[2,1024,4,128]{3,2,1,0:T(4,128)(2,1)} %param.10) | copy-start | bytes 6291460
  17.2 11.2 %copy-start.1 = (bf16[2,1024,4,128]{3,2,1,0:T(4,128)(2,1)S(1)}, bf16[2,1024,4,128]{3,2,1,0:T(4,128)(2,1)}, u32[]{:S(2)}) copy-start(bf16[2,1024,4,128]{3,2,1,0:T(4,128)(2,1)} %param.11) | copy-start | bytes 6291460
  17.2 11.2 %copy-start.5 = (s32[16]{0:T(128)S(1)}, s32[16]{0:T(128)}, u32[]{:S(2)}) copy-start(s32[16]{0:T(128)} %refs_2_.1) | copy-start | bytes 196
  17.2 11.1 %copy-start.6 = (s32[16]{0:T(128)S(1)}, s32[16]{0:T(128)}, u32[]{:S(2)}) copy-start(s32[16]{0:T(128)} %refs_3_.1) | copy-start | bytes 196
  17.2 17.8 %collective-permute-start.6 = (bf16[528,128]{1,0:T(8,128)(2,1)S(1)}, bf16[528,128]{1,0:T(8,128)(2,1)S(1)}, u32[]{:S(2)}, u32[]{:S(2)}) collective-permute-start(bf16[528,128]{1,0:T(8,128)(2,1)S(1)} %root_blocks.3.refs_0_), channel_id=1, source_target_pairs={{0,12},{4,8},{8,4},{12,0},{1,13},{5,9},{9,5},{13,1},{2,14},{6,10},... | collective-permute-start | bytes 405512 | tf_op jit(solution)/shard_map/ppermute | solution.py:46
  21.2 19.3 %collective-permute-start.7 = (bf16[528,128]{1,0:T(8,128)(2,1)S(1)}, bf16[528,128]{1,0:T(8,128)(2,1)S(1)}, u32[]{:S(2)}, u32[]{:S(2)}) collective-permute-start(bf16[528,128]{1,0:T(8,128)(2,1)S(1)} %root_blocks.4.refs_0_), channel_id=1, source_target_pairs={{0,4},{4,0},{8,12},{12,8},{1,5},{5,1},{9,13},{13,9},{2,6},{6,2},{1... | collective-permute-start | bytes 405512 | tf_op jit(solution)/shard_map/ppermute | solution.py:46
  25.3 15.2 %collective-permute-start.8 = (bf16[528,128]{1,0:T(8,128)(2,1)S(1)}, bf16[528,128]{1,0:T(8,128)(2,1)S(1)}, u32[]{:S(2)}, u32[]{:S(2)}) collective-permute-start(bf16[528,128]{1,0:T(8,128)(2,1)S(1)} %root_blocks.5.refs_0_), channel_id=1, source_target_pairs={{0,8},{4,12},{8,0},{12,4},{1,9},{5,13},{9,1},{13,5},{2,10},{6,14},... | collective-permute-start | bytes 405512 | tf_op jit(solution)/shard_map/ppermute | solution.py:46
  35.0 6.3 %collective-permute-start.9 = (bf16[528,128]{1,0:T(8,128)(2,1)S(1)}, bf16[528,128]{1,0:T(8,128)(2,1)S(1)}, u32[]{:S(2)}, u32[]{:S(2)}) collective-permute-start(bf16[528,128]{1,0:T(8,128)(2,1)S(1)} %get-tuple-element.22), channel_id=1, source_target_pairs={{0,1},{1,0},{2,3},{3,2},{4,5},{5,4},{6,7},{7,6},{8,9},{9,8},{10,11... | collective-permute-start | bytes 405512 | tf_op jit(solution)/shard_map/ppermute | solution.py:46

commit v5 on v4

--- a/solution.py
+++ b/solution.py
@@ -38,6 +38,10 @@
     return pl.CostEstimate(flops=1, bytes_accessed=1, transcendentals=0)
 
 
+def heavy_cost():
+    return pl.CostEstimate(flops=10**10, bytes_accessed=1, transcendentals=0)
+
+
 def kernel_params(grant=vmem_grant):
     return pltpu.CompilerParams(vmem_limit_bytes=grant)
 
@@ -82,16 +86,19 @@
 
 def evaluate(pieces, scale, exact):
     state = None
-    visible = None
+    hidden = None
     for query, keys, values, limits in pieces:
         scores = lax.dot_general(
             query, keys, (((1,), (1,)), ((), ())), preferred_element_type=jnp.float32
         )
         seen = None
         if limits is not None:
-            seen = lax.broadcasted_iota(jnp.int32, scores.shape, 1) < limits
-            some = limits > 0
-            visible = some if visible is None else visible | some
+            each = scores.shape[1] // len(limits)
+            ends = [limit for limit in limits for _ in range(each // lane_count)]
+            seen = lax.broadcasted_iota(jnp.int32, scores.shape, 1) < jnp.concatenate(ends, axis=1)
+            counts = [limit - b * each for b, limit in enumerate(limits)]
+            most = functools.reduce(jnp.maximum, counts)
+            hidden = jnp.where(most > 0, 0.0, 1.0)[:, :1]
         if exact:
             if seen is not None:
                 scores = jnp.where(seen, scores, masked_floor)
@@ -115,17 +122,16 @@
         else:
             state = (state[0] + sums, state[1] + totals, None)
     sums, totals, largest = state
-    sound = (totals > least_total) & (totals < most_total)
-    safe = totals
-    if visible is not None:
-        sound = sound | jnp.logical_not(visible)
-        safe = jnp.where(visible, totals, 1.0)
-    level = jnp.log2(safe)
+    sound = jnp.where((totals > least_total) & (totals < most_total), 1.0, 0.0)
+    if hidden is not None:
+        sound = jnp.maximum(sound, hidden)
+        totals = totals + hidden
+    level = jnp.log2(totals)
     if exact:
         level = level + largest
-    if visible is not None:
-        level = jnp.where(visible, level, masked_floor)
-    return sums * (1.0 / safe), level, sound
+    if hidden is not None:
+        level = level + hidden * masked_floor
+    return sums * (1.0 / totals), level, sound
 
 
 def combine(parts):
@@ -156,7 +162,7 @@
                     out, level = combine([(out, level), *added])
                 outs.append(out)
                 levels.append(level)
-                least = jnp.minimum(least, jnp.where(sound, 1.0, 0.0))
+                least = jnp.minimum(least, sound)
             store_packed(out_ref, heads, requests, group_size, outs, levels, same)
         return jnp.min(least)
 
@@ -238,10 +244,10 @@
 
 
 def first_kernel(
-    scale, shared, pair_ref, query_ref, ko_ref, vo_ref, kp_ref, vp_ref, k_ref, v_ref, out_ref, wide_ref
+    scale, shared, query_ref, ko_ref, vo_ref, kp_ref, vp_ref, k_ref, v_ref, out_ref, wide_ref
 ):
     heads, both, _ = k_ref.shape
-    first = pair_ref[0] * heads
+    first = lax.axis_index("pair") * heads
     for base, keys, values in ((0, ko_ref, vo_ref), (both // 2, kp_ref, vp_ref)):
         split_heads(keys, k_ref, wide_ref, shared, first, heads, base)
         split_heads(values, v_ref, wide_ref, shared, first, heads, base)
@@ -251,35 +257,45 @@
     write_partials([(out_ref, pieces)], scale, heads, requests, group_size)
 
 
-def first_block(pair_index, query, keys, values, other_keys, other_values, scale, heads):
+def first_block(query, keys, values, other_keys, other_values, scale, heads, after):
     tokens, shared, width = keys.shape
     shape = jax.ShapeDtypeStruct((heads, 2 * tokens, width), keys.dtype)
     return pl.pallas_call(
-        functools.partial(first_kernel, scale, shared),
+        ordered(functools.partial(first_kernel, scale, shared), after),
         out_shape=(shape, shape, packed_shape(query)),
-        in_specs=[smem_spec()] + [vmem_spec()] * 5,
+        in_specs=any_specs(after) + [vmem_spec()] * 5,
         out_specs=(vmem_spec(),) * 3,
         scratch_shapes=[pltpu.VMEM((chunk_tokens * shared, width), jnp.float32)],
         compiler_params=kernel_params(),
         cost_estimate=light_cost(),
         name="first_block",
-    )(pair_index, query, flat(keys), flat(values), flat(other_keys), flat(other_values))
-
-
-def place_kernel(in_ref, out_ref):
-    out_ref[0] = in_ref[0]
-
-
-def place(pair_index):
-    return pl.pallas_call(
-        place_kernel,
-        out_shape=jax.ShapeDtypeStruct(pair_index.shape, pair_index.dtype),
-        in_specs=[smem_spec()],
-        out_specs=smem_spec(),
+    )(*after, query, flat(keys), flat(values), flat(other_keys), flat(other_values))
+
+
+def limits_kernel(tokens, group_size, branch_ref, seen_ref, limit_ref):
+    branches = limit_ref.shape[0]
+    before = lax.axis_index("pair") * tokens
+    for b in range(branches):
+        for r in range(branch_ref.shape[0]):
+            here = branch_ref[r] % branches == b
+            count = jnp.clip(seen_ref[r] - before, 0, tokens)
+            limit = b * tokens + jnp.where(here, count, 0)
+            limit_ref[b, pl.ds(r * group_size, group_size), :] = jnp.full(
+                (group_size, lane_count), limit, jnp.int32
+            )
+
+
+def limits_block(branch, seen, branches, tokens, group_size):
+    shape = (branches, branch.shape[0] * group_size, lane_count)
+    return pl.pallas_call(
+        functools.partial(limits_kernel, tokens, group_size),
+        out_shape=jax.ShapeDtypeStruct(shape, jnp.int32),
+        in_specs=[smem_spec()] * 2,
+        out_specs=vmem_spec(),
         compiler_params=kernel_params(2**20),
-        cost_estimate=pl.CostEstimate(flops=10**10, bytes_accessed=1, transcendentals=0),
-        name="place",
-    )(pair_index)
+        cost_estimate=heavy_cost(),
+        name="limits_block",
+    )(branch, seen)
 
 
 def root_kernel(scale, count, k_ref, v_ref, *refs):
@@ -307,72 +323,63 @@
 
 def branch_pieces(query_ref, k_ref, v_ref, limit_ref, owner, heads, group_size):
     def pieces(h):
-        query = head_queries(query_ref, h, group_size)
         at = owner * heads + h
-        return [
-            (query, k_ref[b, at], v_ref[b, at], limit_ref[b][:, :1]) for b in range(k_ref.shape[0])
-        ]
+        limits = [limit_ref[b] for b in range(limit_ref.shape[0])]
+        return [(head_queries(query_ref, h, group_size), k_ref[at], v_ref[at], limits)]
 
     return pieces
 
 
 def theirs_kernel(
-    scale, heads, pair_ref, branch_ref, seen_ref, query_ref, bk_ref, bv_ref,
-    out_ref, k_ref, v_ref, limit_ref, wide_ref,
+    scale, heads, limit_ref, query_ref, bk_ref, bv_ref, out_ref, k_ref, v_ref, wide_ref
 ):
     requests, local_heads, _ = query_ref.shape
-    branches, shared, tokens, _ = k_ref.shape
+    shared, slots, _ = k_ref.shape
+    branches = bk_ref.shape[0]
     group_size = local_heads // heads
     for b in range(branches):
-        split_heads(bk_ref.at[b], k_ref.at[b], wide_ref, shared, 0, shared, 0)
-        split_heads(bv_ref.at[b], v_ref.at[b], wide_ref, shared, 0, shared, 0)
-        for r in range(requests):
-            here = branch_ref[r] % branches == b
-            limit = jnp.where(here, seen_ref[r] - pair_ref[0] * tokens, 0)
-            limit_ref[b, pl.ds(r * group_size, group_size), :] = jnp.full(
-                (group_size, lane_count), limit, jnp.int32
-            )
-    owner = 1 - pair_ref[0]
+        base = b * (slots // branches)
+        split_heads(bk_ref.at[b], k_ref, wide_ref, shared, 0, shared, base)
+        split_heads(bv_ref.at[b], v_ref, wide_ref, shared, 0, shared, base)
+    owner = 1 - lax.axis_index("pair")
     pieces = branch_pieces(query_ref, k_ref, v_ref, limit_ref, owner, heads, group_size)
     write_partials([(out_ref, pieces)], scale, heads, requests, group_size)
 
 
-def mine_kernel(scale, heads, pair_ref, query_ref, k_ref, v_ref, limit_ref, *refs):
+def mine_kernel(scale, heads, limit_ref, query_ref, k_ref, v_ref, *refs):
     *others, out_ref = refs
     requests, local_heads, _ = query_ref.shape
     group_size = local_heads // heads
-    pieces = branch_pieces(query_ref, k_ref, v_ref, limit_ref, pair_ref[0], heads, group_size)
+    owner = lax.axis_index("pair")
+    pieces = branch_pieces(query_ref, k_ref, v_ref, limit_ref, owner, heads, group_size)
     write_partials([(out_ref, pieces)], scale, heads, requests, group_size, others)
 
 
-def theirs_block(pair_index, branch, seen, query, keys, values, scale, heads, after):
+def theirs_block(limits, query, keys, values, scale, heads, after):
     branches, tokens, shared, width = keys.shape
-    requests, local_heads, _ = query.shape
-    rows = requests * local_heads // heads
-    held = jax.ShapeDtypeStruct((branches, shared, tokens, width), keys.dtype)
-    limits = jax.ShapeDtypeStruct((branches, rows, lane_count), jnp.int32)
+    held = jax.ShapeDtypeStruct((shared, branches * tokens, width), keys.dtype)
     return pl.pallas_call(
         ordered(functools.partial(theirs_kernel, scale, heads), after),
-        out_shape=(packed_shape(query), held, held, limits),
-        in_specs=any_specs(after) + [smem_spec()] * 3 + [vmem_spec()] * 3,
-        out_specs=(vmem_spec(),) * 4,
+        out_shape=(packed_shape(query), held, held),
+        in_specs=any_specs(after) + [vmem_spec()] * 4,
+        out_specs=(vmem_spec(),) * 3,
         scratch_shapes=[pltpu.VMEM((chunk_tokens * shared, width), jnp.float32)],
         compiler_params=kernel_params(),
         cost_estimate=light_cost(),
         name="theirs_block",
-    )(*after, pair_index, branch, seen, query, flat(keys), flat(values))
-
-
-def mine_block(pair_index, query, keys, values, limits, others, scale, heads):
+    )(*after, limits, query, flat(keys), flat(values))
+
+
+def mine_block(limits, query, keys, values, others, scale, heads):
     return pl.pallas_call(
         functools.partial(mine_kernel, scale, heads),
         out_shape=packed_shape(query),
-        in_specs=[smem_spec()] + [vmem_spec()] * (4 + len(others)),
+        in_specs=[vmem_spec()] * (4 + len(others)),
         out_specs=vmem_spec(),
         compiler_params=kernel_params(),
-        cost_estimate=light_cost(),
+        cost_estimate=heavy_cost(),
         name="mine_block",
-    )(pair_index, query, keys, values, limits, *others)
+    )(limits, query, keys, values, *others)
 
 
 def merge_kernel(last, heads, requests, group_size, *refs):
@@ -415,7 +422,8 @@
     heads = shared // lax.axis_size("pair")
     group_size = local_heads // heads
     scale = math.log2(math.e) / math.sqrt(width)
-    pair_index = place(lax.axis_index("pair").astype(jnp.int32).reshape(1))
+    branches, tokens, _, _ = branch_keys.shape
+    limits = limits_block(request_branch, seen_tokens, branches, tokens, group_size)
 
     other_keys = exchange(root_keys, "pair", 1)
     other_values = exchange(root_values, "pair", 1)
@@ -424,7 +432,7 @@
     arrived = {apart: exchange(queries, "blk", apart) for apart in direct}
 
     keys, values, own = first_block(
-        pair_index, queries, root_keys, root_values, other_keys, other_values, scale, heads
+        queries, root_keys, root_values, other_keys, other_values, scale, heads, (limits,)
     )
     groups = [(apart, apart ^ 1) for apart in direct if apart > 1]
     for far, near in groups:
@@ -435,15 +443,14 @@
     for apart in order:
         previous = root_blocks([arrived[apart]], keys, values, scale, previous)
         returned[apart] = exchange(previous[0], "blk", apart)
-    theirs, held_keys, held_values, limits = theirs_block(
-        pair_index, request_branch, seen_tokens, other_queries, branch_keys, branch_values,
-        scale, heads, previous,
+    theirs, held_keys, held_values = theirs_block(
+        limits, other_queries, branch_keys, branch_values, scale, heads, previous
     )
     from_partner = exchange(theirs, "pair", 1)
-    early = [own] + [returned.pop(apart) for apart in order if apart > 2 and apart % 2]
-    most = mine_block(pair_index, queries, held_keys, held_values, limits, early, scale, heads)
-    most = merge([most, *returned.values()], False, heads, requests, group_size)
-    return merge([most, from_partner], True, heads, requests, group_size)
+    mine = mine_block(limits, queries, held_keys, held_values, [own], scale, heads)
+    last = returned.pop(order[-1])
+    most = merge([mine, from_partner, *returned.values()], False, heads, requests, group_size)
+    return merge([most, last], True, heads, requests, group_size)
 
 
 def solution(mesh):

time: 42.6 us -> 40.3 us (0.946)
  Pallas kernels: 28.8 us -> 26.2 us
    pallas_call x1, Pallas kernels: 6.61 us -> 5.14 us  [theirs_block(): pl.pallas_call(ordered(functools.partial(theirs_kernel, scale, heads), af...]
    pallas_call x1, Pallas kernels: 5.43 us -> 4.56 us  [mine_block(): pl.pallas_call(functools.partial(mine_kernel, scale, heads), out_shape=pa...]
  transfers between devices with their start and end apart: 10 -> 10, of which waited for: 0 -> 0; matrix products, arithmetic and copies ran while one was open for 0% -> 0% of each run, Pallas kernels for 65% -> 63%
where the time goes in v5:
time: 40.3 us; the launch traced here: 40.1 us
  Pallas kernels  26.2 us (65%)
  starting transfers between devices  12.4 us (31%)
  local copies, waits for them, and re-layouts  1.33 us (3%)
    ppermute x10, starting transfers between devices, exchange(): lax.ppermute(value, axis, [(i, i ^ apart) for i in range(lax.axis_size(ax...  12.4 us
    pallas_call x3, Pallas kernels, root_blocks(): pl.pallas_call(ordered(functools.partial(root_kernel, scale, len(queries)...  9.56 us
    pallas_call x1, Pallas kernels, theirs_block(): pl.pallas_call(ordered(functools.partial(theirs_kernel, scale, heads), af...  5.14 us
    pallas_call x1, Pallas kernels, mine_block(): pl.pallas_call(functools.partial(mine_kernel, scale, heads), out_shape=pa...  4.56 us
    pallas_call x1, Pallas kernels, first_block(): pl.pallas_call(ordered(functools.partial(first_kernel, scale, shared), af...  4.3 us
    pallas_call x2, Pallas kernels, merge(): pl.pallas_call(ordered(functools.partial(merge_kernel, last, heads, reque...  2.01 us
    unnamed x14, local copies, waits for them, and re-layouts  1.33 us
  transfers between devices with their start and end apart: 10, of which 0 were waited for; matrix products, arithmetic and copies ran while one was open for 0% of the time, Pallas kernels for 63%

profile of v5, /device:TPU:0, one launch (start us, length us, event | category | flops | bytes accessed | tf_op | source)
XLA Modules:
  0.0 40.1 jit_solution(13673377885220963560)
XLA Ops:
  0.0 0.5 %collective-permute-start = (bf16[1024,4,128]{2,1,0:T(4,128)(2,1)}, bf16[1024,4,128]{2,1,0:T(4,128)(2,1)S(1)}, u32[]{:S(2)}, u32[]{:S(2)}) collective-permute-start(bf16[1024,4,128]{2,1,0:T(4,128)(2,1)} %param.8), channel_id=1, source_target_pairs={{0,1},{1,0},{2,3},{3,2},{4,5},{5,4},{6,7},{7,6},{8,9},{9,8},{10,11... | collective-permute-start | bytes 3145736 | tf_op jit(solution)/shard_map/ppermute | solution.py:50
  0.5 0.1 collective-permute-start.1
  0.6 5.0 %collective-permute-start.2 = (bf16[16,32,128]{2,1,0:T(8,128)(2,1)}, bf16[16,32,128]{2,1,0:T(8,128)(2,1)S(1)}, u32[]{:S(2)}, u32[]{:S(2)}) collective-permute-start(bf16[16,32,128]{2,1,0:T(8,128)(2,1)} %query_ref.1), channel_id=1, source_target_pairs={{0,12},{4,8},{8,4},{12,0},{1,13},{5,9},{9,5},{13,1},{2,14},{6,10},... | collective-permute-start | bytes 393224 | tf_op jit(solution)/shard_map/ppermute | solution.py:50
  5.6 0.0 collective-permute-start.3
  5.6 0.7 %copy-done.5 = s32[16]{0:T(128)S(1)} copy-done((s32[16]{0:T(128)S(1)}, s32[16]{0:T(128)}, u32[]{:S(2)}) %copy-start.5) | copy-done | bytes 88
  6.3 0.7 %copy-done.6 = s32[16]{0:T(128)S(1)} copy-done((s32[16]{0:T(128)S(1)}, s32[16]{0:T(128)}, u32[]{:S(2)}) %copy-start.6) | copy-done | bytes 88
  7.0 0.6 %limits_block.1.refs_0_.refs_1_.limit_ref = s32[2,256,128]{2,1,0:T(8,128)S(1)} custom-call(s32[16]{0:T(128)S(1)} %copy-done.5, s32[16]{0:T(128)S(1)} %copy-done.6), custom_call_target="tpu_custom_call" | custom-call | flops 10000000000 | bytes 1 | tf_op jit(solution)/shard_map/limits_block/pallas_call | solution.py:290
  7.6 0.0 collective-permute-done
  7.7 4.3 %first_block.1 = (bf16[2,2048,128]{2,1,0:T(8,128)(2,1)S(1)}, bf16[2,2048,128]{2,1,0:T(8,128)(2,1)S(1)}, bf16[528,128]{1,0:T(8,128)(2,1)S(1)}) custom-call(s32[2,256,128]{2,1,0:T(8,128)S(1)} %limits_block.1.refs_0_.refs_1_.limit_ref, bf16[16,32,128]{2,1,0:T(8,128)(2,1)S(1)} %copy-done.4, bf16[4096,128]{1,0:T(8,128)(2,1)S(1)} %bitcast.8, ...), custom_call_target="tpu_custom_call" | custom-call | flops 1 | bytes 1 | tf_op jit(solution)/shard_map/first_block/pallas_call | solution.py:263
  12.0 2.1 %collective-permute-start.4 = (bf16[16,32,128]{2,1,0:T(8,128)(2,1)S(1)}, bf16[16,32,128]{2,1,0:T(8,128)(2,1)S(1)}, u32[]{:S(2)}, u32[]{:S(2)}) collective-permute-start(bf16[16,32,128]{2,1,0:T(8,128)(2,1)S(1)} %collective-permute-done.2.refs_2_), channel_id=1, source_target_pairs={{0,4},{4,0},{8,12},{12,8},{1,5},{5,1},{9,13},{13,9},{2,6},{6,2},{1... | collective-permute-start | bytes 393224 | tf_op jit(solution)/shard_map/ppermute | solution.py:50
  14.1 3.1 %root_blocks.3.refs_0_ = bf16[528,128]{1,0:T(8,128)(2,1)S(1)} custom-call(bf16[2,2048,128]{2,1,0:T(8,128)(2,1)S(1)} %get-tuple-element.13.refs_0_.refs_1_, bf16[2,2048,128]{2,1,0:T(8,128)(2,1)S(1)} %get-tuple-element.14.refs_1_.refs_2_, bf16[16,32,128]{2,1,0:T(8,128)(2,1)S(1)} %collective-permute-done.2.refs_2_), custom_call_target="tpu_custom_call" | custom-call | flops 1 | bytes 1 | tf_op jit(solution)/shard_map/root_blocks/pallas_call | solution.py:313
  17.2 0.0 copy-start
  17.2 0.0 copy-start.1
  17.2 0.6 %collective-permute-start.7 = (bf16[528,128]{1,0:T(8,128)(2,1)S(1)}, bf16[528,128]{1,0:T(8,128)(2,1)S(1)}, u32[]{:S(2)}, u32[]{:S(2)}) collective-permute-start(bf16[528,128]{1,0:T(8,128)(2,1)S(1)} %root_blocks.3.refs_0_), channel_id=1, source_target_pairs={{0,12},{4,8},{8,4},{12,0},{1,13},{5,9},{9,5},{13,1},{2,14},{6,10},... | collective-permute-start | bytes 405512 | tf_op jit(solution)/shard_map/ppermute | solution.py:50
  17.8 3.1 %root_blocks.4.refs_0_ = bf16[528,128]{1,0:T(8,128)(2,1)S(1)} custom-call(bf16[528,128]{1,0:T(8,128)(2,1)S(1)} %root_blocks.3.refs_0_, bf16[2,2048,128]{2,1,0:T(8,128)(2,1)S(1)} %get-tuple-element.13.refs_0_.refs_1_, bf16[2,2048,128]{2,1,0:T(8,128)(2,1)S(1)} %get-tuple-element.14.refs_1_.refs_2_, bf16[16,32,128]{2,1,0:T(8,128)(2,1)S(1)} %collective-permute-done.3.refs_3_), custom_call_target="tpu_custom_call" | custom-call | flops 1 | bytes 1 | tf_op jit(solution)/shard_map/root_blocks/pallas_call | solution.py:313
  20.9 0.7 %collective-permute-start.8 = (bf16[528,128]{1,0:T(8,128)(2,1)S(1)}, bf16[528,128]{1,0:T(8,128)(2,1)S(1)}, u32[]{:S(2)}, u32[]{:S(2)}) collective-permute-start(bf16[528,128]{1,0:T(8,128)(2,1)S(1)} %root_blocks.4.refs_0_), channel_id=1, source_target_pairs={{0,4},{4,0},{8,12},{12,8},{1,5},{5,1},{9,13},{13,9},{2,6},{6,2},{1... | collective-permute-start | bytes 405512 | tf_op jit(solution)/shard_map/ppermute | solution.py:50
  21.6 3.3 %root_blocks.5.refs_0_ = bf16[528,128]{1,0:T(8,128)(2,1)S(1)} custom-call(bf16[528,128]{1,0:T(8,128)(2,1)S(1)} %root_blocks.4.refs_0_, bf16[2,2048,128]{2,1,0:T(8,128)(2,1)S(1)} %get-tuple-element.13.refs_0_.refs_1_, bf16[2,2048,128]{2,1,0:T(8,128)(2,1)S(1)} %get-tuple-element.14.refs_1_.refs_2_, bf16[16,32,128]{2,1,0:T(8,128)(2,1)S(1)} %collective-permute-done.4.refs_3_), custom_call_target="tpu_custom_call" | custom-call | flops 1 | bytes 1 | tf_op jit(solution)/shard_map/root_blocks/pallas_call | solution.py:313
  24.9 3.3 %collective-permute-start.9 = (bf16[528,128]{1,0:T(8,128)(2,1)S(1)}, bf16[528,128]{1,0:T(8,128)(2,1)S(1)}, u32[]{:S(2)}, u32[]{:S(2)}) collective-permute-start(bf16[528,128]{1,0:T(8,128)(2,1)S(1)} %root_blocks.5.refs_0_), channel_id=1, source_target_pairs={{0,8},{4,12},{8,0},{12,4},{1,9},{5,13},{9,1},{13,5},{2,10},{6,14},... | collective-permute-start | bytes 405512 | tf_op jit(solution)/shard_map/ppermute | solution.py:50
  28.3 0.0 collective-permute-done.5.refs_2_
  28.3 5.1 %theirs_block.1 = (bf16[528,128]{1,0:T(8,128)(2,1)S(1)}, bf16[4,2048,128]{2,1,0:T(8,128)(2,1)S(1)}, bf16[4,2048,128]{2,1,0:T(8,128)(2,1)S(1)}) custom-call(bf16[528,128]{1,0:T(8,128)(2,1)S(1)} %root_blocks.5.refs_0_, s32[2,256,128]{2,1,0:T(8,128)S(1)} %limits_block.1.refs_0_.refs_1_.limit_ref, bf16[16,32,128]{2,1,0:T(8,128)(2,1)S(1)} %collective-permute-done.5.refs_2_, ...), custom_call_target="tpu_custom_call" | custom-call | flops 1 | bytes 1 | tf_op jit(solution)/shard_map/theirs_block/pallas_call | solution.py:361
  33.4 0.1 collective-permute-start.6
  33.5 4.6 %mine_block.1.refs_0_ = bf16[528,128]{1,0:T(8,128)(2,1)S(1)} custom-call(s32[2,256,128]{2,1,0:T(8,128)S(1)} %limits_block.1.refs_0_.refs_1_.limit_ref, bf16[16,32,128]{2,1,0:T(8,128)(2,1)S(1)} %copy-done.4, bf16[4,2048,128]{2,1,0:T(8,128)(2,1)S(1)} %get-tuple-element.17.k_ref, bf16[4,2048,128]{2,1,0:T(8,128)(2,1)S(1)} %get-tuple-element.18.v_ref, ...), custom_call_target="tpu_custom_call" | custom-call | flops 10000000000 | bytes 1 | tf_op jit(solution)/shard_map/mine_block/pallas_call | solution.py:374
  38.1 0.9 %merge_some.1.refs_0_ = bf16[528,128]{1,0:T(8,128)(2,1)S(1)} custom-call(bf16[528,128]{1,0:T(8,128)(2,1)S(1)} %mine_block.1.refs_0_, bf16[528,128]{1,0:T(8,128)(2,1)S(1)} %collective-permute-done.6.refs_1_, bf16[528,128]{1,0:T(8,128)(2,1)S(1)} %collective-permute-done.7.refs_2_, bf16[528,128]{1,0:T(8,128)(2,1)S(1)} %collective-permute-done.8.refs_3_), custom_call_target="tpu_custom_call" | custom-call | flops 1 | bytes 1 | tf_op jit(solution)/shard_map/merge_some/pallas_call | solution.py:407
  39.0 1.1 %merge_last.1 = bf16[16,32,128]{2,1,0:T(8,128)(2,1)} custom-call(bf16[528,128]{1,0:T(8,128)(2,1)S(1)} %merge_some.1.refs_0_, bf16[528,128]{1,0:T(8,128)(2,1)S(1)} %collective-permute-done.9.refs_1_), custom_call_target="tpu_custom_call" | custom-call | flops 1 | bytes 1 | tf_op jit(solution)/shard_map/merge_last/pallas_call | solution.py:407
  (19 shorter events, 0.0 us)
Async XLA Ops:
  0.0 7.6 %copy-start.2 = (bf16[1024,4,128]{2,1,0:T(4,128)(2,1)S(1)}, bf16[1024,4,128]{2,1,0:T(4,128)(2,1)}, u32[]{:S(2)}) copy-start(bf16[1024,4,128]{2,1,0:T(4,128)(2,1)} %param.8) | copy-start | bytes 3145732
  0.0 7.6 %copy-start.3 = (bf16[1024,4,128]{2,1,0:T(4,128)(2,1)S(1)}, bf16[1024,4,128]{2,1,0:T(4,128)(2,1)}, u32[]{:S(2)}) copy-start(bf16[1024,4,128]{2,1,0:T(4,128)(2,1)} %param.9) | copy-start | bytes 3145732
  0.0 7.6 %copy-start.4 = (bf16[16,32,128]{2,1,0:T(8,128)(2,1)S(1)}, bf16[16,32,128]{2,1,0:T(8,128)(2,1)}, u32[]{:S(2)}) copy-start(bf16[16,32,128]{2,1,0:T(8,128)(2,1)} %query_ref.1) | copy-start | bytes 393220
  0.0 7.6 %collective-permute-start = (bf16[1024,4,128]{2,1,0:T(4,128)(2,1)}, bf16[1024,4,128]{2,1,0:T(4,128)(2,1)S(1)}, u32[]{:S(2)}, u32[]{:S(2)}) collective-permute-start(bf16[1024,4,128]{2,1,0:T(4,128)(2,1)} %param.8), channel_id=1, source_target_pairs={{0,1},{1,0},{2,3},{3,2},{4,5},{5,4},{6,7},{7,6},{8,9},{9,8},{10,11... | collective-permute-start | bytes 3145736 | tf_op jit(solution)/shard_map/ppermute | solution.py:50
  0.5 7.1 %collective-permute-start.1 = (bf16[1024,4,128]{2,1,0:T(4,128)(2,1)}, bf16[1024,4,128]{2,1,0:T(4,128)(2,1)S(1)}, u32[]{:S(2)}, u32[]{:S(2)}) collective-permute-start(bf16[1024,4,128]{2,1,0:T(4,128)(2,1)} %param.9), channel_id=1, source_target_pairs={{0,1},{1,0},{2,3},{3,2},{4,5},{5,4},{6,7},{7,6},{8,9},{9,8},{10,11... | collective-permute-start | bytes 3145736 | tf_op jit(solution)/shard_map/ppermute | solution.py:50
  0.6 11.4 %collective-permute-start.2 = (bf16[16,32,128]{2,1,0:T(8,128)(2,1)}, bf16[16,32,128]{2,1,0:T(8,128)(2,1)S(1)}, u32[]{:S(2)}, u32[]{:S(2)}) collective-permute-start(bf16[16,32,128]{2,1,0:T(8,128)(2,1)} %query_ref.1), channel_id=1, source_target_pairs={{0,12},{4,8},{8,4},{12,0},{1,13},{5,9},{9,5},{13,1},{2,14},{6,10},... | collective-permute-start | bytes 393224 | tf_op jit(solution)/shard_map/ppermute | solution.py:50
  5.6 12.2 %collective-permute-start.3 = (bf16[16,32,128]{2,1,0:T(8,128)(2,1)}, bf16[16,32,128]{2,1,0:T(8,128)(2,1)S(1)}, u32[]{:S(2)}, u32[]{:S(2)}) collective-permute-start(bf16[16,32,128]{2,1,0:T(8,128)(2,1)} %query_ref.1), channel_id=1, source_target_pairs={{0,4},{4,0},{8,12},{12,8},{1,5},{5,1},{9,13},{13,9},{2,6},{6,2},{1... | collective-permute-start | bytes 393224 | tf_op jit(solution)/shard_map/ppermute | solution.py:50
  5.6 0.7 %copy-start.5 = (s32[16]{0:T(128)S(1)}, s32[16]{0:T(128)}, u32[]{:S(2)}) copy-start(s32[16]{0:T(128)} %branch_ref.1) | copy-start | bytes 196
  6.3 0.7 %copy-start.6 = (s32[16]{0:T(128)S(1)}, s32[16]{0:T(128)}, u32[]{:S(2)}) copy-start(s32[16]{0:T(128)} %seen_ref.1) | copy-start | bytes 196
  12.0 9.6 %collective-permute-start.4 = (bf16[16,32,128]{2,1,0:T(8,128)(2,1)S(1)}, bf16[16,32,128]{2,1,0:T(8,128)(2,1)S(1)}, u32[]{:S(2)}, u32[]{:S(2)}) collective-permute-start(bf16[16,32,128]{2,1,0:T(8,128)(2,1)S(1)} %collective-permute-done.2.refs_2_), channel_id=1, source_target_pairs={{0,4},{4,0},{8,12},{12,8},{1,5},{5,1},{9,13},{13,9},{2,6},{6,2},{1... | collective-permute-start | bytes 393224 | tf_op jit(solution)/shard_map/ppermute | solution.py:50
  14.1 14.2 %collective-permute-start.5 = (bf16[16,32,128]{2,1,0:T(8,128)(2,1)S(1)}, bf16[16,32,128]{2,1,0:T(8,128)(2,1)S(1)}, u32[]{:S(2)}, u32[]{:S(2)}) collective-permute-start(bf16[16,32,128]{2,1,0:T(8,128)(2,1)S(1)} %copy-done.4), channel_id=1, source_target_pairs={{0,1},{1,0},{2,3},{3,2},{4,5},{5,4},{6,7},{7,6},{8,9},{9,8},{10,11... | collective-permute-start | bytes 393224 | tf_op jit(solution)/shard_map/ppermute | solution.py:50
  17.2 11.1 %copy-start = (bf16[2,1024,4,128]{3,2,1,0:T(4,128)(2,1)S(1)}, bf16[2,1024,4,128]{3,2,1,0:T(4,128)(2,1)}, u32[]{:S(2)}) copy-start(bf16[2,1024,4,128]{3,2,1,0:T(4,128)(2,1)} %param.10) | copy-start | bytes 6291460
  17.2 11.1 %copy-start.1 = (bf16[2,1024,4,128]{3,2,1,0:T(4,128)(2,1)S(1)}, bf16[2,1024,4,128]{3,2,1,0:T(4,128)(2,1)}, u32[]{:S(2)}) copy-start(bf16[2,1024,4,128]{3,2,1,0:T(4,128)(2,1)} %param.11) | copy-start | bytes 6291460
  17.2 20.8 %collective-permute-start.7 = (bf16[528,128]{1,0:T(8,128)(2,1)S(1)}, bf16[528,128]{1,0:T(8,128)(2,1)S(1)}, u32[]{:S(2)}, u32[]{:S(2)}) collective-permute-start(bf16[528,128]{1,0:T(8,128)(2,1)S(1)} %root_blocks.3.refs_0_), channel_id=1, source_target_pairs={{0,12},{4,8},{8,4},{12,0},{1,13},{5,9},{9,5},{13,1},{2,14},{6,10},... | collective-permute-start | bytes 405512 | tf_op jit(solution)/shard_map/ppermute | solution.py:50
  20.9 17.1 %collective-permute-start.8 = (bf16[528,128]{1,0:T(8,128)(2,1)S(1)}, bf16[528,128]{1,0:T(8,128)(2,1)S(1)}, u32[]{:S(2)}, u32[]{:S(2)}) collective-permute-start(bf16[528,128]{1,0:T(8,128)(2,1)S(1)} %root_blocks.4.refs_0_), channel_id=1, source_target_pairs={{0,4},{4,0},{8,12},{12,8},{1,5},{5,1},{9,13},{13,9},{2,6},{6,2},{1... | collective-permute-start | bytes 405512 | tf_op jit(solution)/shard_map/ppermute | solution.py:50
  24.9 14.1 %collective-permute-start.9 = (bf16[528,128]{1,0:T(8,128)(2,1)S(1)}, bf16[528,128]{1,0:T(8,128)(2,1)S(1)}, u32[]{:S(2)}, u32[]{:S(2)}) collective-permute-start(bf16[528,128]{1,0:T(8,128)(2,1)S(1)} %root_blocks.5.refs_0_), channel_id=1, source_target_pairs={{0,8},{4,12},{8,0},{12,4},{1,9},{5,13},{9,1},{13,5},{2,10},{6,14},... | collective-permute-start | bytes 405512 | tf_op jit(solution)/shard_map/ppermute | solution.py:50
  33.4 4.7 %collective-permute-start.6 = (bf16[528,128]{1,0:T(8,128)(2,1)S(1)}, bf16[528,128]{1,0:T(8,128)(2,1)S(1)}, u32[]{:S(2)}, u32[]{:S(2)}) collective-permute-start(bf16[528,128]{1,0:T(8,128)(2,1)S(1)} %get-tuple-element.20), channel_id=1, source_target_pairs={{0,1},{1,0},{2,3},{3,2},{4,5},{5,4},{6,7},{7,6},{8,9},{9,8},{10,11... | collective-permute-start | bytes 405512 | tf_op jit(solution)/shard_map/ppermute | solution.py:50

commit v6 on v5

--- a/solution.py
+++ b/solution.py
@@ -285,17 +285,32 @@
             )
 
 
-def limits_block(branch, seen, branches, tokens, group_size):
+def limits_block(branch, seen, branches, tokens, group_size, after):
     shape = (branches, branch.shape[0] * group_size, lane_count)
     return pl.pallas_call(
-        functools.partial(limits_kernel, tokens, group_size),
+        ordered(functools.partial(limits_kernel, tokens, group_size), after),
         out_shape=jax.ShapeDtypeStruct(shape, jnp.int32),
-        in_specs=[smem_spec()] * 2,
+        in_specs=any_specs(after) + [smem_spec()] * 2,
+        out_specs=vmem_spec(),
+        compiler_params=kernel_params(2**20),
+        cost_estimate=light_cost(),
+        name="limits_block",
+    )(*after, branch, seen)
+
+
+def mark_kernel(out_ref):
+    out_ref[...] = jnp.zeros_like(out_ref)
+
+
+def mark():
+    return pl.pallas_call(
+        mark_kernel,
+        out_shape=jax.ShapeDtypeStruct((8, lane_count), jnp.float32),
         out_specs=vmem_spec(),
         compiler_params=kernel_params(2**20),
         cost_estimate=heavy_cost(),
-        name="limits_block",
-    )(branch, seen)
+        name="mark",
+    )()
 
 
 def root_kernel(scale, count, k_ref, v_ref, *refs):
@@ -382,37 +397,51 @@
     )(limits, query, keys, values, *others)
 
 
-def merge_kernel(last, heads, requests, group_size, *refs):
-    ins, out_ref = refs[:-1], refs[-1]
+def gather_kernel(requests, group_size, *refs):
+    *ins, sums_ref, level_ref = refs
+    heads = sums_ref.shape[0]
     same = identity_mask()
     loaded = [load_packed(ref, heads, requests, group_size, same) for ref in ins]
-    outs, levels = [], []
     for h in range(heads):
         out, level = combine([(o[h], l[h]) for o, l in loaded])
-        outs.append(out)
-        levels.append(level)
-    if last:
-        for h in range(heads):
-            block = outs[h].astype(out_ref.dtype).reshape(requests, group_size, lane_count)
-            out_ref[:, h * group_size : (h + 1) * group_size, :] = block
-    else:
-        store_packed(out_ref, heads, requests, group_size, outs, levels, same)
-
-
-def merge(parts, last, heads, requests, group_size, after=()):
-    if last:
-        shape = (requests, heads * group_size, lane_count)
-    else:
-        shape = parts[0].shape
-    return pl.pallas_call(
-        ordered(functools.partial(merge_kernel, last, heads, requests, group_size), after),
-        out_shape=jax.ShapeDtypeStruct(shape, parts[0].dtype),
-        in_specs=any_specs(after) + [vmem_spec()] * len(parts),
+        sums_ref[h] = out
+        level_ref[h] = jnp.broadcast_to(level, out.shape)
+
+
+def gather_partials(parts, heads, requests, group_size):
+    shape = jax.ShapeDtypeStruct((heads, requests * group_size, lane_count), jnp.float32)
+    return pl.pallas_call(
+        functools.partial(gather_kernel, requests, group_size),
+        out_shape=(shape, shape),
+        in_specs=[vmem_spec()] * len(parts),
+        out_specs=(vmem_spec(), vmem_spec()),
+        compiler_params=kernel_params(),
+        cost_estimate=light_cost(),
+        name="gather_partials",
+    )(*parts)
+
+
+def last_kernel(requests, group_size, sums_ref, level_ref, back_ref, out_ref):
+    heads = sums_ref.shape[0]
+    outs, levels = load_packed(back_ref, heads, requests, group_size, identity_mask())
+    for h in range(heads):
+        parts = [(sums_ref[h], level_ref[h]), (outs[h], levels[h])]
+        out, _ = combine(parts)
+        block = out.astype(out_ref.dtype).reshape(requests, group_size, lane_count)
+        out_ref[:, h * group_size : (h + 1) * group_size, :] = block
+
+
+def merge_last(sums, levels, back, requests, group_size):
+    shape = (requests, sums.shape[0] * group_size, lane_count)
+    return pl.pallas_call(
+        functools.partial(last_kernel, requests, group_size),
+        out_shape=jax.ShapeDtypeStruct(shape, back.dtype),
+        in_specs=[vmem_spec()] * 3,
         out_specs=vmem_spec(),
         compiler_params=kernel_params(),
         cost_estimate=light_cost(),
-        name="merge_last" if last else "merge_some",
-    )(*after, *parts)
+        name="merge_last",
+    )(sums, levels, back)
 
 
 def local(queries, root_keys, root_values, branch_keys, branch_values, request_branch, seen_tokens):
@@ -422,8 +451,6 @@
     heads = shared // lax.axis_size("pair")
     group_size = local_heads // heads
     scale = math.log2(math.e) / math.sqrt(width)
-    branches, tokens, _, _ = branch_keys.shape
-    limits = limits_block(request_branch, seen_tokens, branches, tokens, group_size)
 
     other_keys = exchange(root_keys, "pair", 1)
     other_values = exchange(root_values, "pair", 1)
@@ -432,7 +459,7 @@
     arrived = {apart: exchange(queries, "blk", apart) for apart in direct}
 
     keys, values, own = first_block(
-        queries, root_keys, root_values, other_keys, other_values, scale, heads, (limits,)
+        queries, root_keys, root_values, other_keys, other_values, scale, heads, (mark(),)
     )
     groups = [(apart, apart ^ 1) for apart in direct if apart > 1]
     for far, near in groups:
@@ -443,14 +470,19 @@
     for apart in order:
         previous = root_blocks([arrived[apart]], keys, values, scale, previous)
         returned[apart] = exchange(previous[0], "blk", apart)
+    branches, tokens, _, _ = branch_keys.shape
+    limits = limits_block(
+        request_branch, seen_tokens, branches, tokens, group_size, previous
+    )
     theirs, held_keys, held_values = theirs_block(
         limits, other_queries, branch_keys, branch_values, scale, heads, previous
     )
     from_partner = exchange(theirs, "pair", 1)
     mine = mine_block(limits, queries, held_keys, held_values, [own], scale, heads)
     last = returned.pop(order[-1])
-    most = merge([mine, from_partner, *returned.values()], False, heads, requests, group_size)
-    return merge([most, last], True, heads, requests, group_size)
+    parts = [mine, from_partner, *returned.values()]
+    sums, levels = gather_partials(parts, heads, requests, group_size)
+    return merge_last(sums, levels, last, requests, group_size)
 
 
 def solution(mesh):

time: 40.3 us -> 39 us (0.968)
  local copies, waits for them, and re-layouts: 1.33 us -> 0.04 us
    unnamed x14, local copies, waits for them, and re-layouts: 1.33 us -> 0.04 us
    pallas_call x3 -> x4, Pallas kernels: 2.65 us -> 2.48 us  [the longest x1 0.96 us: merge_last(): pl.pallas_call(functools.partial(last_kernel, requests, group_size), out_...]
  transfers between devices with their start and end apart: 10 -> 10, of which waited for: 0 -> 1; matrix products, arithmetic and copies ran while one was open for 0% -> 0% of each run, Pallas kernels for 63% -> 65%
where the time goes in v6:
time: 39 us; the launch traced here: 38.8 us
  Pallas kernels  26.2 us (67%)
  starting transfers between devices  12.2 us (31%)
    ppermute x10, starting transfers between devices, exchange(): lax.ppermute(value, axis, [(i, i ^ apart) for i in range(lax.axis_size(ax...  12.2 us
    pallas_call x3, Pallas kernels, root_blocks(): pl.pallas_call(ordered(functools.partial(root_kernel, scale, len(queries)...  9.67 us
    pallas_call x1, Pallas kernels, theirs_block(): pl.pallas_call(ordered(functools.partial(theirs_kernel, scale, heads), af...  5.17 us
    pallas_call x1, Pallas kernels, mine_block(): pl.pallas_call(functools.partial(mine_kernel, scale, heads), out_shape=pa...  4.55 us
    pallas_call x1, Pallas kernels, first_block(): pl.pallas_call(ordered(functools.partial(first_kernel, scale, shared), af...  4.34 us
    pallas_call x1, Pallas kernels, merge_last(): pl.pallas_call(functools.partial(last_kernel, requests, group_size), out_...  0.96 us
    pallas_call x1, Pallas kernels, gather_partials(): pl.pallas_call(functools.partial(gather_kernel, requests, group_size), ou...  0.87 us
  transfers between devices with their start and end apart: 10, of which 1 were waited for; matrix products, arithmetic and copies ran while one was open for 0% of the time, Pallas kernels for 65%

profile of v6, /device:TPU:0, one launch (start us, length us, event | category | flops | bytes accessed | tf_op | source)
XLA Modules:
  0.0 38.8 jit_solution(1747524603043185161)
XLA Ops:
  0.0 0.5 %collective-permute-start = (bf16[1024,4,128]{2,1,0:T(4,128)(2,1)}, bf16[1024,4,128]{2,1,0:T(4,128)(2,1)S(1)}, u32[]{:S(2)}, u32[]{:S(2)}) collective-permute-start(bf16[1024,4,128]{2,1,0:T(4,128)(2,1)} %param.8), channel_id=1, source_target_pairs={{0,1},{1,0},{2,3},{3,2},{4,5},{5,4},{6,7},{7,6},{8,9},{9,8},{10,11... | collective-permute-start | bytes 3145736 | tf_op jit(solution)/shard_map/ppermute | solution.py:50
  0.5 0.1 collective-permute-start.1
  0.6 5.0 %collective-permute-start.2 = (bf16[16,32,128]{2,1,0:T(8,128)(2,1)}, bf16[16,32,128]{2,1,0:T(8,128)(2,1)S(1)}, u32[]{:S(2)}, u32[]{:S(2)}) collective-permute-start(bf16[16,32,128]{2,1,0:T(8,128)(2,1)} %query_ref.1), channel_id=1, source_target_pairs={{0,12},{4,8},{8,4},{12,0},{1,13},{5,9},{9,5},{13,1},{2,14},{6,10},... | collective-permute-start | bytes 393224 | tf_op jit(solution)/shard_map/ppermute | solution.py:50
  5.6 0.0 collective-permute-done
  5.6 0.0 collective-permute-done.1
  5.7 4.3 %first_block.1 = (bf16[2,2048,128]{2,1,0:T(8,128)(2,1)S(1)}, bf16[2,2048,128]{2,1,0:T(8,128)(2,1)S(1)}, bf16[528,128]{1,0:T(8,128)(2,1)S(1)}) custom-call(f32[8,128]{1,0:T(8,128)S(1)} %mark.1.refs_0_, bf16[16,32,128]{2,1,0:T(8,128)(2,1)S(1)} %copy-done.4, bf16[4096,128]{1,0:T(8,128)(2,1)S(1)} %bitcast.8, bf16[4096,128]{1,0:T(8,128)(2,1)S(1)} %bitcast.9, ...), custom_call_target="tpu_custom_call" | custom-call | flops 1 | bytes 1 | tf_op jit(solution)/shard_map/first_block/pallas_call | solution.py:263
  10.0 0.2 collective-permute-done.2.refs_2_
  10.2 1.9 %collective-permute-start.4 = (bf16[16,32,128]{2,1,0:T(8,128)(2,1)S(1)}, bf16[16,32,128]{2,1,0:T(8,128)(2,1)S(1)}, u32[]{:S(2)}, u32[]{:S(2)}) collective-permute-start(bf16[16,32,128]{2,1,0:T(8,128)(2,1)S(1)} %collective-permute-done.2.refs_2_), channel_id=1, source_target_pairs={{0,4},{4,0},{8,12},{12,8},{1,5},{5,1},{9,13},{13,9},{2,6},{6,2},{1... | collective-permute-start | bytes 393224 | tf_op jit(solution)/shard_map/ppermute | solution.py:50
  12.1 3.2 %root_blocks.3.refs_0_ = bf16[528,128]{1,0:T(8,128)(2,1)S(1)} custom-call(bf16[2,2048,128]{2,1,0:T(8,128)(2,1)S(1)} %get-tuple-element.15.refs_0_.refs_1_, bf16[2,2048,128]{2,1,0:T(8,128)(2,1)S(1)} %get-tuple-element.16.refs_1_.refs_2_, bf16[16,32,128]{2,1,0:T(8,128)(2,1)S(1)} %collective-permute-done.2.refs_2_), custom_call_target="tpu_custom_call" | custom-call | flops 1 | bytes 1 | tf_op jit(solution)/shard_map/root_blocks/pallas_call | solution.py:328
  15.3 0.0 copy-start.5
  15.3 0.0 copy-start.6
  15.3 0.0 copy-start
  15.3 0.0 copy-start.1
  15.3 2.5 %collective-permute-start.7 = (bf16[528,128]{1,0:T(8,128)(2,1)S(1)}, bf16[528,128]{1,0:T(8,128)(2,1)S(1)}, u32[]{:S(2)}, u32[]{:S(2)}) collective-permute-start(bf16[528,128]{1,0:T(8,128)(2,1)S(1)} %root_blocks.3.refs_0_), channel_id=1, source_target_pairs={{0,12},{4,8},{8,4},{12,0},{1,13},{5,9},{9,5},{13,1},{2,14},{6,10},... | collective-permute-start | bytes 405512 | tf_op jit(solution)/shard_map/ppermute | solution.py:50
  17.8 3.2 %root_blocks.4.refs_0_ = bf16[528,128]{1,0:T(8,128)(2,1)S(1)} custom-call(bf16[528,128]{1,0:T(8,128)(2,1)S(1)} %root_blocks.3.refs_0_, bf16[2,2048,128]{2,1,0:T(8,128)(2,1)S(1)} %get-tuple-element.15.refs_0_.refs_1_, bf16[2,2048,128]{2,1,0:T(8,128)(2,1)S(1)} %get-tuple-element.16.refs_1_.refs_2_, bf16[16,32,128]{2,1,0:T(8,128)(2,1)S(1)} %collective-permute-done.3.refs_3_), custom_call_target="tpu_custom_call" | custom-call | flops 1 | bytes 1 | tf_op jit(solution)/shard_map/root_blocks/pallas_call | solution.py:328
  21.0 0.7 %collective-permute-start.8 = (bf16[528,128]{1,0:T(8,128)(2,1)S(1)}, bf16[528,128]{1,0:T(8,128)(2,1)S(1)}, u32[]{:S(2)}, u32[]{:S(2)}) collective-permute-start(bf16[528,128]{1,0:T(8,128)(2,1)S(1)} %root_blocks.4.refs_0_), channel_id=1, source_target_pairs={{0,4},{4,0},{8,12},{12,8},{1,5},{5,1},{9,13},{13,9},{2,6},{6,2},{1... | collective-permute-start | bytes 405512 | tf_op jit(solution)/shard_map/ppermute | solution.py:50
  21.7 3.3 %root_blocks.5.refs_0_ = bf16[528,128]{1,0:T(8,128)(2,1)S(1)} custom-call(bf16[528,128]{1,0:T(8,128)(2,1)S(1)} %root_blocks.4.refs_0_, bf16[2,2048,128]{2,1,0:T(8,128)(2,1)S(1)} %get-tuple-element.15.refs_0_.refs_1_, bf16[2,2048,128]{2,1,0:T(8,128)(2,1)S(1)} %get-tuple-element.16.refs_1_.refs_2_, bf16[16,32,128]{2,1,0:T(8,128)(2,1)S(1)} %collective-permute-done.4.refs_3_), custom_call_target="tpu_custom_call" | custom-call | flops 1 | bytes 1 | tf_op jit(solution)/shard_map/root_blocks/pallas_call | solution.py:328
  25.1 1.4 %collective-permute-start.9 = (bf16[528,128]{1,0:T(8,128)(2,1)S(1)}, bf16[528,128]{1,0:T(8,128)(2,1)S(1)}, u32[]{:S(2)}, u32[]{:S(2)}) collective-permute-start(bf16[528,128]{1,0:T(8,128)(2,1)S(1)} %root_blocks.5.refs_0_), channel_id=1, source_target_pairs={{0,8},{4,12},{8,0},{12,4},{1,9},{5,13},{9,1},{13,5},{2,10},{6,14},... | collective-permute-start | bytes 405512 | tf_op jit(solution)/shard_map/ppermute | solution.py:50
  26.5 0.6 %limits_block.1.refs_1_.limit_ref = s32[2,256,128]{2,1,0:T(8,128)S(1)} custom-call(bf16[528,128]{1,0:T(8,128)(2,1)S(1)} %root_blocks.5.refs_0_, s32[16]{0:T(128)S(1)} %copy-done.5, s32[16]{0:T(128)S(1)} %copy-done.6), custom_call_target="tpu_custom_call" | custom-call | flops 1 | bytes 1 | tf_op jit(solution)/shard_map/limits_block/pallas_call | solution.py:290
  27.1 5.2 %theirs_block.1 = (bf16[528,128]{1,0:T(8,128)(2,1)S(1)}, bf16[4,2048,128]{2,1,0:T(8,128)(2,1)S(1)}, bf16[4,2048,128]{2,1,0:T(8,128)(2,1)S(1)}) custom-call(bf16[528,128]{1,0:T(8,128)(2,1)S(1)} %root_blocks.5.refs_0_, s32[2,256,128]{2,1,0:T(8,128)S(1)} %limits_block.1.refs_1_.limit_ref, bf16[16,32,128]{2,1,0:T(8,128)(2,1)S(1)} %collective-permute-done.5.refs_2_, ...), custom_call_target="tpu_custom_call" | custom-call | flops 1 | bytes 1 | tf_op jit(solution)/shard_map/theirs_block/pallas_call | solution.py:376
  32.3 0.1 collective-permute-start.6
  32.4 4.5 %mine_block.1.refs_0_ = bf16[528,128]{1,0:T(8,128)(2,1)S(1)} custom-call(s32[2,256,128]{2,1,0:T(8,128)S(1)} %limits_block.1.refs_1_.limit_ref, bf16[16,32,128]{2,1,0:T(8,128)(2,1)S(1)} %copy-done.4, bf16[4,2048,128]{2,1,0:T(8,128)(2,1)S(1)} %get-tuple-element.19.k_ref, bf16[4,2048,128]{2,1,0:T(8,128)(2,1)S(1)} %get-tuple-element.20.v_ref, ...), custom_call_target="tpu_custom_call" | custom-call | flops 10000000000 | bytes 1 | tf_op jit(solution)/shard_map/mine_block/pallas_call | solution.py:389
  37.0 0.9 %gather_partials.1 = (f32[2,256,128]{2,1,0:T(8,128)S(1)}, f32[2,256,128]{2,1,0:T(8,128)S(1)}) custom-call(bf16[528,128]{1,0:T(8,128)(2,1)S(1)} %mine_block.1.refs_0_, bf16[528,128]{1,0:T(8,128)(2,1)S(1)} %collective-permute-done.6.refs_1_, bf16[528,128]{1,0:T(8,128)(2,1)S(1)} %collective-permute-done.7.refs_2_, ...), custom_call_target="tpu_custom_call" | custom-call | flops 1 | bytes 1 | tf_op jit(solution)/shard_map/gather_partials/pallas_call | solution.py:413
  37.9 1.0 %merge_last.1 = bf16[16,32,128]{2,1,0:T(8,128)(2,1)} custom-call(f32[2,256,128]{2,1,0:T(8,128)S(1)} %get-tuple-element.23.sums_ref, f32[2,256,128]{2,1,0:T(8,128)S(1)} %get-tuple-element.24.level_ref, bf16[528,128]{1,0:T(8,128)(2,1)S(1)} %collective-permute-done.9.back_ref), custom_call_target="tpu_custom_call" | custom-call | flops 1 | bytes 1 | tf_op jit(solution)/shard_map/merge_last/pallas_call | solution.py:436
  (20 shorter events, 0.0 us)
Async XLA Ops:
  0.0 5.7 %copy-start.2 = (bf16[1024,4,128]{2,1,0:T(4,128)(2,1)S(1)}, bf16[1024,4,128]{2,1,0:T(4,128)(2,1)}, u32[]{:S(2)}) copy-start(bf16[1024,4,128]{2,1,0:T(4,128)(2,1)} %param.8) | copy-start | bytes 3145732
  0.0 5.7 %copy-start.3 = (bf16[1024,4,128]{2,1,0:T(4,128)(2,1)S(1)}, bf16[1024,4,128]{2,1,0:T(4,128)(2,1)}, u32[]{:S(2)}) copy-start(bf16[1024,4,128]{2,1,0:T(4,128)(2,1)} %param.9) | copy-start | bytes 3145732
  0.0 5.7 %copy-start.4 = (bf16[16,32,128]{2,1,0:T(8,128)(2,1)S(1)}, bf16[16,32,128]{2,1,0:T(8,128)(2,1)}, u32[]{:S(2)}) copy-start(bf16[16,32,128]{2,1,0:T(8,128)(2,1)} %query_ref.1) | copy-start | bytes 393220
  0.0 5.6 %collective-permute-start = (bf16[1024,4,128]{2,1,0:T(4,128)(2,1)}, bf16[1024,4,128]{2,1,0:T(4,128)(2,1)S(1)}, u32[]{:S(2)}, u32[]{:S(2)}) collective-permute-start(bf16[1024,4,128]{2,1,0:T(4,128)(2,1)} %param.8), channel_id=1, source_target_pairs={{0,1},{1,0},{2,3},{3,2},{4,5},{5,4},{6,7},{7,6},{8,9},{9,8},{10,11... | collective-permute-start | bytes 3145736 | tf_op jit(solution)/shard_map/ppermute | solution.py:50
  0.5 5.1 %collective-permute-start.1 = (bf16[1024,4,128]{2,1,0:T(4,128)(2,1)}, bf16[1024,4,128]{2,1,0:T(4,128)(2,1)S(1)}, u32[]{:S(2)}, u32[]{:S(2)}) collective-permute-start(bf16[1024,4,128]{2,1,0:T(4,128)(2,1)} %param.9), channel_id=1, source_target_pairs={{0,1},{1,0},{2,3},{3,2},{4,5},{5,4},{6,7},{7,6},{8,9},{9,8},{10,11... | collective-permute-start | bytes 3145736 | tf_op jit(solution)/shard_map/ppermute | solution.py:50
  0.6 9.6 %collective-permute-start.2 = (bf16[16,32,128]{2,1,0:T(8,128)(2,1)}, bf16[16,32,128]{2,1,0:T(8,128)(2,1)S(1)}, u32[]{:S(2)}, u32[]{:S(2)}) collective-permute-start(bf16[16,32,128]{2,1,0:T(8,128)(2,1)} %query_ref.1), channel_id=1, source_target_pairs={{0,12},{4,8},{8,4},{12,0},{1,13},{5,9},{9,5},{13,1},{2,14},{6,10},... | collective-permute-start | bytes 393224 | tf_op jit(solution)/shard_map/ppermute | solution.py:50
  5.6 12.2 %collective-permute-start.3 = (bf16[16,32,128]{2,1,0:T(8,128)(2,1)}, bf16[16,32,128]{2,1,0:T(8,128)(2,1)S(1)}, u32[]{:S(2)}, u32[]{:S(2)}) collective-permute-start(bf16[16,32,128]{2,1,0:T(8,128)(2,1)} %query_ref.1), channel_id=1, source_target_pairs={{0,4},{4,0},{8,12},{12,8},{1,5},{5,1},{9,13},{13,9},{2,6},{6,2},{1... | collective-permute-start | bytes 393224 | tf_op jit(solution)/shard_map/ppermute | solution.py:50
  10.2 11.5 %collective-permute-start.4 = (bf16[16,32,128]{2,1,0:T(8,128)(2,1)S(1)}, bf16[16,32,128]{2,1,0:T(8,128)(2,1)S(1)}, u32[]{:S(2)}, u32[]{:S(2)}) collective-permute-start(bf16[16,32,128]{2,1,0:T(8,128)(2,1)S(1)} %collective-permute-done.2.refs_2_), channel_id=1, source_target_pairs={{0,4},{4,0},{8,12},{12,8},{1,5},{5,1},{9,13},{13,9},{2,6},{6,2},{1... | collective-permute-start | bytes 393224 | tf_op jit(solution)/shard_map/ppermute | solution.py:50
  12.1 15.0 %collective-permute-start.5 = (bf16[16,32,128]{2,1,0:T(8,128)(2,1)S(1)}, bf16[16,32,128]{2,1,0:T(8,128)(2,1)S(1)}, u32[]{:S(2)}, u32[]{:S(2)}) collective-permute-start(bf16[16,32,128]{2,1,0:T(8,128)(2,1)S(1)} %copy-done.4), channel_id=1, source_target_pairs={{0,1},{1,0},{2,3},{3,2},{4,5},{5,4},{6,7},{7,6},{8,9},{9,8},{10,11... | collective-permute-start | bytes 393224 | tf_op jit(solution)/shard_map/ppermute | solution.py:50
  15.3 11.2 %copy-start.5 = (s32[16]{0:T(128)S(1)}, s32[16]{0:T(128)}, u32[]{:S(2)}) copy-start(s32[16]{0:T(128)} %refs_1_.3) | copy-start | bytes 196
  15.3 11.2 %copy-start.6 = (s32[16]{0:T(128)S(1)}, s32[16]{0:T(128)}, u32[]{:S(2)}) copy-start(s32[16]{0:T(128)} %refs_2_.1) | copy-start | bytes 196
  15.3 11.8 %copy-start = (bf16[2,1024,4,128]{3,2,1,0:T(4,128)(2,1)S(1)}, bf16[2,1024,4,128]{3,2,1,0:T(4,128)(2,1)}, u32[]{:S(2)}) copy-start(bf16[2,1024,4,128]{3,2,1,0:T(4,128)(2,1)} %param.10) | copy-start | bytes 6291460
  15.3 11.8 %copy-start.1 = (bf16[2,1024,4,128]{3,2,1,0:T(4,128)(2,1)S(1)}, bf16[2,1024,4,128]{3,2,1,0:T(4,128)(2,1)}, u32[]{:S(2)}) copy-start(bf16[2,1024,4,128]{3,2,1,0:T(4,128)(2,1)} %param.11) | copy-start | bytes 6291460
  15.3 21.6 %collective-permute-start.7 = (bf16[528,128]{1,0:T(8,128)(2,1)S(1)}, bf16[528,128]{1,0:T(8,128)(2,1)S(1)}, u32[]{:S(2)}, u32[]{:S(2)}) collective-permute-start(bf16[528,128]{1,0:T(8,128)(2,1)S(1)} %root_blocks.3.refs_0_), channel_id=1, source_target_pairs={{0,12},{4,8},{8,4},{12,0},{1,13},{5,9},{9,5},{13,1},{2,14},{6,10},... | collective-permute-start | bytes 405512 | tf_op jit(solution)/shard_map/ppermute | solution.py:50
  21.0 15.9 %collective-permute-start.8 = (bf16[528,128]{1,0:T(8,128)(2,1)S(1)}, bf16[528,128]{1,0:T(8,128)(2,1)S(1)}, u32[]{:S(2)}, u32[]{:S(2)}) collective-permute-start(bf16[528,128]{1,0:T(8,128)(2,1)S(1)} %root_blocks.4.refs_0_), channel_id=1, source_target_pairs={{0,4},{4,0},{8,12},{12,8},{1,5},{5,1},{9,13},{13,9},{2,6},{6,2},{1... | collective-permute-start | bytes 405512 | tf_op jit(solution)/shard_map/ppermute | solution.py:50
  25.1 12.8 %collective-permute-start.9 = (bf16[528,128]{1,0:T(8,128)(2,1)S(1)}, bf16[528,128]{1,0:T(8,128)(2,1)S(1)}, u32[]{:S(2)}, u32[]{:S(2)}) collective-permute-start(bf16[528,128]{1,0:T(8,128)(2,1)S(1)} %root_blocks.5.refs_0_), channel_id=1, source_target_pairs={{0,8},{4,12},{8,0},{12,4},{1,9},{5,13},{9,1},{13,5},{2,10},{6,14},... | collective-permute-start | bytes 405512 | tf_op jit(solution)/shard_map/ppermute | solution.py:50
  32.3 4.7 %collective-permute-start.6 = (bf16[528,128]{1,0:T(8,128)(2,1)S(1)}, bf16[528,128]{1,0:T(8,128)(2,1)S(1)}, u32[]{:S(2)}, u32[]{:S(2)}) collective-permute-start(bf16[528,128]{1,0:T(8,128)(2,1)S(1)} %get-tuple-element.22), channel_id=1, source_target_pairs={{0,1},{1,0},{2,3},{3,2},{4,5},{5,4},{6,7},{7,6},{8,9},{9,8},{10,11... | collective-permute-start | bytes 405512 | tf_op jit(solution)/shard_map/ppermute | solution.py:50

commit v7 on v6

--- a/solution.py
+++ b/solution.py
@@ -324,6 +324,27 @@
     write_partials(jobs, scale, heads, requests, group_size)
 
 
+def head_kernel(scale, head, k_ref, v_ref, query_ref, out_ref):
+    requests, local_heads, _ = query_ref.shape
+    group_size = local_heads // k_ref.shape[0]
+    pieces = root_pieces(query_ref, k_ref, v_ref, group_size)
+    write_partials([(out_ref, lambda _: pieces(head))], scale, 1, requests, group_size)
+
+
+def head_block(head, query, keys, values, scale, after):
+    requests, local_heads, width = query.shape
+    rows = requests * local_heads // keys.shape[0]
+    return pl.pallas_call(
+        ordered(functools.partial(head_kernel, scale, head), after),
+        out_shape=jax.ShapeDtypeStruct((rows + stat_rows(rows), width), query.dtype),
+        in_specs=any_specs(after) + [vmem_spec()] * 3,
+        out_specs=vmem_spec(),
+        compiler_params=kernel_params(),
+        cost_estimate=light_cost(),
+        name="head_block",
+    )(*after, keys, values, query)
+
+
 def root_blocks(queries, keys, values, scale, after):
     return pl.pallas_call(
         ordered(functools.partial(root_kernel, scale, len(queries)), after),
@@ -385,40 +406,43 @@
     )(*after, limits, query, flat(keys), flat(values))
 
 
-def mine_block(limits, query, keys, values, others, scale, heads):
-    return pl.pallas_call(
-        functools.partial(mine_kernel, scale, heads),
+def mine_block(limits, query, keys, values, others, scale, heads, after):
+    return pl.pallas_call(
+        ordered(functools.partial(mine_kernel, scale, heads), after),
         out_shape=packed_shape(query),
-        in_specs=[vmem_spec()] * (4 + len(others)),
+        in_specs=any_specs(after) + [vmem_spec()] * (4 + len(others)),
         out_specs=vmem_spec(),
         compiler_params=kernel_params(),
         cost_estimate=heavy_cost(),
         name="mine_block",
-    )(limits, query, keys, values, *others)
-
-
-def gather_kernel(requests, group_size, *refs):
+    )(*after, limits, query, keys, values, *others)
+
+
+def gather_kernel(requests, group_size, whole, *refs):
     *ins, sums_ref, level_ref = refs
     heads = sums_ref.shape[0]
     same = identity_mask()
-    loaded = [load_packed(ref, heads, requests, group_size, same) for ref in ins]
+    loaded = [load_packed(ref, heads, requests, group_size, same) for ref in ins[:whole]]
+    for at in range(whole, len(ins), heads):
+        ones = [load_packed(ref, 1, requests, group_size, same) for ref in ins[at : at + heads]]
+        loaded.append(([o[0] for o, _ in ones], [l[0] for _, l in ones]))
     for h in range(heads):
         out, level = combine([(o[h], l[h]) for o, l in loaded])
         sums_ref[h] = out
         level_ref[h] = jnp.broadcast_to(level, out.shape)
 
 
-def gather_partials(parts, heads, requests, group_size):
+def gather_partials(parts, halves, heads, requests, group_size):
     shape = jax.ShapeDtypeStruct((heads, requests * group_size, lane_count), jnp.float32)
     return pl.pallas_call(
-        functools.partial(gather_kernel, requests, group_size),
+        functools.partial(gather_kernel, requests, group_size, len(parts)),
         out_shape=(shape, shape),
-        in_specs=[vmem_spec()] * len(parts),
+        in_specs=[vmem_spec()] * (len(parts) + len(halves)),
         out_specs=(vmem_spec(), vmem_spec()),
         compiler_params=kernel_params(),
         cost_estimate=light_cost(),
         name="gather_partials",
-    )(*parts)
+    )(*parts, *halves)
 
 
 def last_kernel(requests, group_size, sums_ref, level_ref, back_ref, out_ref):
@@ -466,8 +490,13 @@
         arrived[far], own = lax.optimization_barrier((arrived[far], own))
         arrived[near] = exchange(arrived[far], "blk", 1)
     order = sorted(arrived, key=lambda apart: (apart % 2 == 0, -apart))
-    returned, previous = {}, ()
+    returned, halves, previous = {}, [], ()
     for apart in order:
+        if apart > 2 and apart % 2:
+            for head in range(heads):
+                previous = (head_block(head, arrived[apart], keys, values, scale, previous),)
+                halves.append(exchange(previous[0], "blk", apart))
+            continue
         previous = root_blocks([arrived[apart]], keys, values, scale, previous)
         returned[apart] = exchange(previous[0], "blk", apart)
     branches, tokens, _, _ = branch_keys.shape
@@ -478,10 +507,10 @@
         limits, other_queries, branch_keys, branch_values, scale, heads, previous
     )
     from_partner = exchange(theirs, "pair", 1)
-    mine = mine_block(limits, queries, held_keys, held_values, [own], scale, heads)
+    mine = mine_block(limits, queries, held_keys, held_values, [own], scale, heads, halves[:1])
     last = returned.pop(order[-1])
     parts = [mine, from_partner, *returned.values()]
-    sums, levels = gather_partials(parts, heads, requests, group_size)
+    sums, levels = gather_partials(parts, halves, heads, requests, group_size)
     return merge_last(sums, levels, last, requests, group_size)
 
 

time: 39 us -> 41.8 us (1.072)
  starting transfers between devices: 12.2 us -> 14.7 us
    pallas_call x2 -> x4, Pallas kernels: 5.41 us -> 9.01 us  [the longest x1 4.48 us: mine_block(): pl.pallas_call(ordered(functools.partial(mine_kernel, scale, heads), afte...]
    pallas_call x3 -> x2, Pallas kernels: 9.67 us -> 6.5 us  [root_blocks(): pl.pallas_call(ordered(functools.partial(root_kernel, scale, len(queries)...]
    ppermute x10 -> x11, starting transfers between devices: 12.2 us -> 14.7 us  [exchange(): lax.ppermute(value, axis, [(i, i ^ apart) for i in range(lax.axis_size(ax...]
  transfers between devices with their start and end apart: 10 -> 11, of which waited for: 1 -> 1; matrix products, arithmetic and copies ran while one was open for 0% -> 0% of each run, Pallas kernels for 65% -> 61%
where the time goes in v7:
time: 41.8 us; the launch traced here: 41.7 us
  Pallas kernels  26.5 us (63%)
  starting transfers between devices  14.7 us (35%)
    ppermute x11, starting transfers between devices, exchange(): lax.ppermute(value, axis, [(i, i ^ apart) for i in range(lax.axis_size(ax...  14.7 us
    pallas_call x2, Pallas kernels, root_blocks(): pl.pallas_call(ordered(functools.partial(root_kernel, scale, len(queries)...  6.5 us
    pallas_call x1, Pallas kernels, theirs_block(): pl.pallas_call(ordered(functools.partial(theirs_kernel, scale, heads), af...  5.08 us
    pallas_call x1, Pallas kernels, mine_block(): pl.pallas_call(ordered(functools.partial(mine_kernel, scale, heads), afte...  4.48 us
    pallas_call x1, Pallas kernels, first_block(): pl.pallas_call(ordered(functools.partial(first_kernel, scale, shared), af...  4.33 us
    pallas_call x2, Pallas kernels, head_block(): pl.pallas_call(ordered(functools.partial(head_kernel, scale, head), after...  3.67 us
    pallas_call x1, Pallas kernels, merge_last(): pl.pallas_call(functools.partial(last_kernel, requests, group_size), out_...  0.95 us
    pallas_call x1, Pallas kernels, gather_partials(): pl.pallas_call(functools.partial(gather_kernel, requests, group_size, len...  0.86 us
  transfers between devices with their start and end apart: 11, of which 1 were waited for; matrix products, arithmetic and copies ran while one was open for 0% of the time, Pallas kernels for 61%

profile of v7, /device:TPU:0, one launch (start us, length us, event | category | flops | bytes accessed | tf_op | source)
XLA Modules:
  0.0 41.7 jit_solution(17282505391999233704)
XLA Ops:
  0.0 0.5 %collective-permute-start = (bf16[1024,4,128]{2,1,0:T(4,128)(2,1)}, bf16[1024,4,128]{2,1,0:T(4,128)(2,1)S(1)}, u32[]{:S(2)}, u32[]{:S(2)}) collective-permute-start(bf16[1024,4,128]{2,1,0:T(4,128)(2,1)} %param.8), channel_id=1, source_target_pairs={{0,1},{1,0},{2,3},{3,2},{4,5},{5,4},{6,7},{7,6},{8,9},{9,8},{10,11... | collective-permute-start | bytes 3145736 | tf_op jit(solution)/shard_map/ppermute | solution.py:50
  0.5 0.1 collective-permute-start.1
  0.6 5.0 %collective-permute-start.2 = (bf16[16,32,128]{2,1,0:T(8,128)(2,1)}, bf16[16,32,128]{2,1,0:T(8,128)(2,1)S(1)}, u32[]{:S(2)}, u32[]{:S(2)}) collective-permute-start(bf16[16,32,128]{2,1,0:T(8,128)(2,1)} %refs_2_.3), channel_id=1, source_target_pairs={{0,12},{4,8},{8,4},{12,0},{1,13},{5,9},{9,5},{13,1},{2,14},{6,10},... | collective-permute-start | bytes 393224 | tf_op jit(solution)/shard_map/ppermute | solution.py:50
  5.7 4.3 %first_block.1 = (bf16[2,2048,128]{2,1,0:T(8,128)(2,1)S(1)}, bf16[2,2048,128]{2,1,0:T(8,128)(2,1)S(1)}, bf16[528,128]{1,0:T(8,128)(2,1)S(1)}) custom-call(f32[8,128]{1,0:T(8,128)S(1)} %mark.1.refs_0_, bf16[16,32,128]{2,1,0:T(8,128)(2,1)S(1)} %copy-done.4, bf16[4096,128]{1,0:T(8,128)(2,1)S(1)} %bitcast.8, bf16[4096,128]{1,0:T(8,128)(2,1)S(1)} %bitcast.9, ...), custom_call_target="tpu_custom_call" | custom-call | flops 1 | bytes 1 | tf_op jit(solution)/shard_map/first_block/pallas_call | solution.py:263
  10.0 0.2 collective-permute-done.2.refs_2_.refs_3_
  10.2 1.9 %collective-permute-start.5 = (bf16[16,32,128]{2,1,0:T(8,128)(2,1)S(1)}, bf16[16,32,128]{2,1,0:T(8,128)(2,1)S(1)}, u32[]{:S(2)}, u32[]{:S(2)}) collective-permute-start(bf16[16,32,128]{2,1,0:T(8,128)(2,1)S(1)} %collective-permute-done.2.refs_2_.refs_3_), channel_id=1, source_target_pairs={{0,4},{4,0},{8,12},{12,8},{1,5},{5,1},{9,13},{13,9},{2,6},{6,2},{1... | collective-permute-start | bytes 393224 | tf_op jit(solution)/shard_map/ppermute | solution.py:50
  12.1 1.8 %head_block.2.refs_0_ = bf16[272,128]{1,0:T(8,128)(2,1)S(1)} custom-call(bf16[2,2048,128]{2,1,0:T(8,128)(2,1)S(1)} %get-tuple-element.15.refs_0_.refs_1_, bf16[2,2048,128]{2,1,0:T(8,128)(2,1)S(1)} %get-tuple-element.16.refs_1_.refs_2_, bf16[16,32,128]{2,1,0:T(8,128)(2,1)S(1)} %collective-permute-done.2.refs_2_.refs_3_), custom_call_target="tpu_custom_call" | custom-call | flops 1 | bytes 1 | tf_op jit(solution)/shard_map/head_block/pallas_call | solution.py:337
  14.0 2.5 %collective-permute-start.3 = (bf16[272,128]{1,0:T(8,128)(2,1)S(1)}, bf16[272,128]{1,0:T(8,128)(2,1)S(1)}, u32[]{:S(2)}, u32[]{:S(2)}) collective-permute-start(bf16[272,128]{1,0:T(8,128)(2,1)S(1)} %head_block.2.refs_0_), channel_id=1, source_target_pairs={{0,12},{4,8},{8,4},{12,0},{1,13},{5,9},{9,5},{13,1},{2,14},{6,10},... | collective-permute-start | bytes 208904 | tf_op jit(solution)/shard_map/ppermute | solution.py:50
  16.5 1.8 %head_block.3.refs_0_ = bf16[272,128]{1,0:T(8,128)(2,1)S(1)} custom-call(bf16[272,128]{1,0:T(8,128)(2,1)S(1)} %head_block.2.refs_0_, bf16[2,2048,128]{2,1,0:T(8,128)(2,1)S(1)} %get-tuple-element.15.refs_0_.refs_1_, bf16[2,2048,128]{2,1,0:T(8,128)(2,1)S(1)} %get-tuple-element.16.refs_1_.refs_2_, bf16[16,32,128]{2,1,0:T(8,128)(2,1)S(1)} %collective-permute-done.2.refs_2_.refs_3_), custom_call_target="tpu_custom_call" | custom-call | flops 1 | bytes 1 | tf_op jit(solution)/shard_map/head_block/pallas_call | solution.py:337
  18.3 0.0 copy-start.5
  18.3 0.0 copy-start.6
  18.3 0.0 copy-start
  18.3 0.0 copy-start.1
  18.4 1.4 %collective-permute-start.9 = (bf16[272,128]{1,0:T(8,128)(2,1)S(1)}, bf16[272,128]{1,0:T(8,128)(2,1)S(1)}, u32[]{:S(2)}, u32[]{:S(2)}) collective-permute-start(bf16[272,128]{1,0:T(8,128)(2,1)S(1)} %head_block.3.refs_0_), channel_id=1, source_target_pairs={{0,12},{4,8},{8,4},{12,0},{1,13},{5,9},{9,5},{13,1},{2,14},{6,10},... | collective-permute-start | bytes 208904 | tf_op jit(solution)/shard_map/ppermute | solution.py:50
  19.8 3.2 %root_blocks.2.refs_0_ = bf16[528,128]{1,0:T(8,128)(2,1)S(1)} custom-call(bf16[272,128]{1,0:T(8,128)(2,1)S(1)} %head_block.3.refs_0_, bf16[2,2048,128]{2,1,0:T(8,128)(2,1)S(1)} %get-tuple-element.15.refs_0_.refs_1_, bf16[2,2048,128]{2,1,0:T(8,128)(2,1)S(1)} %get-tuple-element.16.refs_1_.refs_2_, bf16[16,32,128]{2,1,0:T(8,128)(2,1)S(1)} %collective-permute-done.4.refs_3_), custom_call_target="tpu_custom_call" | custom-call | flops 1 | bytes 1 | tf_op jit(solution)/shard_map/root_blocks/pallas_call | solution.py:349
  23.0 0.1 collective-permute-start.8
  23.1 3.3 %root_blocks.3.refs_0_ = bf16[528,128]{1,0:T(8,128)(2,1)S(1)} custom-call(bf16[528,128]{1,0:T(8,128)(2,1)S(1)} %root_blocks.2.refs_0_, bf16[2,2048,128]{2,1,0:T(8,128)(2,1)S(1)} %get-tuple-element.15.refs_0_.refs_1_, bf16[2,2048,128]{2,1,0:T(8,128)(2,1)S(1)} %get-tuple-element.16.refs_1_.refs_2_, bf16[16,32,128]{2,1,0:T(8,128)(2,1)S(1)} %collective-permute-done.5.refs_3_), custom_call_target="tpu_custom_call" | custom-call | flops 1 | bytes 1 | tf_op jit(solution)/shard_map/root_blocks/pallas_call | solution.py:349
  26.4 3.1 %collective-permute-start.10 = (bf16[528,128]{1,0:T(8,128)(2,1)S(1)}, bf16[528,128]{1,0:T(8,128)(2,1)S(1)}, u32[]{:S(2)}, u32[]{:S(2)}) collective-permute-start(bf16[528,128]{1,0:T(8,128)(2,1)S(1)} %root_blocks.3.refs_0_), channel_id=1, source_target_pairs={{0,8},{4,12},{8,0},{12,4},{1,9},{5,13},{9,1},{13,5},{2,10},{6,14},... | collective-permute-start | bytes 405512 | tf_op jit(solution)/shard_map/ppermute | solution.py:50
  29.5 0.6 %limits_block.1.refs_1_ = s32[2,256,128]{2,1,0:T(8,128)S(1)} custom-call(bf16[528,128]{1,0:T(8,128)(2,1)S(1)} %root_blocks.3.refs_0_, s32[16]{0:T(128)S(1)} %copy-done.5, s32[16]{0:T(128)S(1)} %copy-done.6), custom_call_target="tpu_custom_call" | custom-call | flops 1 | bytes 1 | tf_op jit(solution)/shard_map/limits_block/pallas_call | solution.py:290
  30.2 5.1 %theirs_block.1 = (bf16[528,128]{1,0:T(8,128)(2,1)S(1)}, bf16[4,2048,128]{2,1,0:T(8,128)(2,1)S(1)}, bf16[4,2048,128]{2,1,0:T(8,128)(2,1)S(1)}) custom-call(bf16[528,128]{1,0:T(8,128)(2,1)S(1)} %root_blocks.3.refs_0_, s32[2,256,128]{2,1,0:T(8,128)S(1)} %limits_block.1.refs_1_, bf16[16,32,128]{2,1,0:T(8,128)(2,1)S(1)} %collective-permute-done.6.refs_2_, ...), custom_call_target="tpu_custom_call" | custom-call | flops 1 | bytes 1 | tf_op jit(solution)/shard_map/theirs_block/pallas_call | solution.py:397
  35.2 0.1 collective-permute-start.7
  35.3 4.5 %mine_block.1.refs_0_ = bf16[528,128]{1,0:T(8,128)(2,1)S(1)} custom-call(bf16[272,128]{1,0:T(8,128)(2,1)S(1)} %collective-permute-done.3.refs_0_.refs_3_, s32[2,256,128]{2,1,0:T(8,128)S(1)} %limits_block.1.refs_1_, bf16[16,32,128]{2,1,0:T(8,128)(2,1)S(1)} %copy-done.4, bf16[4,2048,128]{2,1,0:T(8,128)(2,1)S(1)} %get-tuple-element.19.refs_3_, ...), custom_call_target="tpu_custom_call" | custom-call | flops 10000000000 | bytes 1 | tf_op jit(solution)/shard_map/mine_block/pallas_call | solution.py:410
  39.8 0.9 %gather_partials.1 = (f32[2,256,128]{2,1,0:T(8,128)S(1)}, f32[2,256,128]{2,1,0:T(8,128)S(1)}) custom-call(bf16[528,128]{1,0:T(8,128)(2,1)S(1)} %mine_block.1.refs_0_, bf16[528,128]{1,0:T(8,128)(2,1)S(1)} %collective-permute-done.7.refs_1_, bf16[528,128]{1,0:T(8,128)(2,1)S(1)} %collective-permute-done.8.refs_2_, ...), custom_call_target="tpu_custom_call" | custom-call | flops 1 | bytes 1 | tf_op jit(solution)/shard_map/gather_partials/pallas_call | solution.py:437
  40.7 1.0 %merge_last.1 = bf16[16,32,128]{2,1,0:T(8,128)(2,1)} custom-call(f32[2,256,128]{2,1,0:T(8,128)S(1)} %get-tuple-element.23.sums_ref, f32[2,256,128]{2,1,0:T(8,128)S(1)} %get-tuple-element.24.level_ref, bf16[528,128]{1,0:T(8,128)(2,1)S(1)} %collective-permute-done.10.back_ref), custom_call_target="tpu_custom_call" | custom-call | flops 1 | bytes 1 | tf_op jit(solution)/shard_map/merge_last/pallas_call | solution.py:460
  (23 shorter events, 0.1 us)
Async XLA Ops:
  0.0 5.7 %copy-start.2 = (bf16[1024,4,128]{2,1,0:T(4,128)(2,1)S(1)}, bf16[1024,4,128]{2,1,0:T(4,128)(2,1)}, u32[]{:S(2)}) copy-start(bf16[1024,4,128]{2,1,0:T(4,128)(2,1)} %param.8) | copy-start | bytes 3145732
  0.0 5.7 %copy-start.3 = (bf16[1024,4,128]{2,1,0:T(4,128)(2,1)S(1)}, bf16[1024,4,128]{2,1,0:T(4,128)(2,1)}, u32[]{:S(2)}) copy-start(bf16[1024,4,128]{2,1,0:T(4,128)(2,1)} %param.9) | copy-start | bytes 3145732
  0.0 5.7 %copy-start.4 = (bf16[16,32,128]{2,1,0:T(8,128)(2,1)S(1)}, bf16[16,32,128]{2,1,0:T(8,128)(2,1)}, u32[]{:S(2)}) copy-start(bf16[16,32,128]{2,1,0:T(8,128)(2,1)} %refs_2_.3) | copy-start | bytes 393220
  0.0 5.6 %collective-permute-start = (bf16[1024,4,128]{2,1,0:T(4,128)(2,1)}, bf16[1024,4,128]{2,1,0:T(4,128)(2,1)S(1)}, u32[]{:S(2)}, u32[]{:S(2)}) collective-permute-start(bf16[1024,4,128]{2,1,0:T(4,128)(2,1)} %param.8), channel_id=1, source_target_pairs={{0,1},{1,0},{2,3},{3,2},{4,5},{5,4},{6,7},{7,6},{8,9},{9,8},{10,11... | collective-permute-start | bytes 3145736 | tf_op jit(solution)/shard_map/ppermute | solution.py:50
  0.5 5.1 %collective-permute-start.1 = (bf16[1024,4,128]{2,1,0:T(4,128)(2,1)}, bf16[1024,4,128]{2,1,0:T(4,128)(2,1)S(1)}, u32[]{:S(2)}, u32[]{:S(2)}) collective-permute-start(bf16[1024,4,128]{2,1,0:T(4,128)(2,1)} %param.9), channel_id=1, source_target_pairs={{0,1},{1,0},{2,3},{3,2},{4,5},{5,4},{6,7},{7,6},{8,9},{9,8},{10,11... | collective-permute-start | bytes 3145736 | tf_op jit(solution)/shard_map/ppermute | solution.py:50
  0.6 9.6 %collective-permute-start.2 = (bf16[16,32,128]{2,1,0:T(8,128)(2,1)}, bf16[16,32,128]{2,1,0:T(8,128)(2,1)S(1)}, u32[]{:S(2)}, u32[]{:S(2)}) collective-permute-start(bf16[16,32,128]{2,1,0:T(8,128)(2,1)} %refs_2_.3), channel_id=1, source_target_pairs={{0,12},{4,8},{8,4},{12,0},{1,13},{5,9},{9,5},{13,1},{2,14},{6,10},... | collective-permute-start | bytes 393224 | tf_op jit(solution)/shard_map/ppermute | solution.py:50
  5.6 14.2 %collective-permute-start.4 = (bf16[16,32,128]{2,1,0:T(8,128)(2,1)}, bf16[16,32,128]{2,1,0:T(8,128)(2,1)S(1)}, u32[]{:S(2)}, u32[]{:S(2)}) collective-permute-start(bf16[16,32,128]{2,1,0:T(8,128)(2,1)} %refs_2_.3), channel_id=1, source_target_pairs={{0,4},{4,0},{8,12},{12,8},{1,5},{5,1},{9,13},{13,9},{2,6},{6,2},{1... | collective-permute-start | bytes 393224 | tf_op jit(solution)/shard_map/ppermute | solution.py:50
  10.2 12.9 %collective-permute-start.5 = (bf16[16,32,128]{2,1,0:T(8,128)(2,1)S(1)}, bf16[16,32,128]{2,1,0:T(8,128)(2,1)S(1)}, u32[]{:S(2)}, u32[]{:S(2)}) collective-permute-start(bf16[16,32,128]{2,1,0:T(8,128)(2,1)S(1)} %collective-permute-done.2.refs_2_.refs_3_), channel_id=1, source_target_pairs={{0,4},{4,0},{8,12},{12,8},{1,5},{5,1},{9,13},{13,9},{2,6},{6,2},{1... | collective-permute-start | bytes 393224 | tf_op jit(solution)/shard_map/ppermute | solution.py:50
  12.1 18.0 %collective-permute-start.6 = (bf16[16,32,128]{2,1,0:T(8,128)(2,1)S(1)}, bf16[16,32,128]{2,1,0:T(8,128)(2,1)S(1)}, u32[]{:S(2)}, u32[]{:S(2)}) collective-permute-start(bf16[16,32,128]{2,1,0:T(8,128)(2,1)S(1)} %copy-done.4), channel_id=1, source_target_pairs={{0,1},{1,0},{2,3},{3,2},{4,5},{5,4},{6,7},{7,6},{8,9},{9,8},{10,11... | collective-permute-start | bytes 393224 | tf_op jit(solution)/shard_map/ppermute | solution.py:50
  14.0 21.4 %collective-permute-start.3 = (bf16[272,128]{1,0:T(8,128)(2,1)S(1)}, bf16[272,128]{1,0:T(8,128)(2,1)S(1)}, u32[]{:S(2)}, u32[]{:S(2)}) collective-permute-start(bf16[272,128]{1,0:T(8,128)(2,1)S(1)} %head_block.2.refs_0_), channel_id=1, source_target_pairs={{0,12},{4,8},{8,4},{12,0},{1,13},{5,9},{9,5},{13,1},{2,14},{6,10},... | collective-permute-start | bytes 208904 | tf_op jit(solution)/shard_map/ppermute | solution.py:50
  18.3 11.2 %copy-start.5 = (s32[16]{0:T(128)S(1)}, s32[16]{0:T(128)}, u32[]{:S(2)}) copy-start(s32[16]{0:T(128)} %refs_1_.3) | copy-start | bytes 196
  18.3 11.1 %copy-start.6 = (s32[16]{0:T(128)S(1)}, s32[16]{0:T(128)}, u32[]{:S(2)}) copy-start(s32[16]{0:T(128)} %refs_2_.2) | copy-start | bytes 196
  18.3 11.8 %copy-start = (bf16[2,1024,4,128]{3,2,1,0:T(4,128)(2,1)S(1)}, bf16[2,1024,4,128]{3,2,1,0:T(4,128)(2,1)}, u32[]{:S(2)}) copy-start(bf16[2,1024,4,128]{3,2,1,0:T(4,128)(2,1)} %param.10) | copy-start | bytes 6291460
  18.3 11.8 %copy-start.1 = (bf16[2,1024,4,128]{3,2,1,0:T(4,128)(2,1)S(1)}, bf16[2,1024,4,128]{3,2,1,0:T(4,128)(2,1)}, u32[]{:S(2)}) copy-start(bf16[2,1024,4,128]{3,2,1,0:T(4,128)(2,1)} %param.11) | copy-start | bytes 6291460
  18.4 21.5 %collective-permute-start.9 = (bf16[272,128]{1,0:T(8,128)(2,1)S(1)}, bf16[272,128]{1,0:T(8,128)(2,1)S(1)}, u32[]{:S(2)}, u32[]{:S(2)}) collective-permute-start(bf16[272,128]{1,0:T(8,128)(2,1)S(1)} %head_block.3.refs_0_), channel_id=1, source_target_pairs={{0,12},{4,8},{8,4},{12,0},{1,13},{5,9},{9,5},{13,1},{2,14},{6,10},... | collective-permute-start | bytes 208904 | tf_op jit(solution)/shard_map/ppermute | solution.py:50
  23.0 16.9 %collective-permute-start.8 = (bf16[528,128]{1,0:T(8,128)(2,1)S(1)}, bf16[528,128]{1,0:T(8,128)(2,1)S(1)}, u32[]{:S(2)}, u32[]{:S(2)}) collective-permute-start(bf16[528,128]{1,0:T(8,128)(2,1)S(1)} %root_blocks.2.refs_0_), channel_id=1, source_target_pairs={{0,4},{4,0},{8,12},{12,8},{1,5},{5,1},{9,13},{13,9},{2,6},{6,2},{1... | collective-permute-start | bytes 405512 | tf_op jit(solution)/shard_map/ppermute | solution.py:50
  26.4 14.3 %collective-permute-start.10 = (bf16[528,128]{1,0:T(8,128)(2,1)S(1)}, bf16[528,128]{1,0:T(8,128)(2,1)S(1)}, u32[]{:S(2)}, u32[]{:S(2)}) collective-permute-start(bf16[528,128]{1,0:T(8,128)(2,1)S(1)} %root_blocks.3.refs_0_), channel_id=1, source_target_pairs={{0,8},{4,12},{8,0},{12,4},{1,9},{5,13},{9,1},{13,5},{2,10},{6,14},... | collective-permute-start | bytes 405512 | tf_op jit(solution)/shard_map/ppermute | solution.py:50
  35.2 4.6 %collective-permute-start.7 = (bf16[528,128]{1,0:T(8,128)(2,1)S(1)}, bf16[528,128]{1,0:T(8,128)(2,1)S(1)}, u32[]{:S(2)}, u32[]{:S(2)}) collective-permute-start(bf16[528,128]{1,0:T(8,128)(2,1)S(1)} %get-tuple-element.22), channel_id=1, source_target_pairs={{0,1},{1,0},{2,3},{3,2},{4,5},{5,4},{6,7},{7,6},{8,9},{9,8},{10,11... | collective-permute-start | bytes 405512 | tf_op jit(solution)/shard_map/ppermute | solution.py:50

commit v8 on v6

--- a/solution.py
+++ b/solution.py
@@ -465,7 +465,7 @@
     for far, near in groups:
         arrived[far], own = lax.optimization_barrier((arrived[far], own))
         arrived[near] = exchange(arrived[far], "blk", 1)
-    order = sorted(arrived, key=lambda apart: (apart % 2 == 0, -apart))
+    order = sorted(arrived, reverse=True)
     returned, previous = {}, ()
     for apart in order:
         previous = root_blocks([arrived[apart]], keys, values, scale, previous)
@@ -479,7 +479,7 @@
     )
     from_partner = exchange(theirs, "pair", 1)
     mine = mine_block(limits, queries, held_keys, held_values, [own], scale, heads)
-    last = returned.pop(order[-1])
+    last = returned.pop(min(order, key=lambda apart: abs(apart - 2)))
     parts = [mine, from_partner, *returned.values()]
     sums, levels = gather_partials(parts, heads, requests, group_size)
     return merge_last(sums, levels, last, requests, group_size)

time: 39 us -> 40 us (1.026)
  starting transfers between devices: 12.2 us -> 13.4 us
    ppermute x10, starting transfers between devices: 12.2 us -> 13.4 us  [exchange(): lax.ppermute(value, axis, [(i, i ^ apart) for i in range(lax.axis_size(ax...]
  transfers between devices with their start and end apart: 10 -> 10, of which waited for: 1 -> 0; matrix products, arithmetic and copies ran while one was open for 0% -> 0% of each run, Pallas kernels for 65% -> 63%
where the time goes in v8:
time: 40 us; the launch traced here: 39.9 us
  Pallas kernels  26.2 us (66%)
  starting transfers between devices  13.4 us (34%)
    ppermute x10, starting transfers between devices, exchange(): lax.ppermute(value, axis, [(i, i ^ apart) for i in range(lax.axis_size(ax...  13.4 us
    pallas_call x3, Pallas kernels, root_blocks(): pl.pallas_call(ordered(functools.partial(root_kernel, scale, len(queries)...  9.68 us
    pallas_call x1, Pallas kernels, theirs_block(): pl.pallas_call(ordered(functools.partial(theirs_kernel, scale, heads), af...  5.17 us
    pallas_call x1, Pallas kernels, mine_block(): pl.pallas_call(functools.partial(mine_kernel, scale, heads), out_shape=pa...  4.54 us
    pallas_call x1, Pallas kernels, first_block(): pl.pallas_call(ordered(functools.partial(first_kernel, scale, shared), af...  4.34 us
    pallas_call x1, Pallas kernels, merge_last(): pl.pallas_call(functools.partial(last_kernel, requests, group_size), out_...  0.96 us
    pallas_call x1, Pallas kernels, gather_partials(): pl.pallas_call(functools.partial(gather_kernel, requests, group_size), ou...  0.87 us
  transfers between devices with their start and end apart: 10, of which 0 were waited for; matrix products, arithmetic and copies ran while one was open for 0% of the time, Pallas kernels for 63%

profile of v8, /device:TPU:0, one launch (start us, length us, event | category | flops | bytes accessed | tf_op | source)
XLA Modules:
  0.0 39.9 jit_solution(9998910184425070439)
XLA Ops:
  0.0 0.5 %collective-permute-start = (bf16[1024,4,128]{2,1,0:T(4,128)(2,1)}, bf16[1024,4,128]{2,1,0:T(4,128)(2,1)S(1)}, u32[]{:S(2)}, u32[]{:S(2)}) collective-permute-start(bf16[1024,4,128]{2,1,0:T(4,128)(2,1)} %param.8), channel_id=1, source_target_pairs={{0,1},{1,0},{2,3},{3,2},{4,5},{5,4},{6,7},{7,6},{8,9},{9,8},{10,11... | collective-permute-start | bytes 3145736 | tf_op jit(solution)/shard_map/ppermute | solution.py:50
  0.5 0.1 collective-permute-start.1
  0.6 5.0 %collective-permute-start.2 = (bf16[16,32,128]{2,1,0:T(8,128)(2,1)}, bf16[16,32,128]{2,1,0:T(8,128)(2,1)S(1)}, u32[]{:S(2)}, u32[]{:S(2)}) collective-permute-start(bf16[16,32,128]{2,1,0:T(8,128)(2,1)} %query_ref.1), channel_id=1, source_target_pairs={{0,12},{4,8},{8,4},{12,0},{1,13},{5,9},{9,5},{13,1},{2,14},{6,10},... | collective-permute-start | bytes 393224 | tf_op jit(solution)/shard_map/ppermute | solution.py:50
  5.6 0.0 collective-permute-done
  5.6 0.0 collective-permute-done.1
  5.7 4.3 %first_block.1 = (bf16[2,2048,128]{2,1,0:T(8,128)(2,1)S(1)}, bf16[2,2048,128]{2,1,0:T(8,128)(2,1)S(1)}, bf16[528,128]{1,0:T(8,128)(2,1)S(1)}) custom-call(f32[8,128]{1,0:T(8,128)S(1)} %mark.1.refs_0_, bf16[16,32,128]{2,1,0:T(8,128)(2,1)S(1)} %copy-done.4, bf16[4096,128]{1,0:T(8,128)(2,1)S(1)} %bitcast.8, bf16[4096,128]{1,0:T(8,128)(2,1)S(1)} %bitcast.9, ...), custom_call_target="tpu_custom_call" | custom-call | flops 1 | bytes 1 | tf_op jit(solution)/shard_map/first_block/pallas_call | solution.py:263
  10.0 2.1 %collective-permute-start.3 = (bf16[16,32,128]{2,1,0:T(8,128)(2,1)S(1)}, bf16[16,32,128]{2,1,0:T(8,128)(2,1)S(1)}, u32[]{:S(2)}, u32[]{:S(2)}) collective-permute-start(bf16[16,32,128]{2,1,0:T(8,128)(2,1)S(1)} %collective-permute-done.2.refs_2_), channel_id=1, source_target_pairs={{0,4},{4,0},{8,12},{12,8},{1,5},{5,1},{9,13},{13,9},{2,6},{6,2},{1... | collective-permute-start | bytes 393224 | tf_op jit(solution)/shard_map/ppermute | solution.py:50
  12.1 0.0 collective-permute-start.4
  12.1 3.2 %root_blocks.3.refs_0_ = bf16[528,128]{1,0:T(8,128)(2,1)S(1)} custom-call(bf16[2,2048,128]{2,1,0:T(8,128)(2,1)S(1)} %get-tuple-element.15.refs_0_.refs_1_, bf16[2,2048,128]{2,1,0:T(8,128)(2,1)S(1)} %get-tuple-element.16.refs_1_.refs_2_, bf16[16,32,128]{2,1,0:T(8,128)(2,1)S(1)} %collective-permute-done.2.refs_2_), custom_call_target="tpu_custom_call" | custom-call | flops 1 | bytes 1 | tf_op jit(solution)/shard_map/root_blocks/pallas_call | solution.py:328
  15.3 0.0 copy-start.5
  15.3 0.0 copy-start.6
  15.3 0.0 copy-start
  15.4 0.0 copy-start.1
  15.4 3.9 %collective-permute-start.7 = (bf16[528,128]{1,0:T(8,128)(2,1)S(1)}, bf16[528,128]{1,0:T(8,128)(2,1)S(1)}, u32[]{:S(2)}, u32[]{:S(2)}) collective-permute-start(bf16[528,128]{1,0:T(8,128)(2,1)S(1)} %root_blocks.3.refs_0_), channel_id=1, source_target_pairs={{0,12},{4,8},{8,4},{12,0},{1,13},{5,9},{9,5},{13,1},{2,14},{6,10},... | collective-permute-start | bytes 405512 | tf_op jit(solution)/shard_map/ppermute | solution.py:50
  19.2 3.2 %root_blocks.4.refs_0_ = bf16[528,128]{1,0:T(8,128)(2,1)S(1)} custom-call(bf16[528,128]{1,0:T(8,128)(2,1)S(1)} %root_blocks.3.refs_0_, bf16[2,2048,128]{2,1,0:T(8,128)(2,1)S(1)} %get-tuple-element.15.refs_0_.refs_1_, bf16[2,2048,128]{2,1,0:T(8,128)(2,1)S(1)} %get-tuple-element.16.refs_1_.refs_2_, bf16[16,32,128]{2,1,0:T(8,128)(2,1)S(1)} %collective-permute-done.3.refs_3_), custom_call_target="tpu_custom_call" | custom-call | flops 1 | bytes 1 | tf_op jit(solution)/shard_map/root_blocks/pallas_call | solution.py:328
  22.4 0.3 collective-permute-start.9
  22.7 3.3 %root_blocks.5.refs_0_ = bf16[528,128]{1,0:T(8,128)(2,1)S(1)} custom-call(bf16[528,128]{1,0:T(8,128)(2,1)S(1)} %root_blocks.4.refs_0_, bf16[2,2048,128]{2,1,0:T(8,128)(2,1)S(1)} %get-tuple-element.15.refs_0_.refs_1_, bf16[2,2048,128]{2,1,0:T(8,128)(2,1)S(1)} %get-tuple-element.16.refs_1_.refs_2_, bf16[16,32,128]{2,1,0:T(8,128)(2,1)S(1)} %collective-permute-done.4.refs_3_), custom_call_target="tpu_custom_call" | custom-call | flops 1 | bytes 1 | tf_op jit(solution)/shard_map/root_blocks/pallas_call | solution.py:328
  26.1 1.4 %collective-permute-start.8 = (bf16[528,128]{1,0:T(8,128)(2,1)S(1)}, bf16[528,128]{1,0:T(8,128)(2,1)S(1)}, u32[]{:S(2)}, u32[]{:S(2)}) collective-permute-start(bf16[528,128]{1,0:T(8,128)(2,1)S(1)} %root_blocks.5.refs_0_), channel_id=1, source_target_pairs={{0,4},{4,0},{8,12},{12,8},{1,5},{5,1},{9,13},{13,9},{2,6},{6,2},{1... | collective-permute-start | bytes 405512 | tf_op jit(solution)/shard_map/ppermute | solution.py:50
  27.5 0.6 %limits_block.1.refs_1_.limit_ref = s32[2,256,128]{2,1,0:T(8,128)S(1)} custom-call(bf16[528,128]{1,0:T(8,128)(2,1)S(1)} %root_blocks.5.refs_0_, s32[16]{0:T(128)S(1)} %copy-done.5, s32[16]{0:T(128)S(1)} %copy-done.6), custom_call_target="tpu_custom_call" | custom-call | flops 1 | bytes 1 | tf_op jit(solution)/shard_map/limits_block/pallas_call | solution.py:290
  28.2 5.2 %theirs_block.1 = (bf16[528,128]{1,0:T(8,128)(2,1)S(1)}, bf16[4,2048,128]{2,1,0:T(8,128)(2,1)S(1)}, bf16[4,2048,128]{2,1,0:T(8,128)(2,1)S(1)}) custom-call(bf16[528,128]{1,0:T(8,128)(2,1)S(1)} %root_blocks.5.refs_0_, s32[2,256,128]{2,1,0:T(8,128)S(1)} %limits_block.1.refs_1_.limit_ref, bf16[16,32,128]{2,1,0:T(8,128)(2,1)S(1)} %collective-permute-done.5.refs_2_, ...), custom_call_target="tpu_custom_call" | custom-call | flops 1 | bytes 1 | tf_op jit(solution)/shard_map/theirs_block/pallas_call | solution.py:376
  33.4 0.1 collective-permute-start.6
  33.4 4.5 %mine_block.1.refs_0_ = bf16[528,128]{1,0:T(8,128)(2,1)S(1)} custom-call(s32[2,256,128]{2,1,0:T(8,128)S(1)} %limits_block.1.refs_1_.limit_ref, bf16[16,32,128]{2,1,0:T(8,128)(2,1)S(1)} %copy-done.4, bf16[4,2048,128]{2,1,0:T(8,128)(2,1)S(1)} %get-tuple-element.19.k_ref, bf16[4,2048,128]{2,1,0:T(8,128)(2,1)S(1)} %get-tuple-element.20.v_ref, ...), custom_call_target="tpu_custom_call" | custom-call | flops 10000000000 | bytes 1 | tf_op jit(solution)/shard_map/mine_block/pallas_call | solution.py:389
  38.0 0.9 %gather_partials.1 = (f32[2,256,128]{2,1,0:T(8,128)S(1)}, f32[2,256,128]{2,1,0:T(8,128)S(1)}) custom-call(bf16[528,128]{1,0:T(8,128)(2,1)S(1)} %mine_block.1.refs_0_, bf16[528,128]{1,0:T(8,128)(2,1)S(1)} %collective-permute-done.6.refs_1_, bf16[528,128]{1,0:T(8,128)(2,1)S(1)} %collective-permute-done.7.refs_2_, ...), custom_call_target="tpu_custom_call" | custom-call | flops 1 | bytes 1 | tf_op jit(solution)/shard_map/gather_partials/pallas_call | solution.py:413
  38.9 1.0 %merge_last.1 = bf16[16,32,128]{2,1,0:T(8,128)(2,1)} custom-call(f32[2,256,128]{2,1,0:T(8,128)S(1)} %get-tuple-element.23.sums_ref, f32[2,256,128]{2,1,0:T(8,128)S(1)} %get-tuple-element.24.level_ref, bf16[528,128]{1,0:T(8,128)(2,1)S(1)} %collective-permute-done.9.back_ref), custom_call_target="tpu_custom_call" | custom-call | flops 1 | bytes 1 | tf_op jit(solution)/shard_map/merge_last/pallas_call | solution.py:436
  (20 shorter events, 0.0 us)
Async XLA Ops:
  0.0 5.6 %copy-start.2 = (bf16[1024,4,128]{2,1,0:T(4,128)(2,1)S(1)}, bf16[1024,4,128]{2,1,0:T(4,128)(2,1)}, u32[]{:S(2)}) copy-start(bf16[1024,4,128]{2,1,0:T(4,128)(2,1)} %param.8) | copy-start | bytes 3145732
  0.0 5.7 %copy-start.3 = (bf16[1024,4,128]{2,1,0:T(4,128)(2,1)S(1)}, bf16[1024,4,128]{2,1,0:T(4,128)(2,1)}, u32[]{:S(2)}) copy-start(bf16[1024,4,128]{2,1,0:T(4,128)(2,1)} %param.9) | copy-start | bytes 3145732
  0.0 5.7 %copy-start.4 = (bf16[16,32,128]{2,1,0:T(8,128)(2,1)S(1)}, bf16[16,32,128]{2,1,0:T(8,128)(2,1)}, u32[]{:S(2)}) copy-start(bf16[16,32,128]{2,1,0:T(8,128)(2,1)} %query_ref.1) | copy-start | bytes 393220
  0.0 5.6 %collective-permute-start = (bf16[1024,4,128]{2,1,0:T(4,128)(2,1)}, bf16[1024,4,128]{2,1,0:T(4,128)(2,1)S(1)}, u32[]{:S(2)}, u32[]{:S(2)}) collective-permute-start(bf16[1024,4,128]{2,1,0:T(4,128)(2,1)} %param.8), channel_id=1, source_target_pairs={{0,1},{1,0},{2,3},{3,2},{4,5},{5,4},{6,7},{7,6},{8,9},{9,8},{10,11... | collective-permute-start | bytes 3145736 | tf_op jit(solution)/shard_map/ppermute | solution.py:50
  0.5 5.1 %collective-permute-start.1 = (bf16[1024,4,128]{2,1,0:T(4,128)(2,1)}, bf16[1024,4,128]{2,1,0:T(4,128)(2,1)S(1)}, u32[]{:S(2)}, u32[]{:S(2)}) collective-permute-start(bf16[1024,4,128]{2,1,0:T(4,128)(2,1)} %param.9), channel_id=1, source_target_pairs={{0,1},{1,0},{2,3},{3,2},{4,5},{5,4},{6,7},{7,6},{8,9},{9,8},{10,11... | collective-permute-start | bytes 3145736 | tf_op jit(solution)/shard_map/ppermute | solution.py:50
  0.6 9.4 %collective-permute-start.2 = (bf16[16,32,128]{2,1,0:T(8,128)(2,1)}, bf16[16,32,128]{2,1,0:T(8,128)(2,1)S(1)}, u32[]{:S(2)}, u32[]{:S(2)}) collective-permute-start(bf16[16,32,128]{2,1,0:T(8,128)(2,1)} %query_ref.1), channel_id=1, source_target_pairs={{0,12},{4,8},{8,4},{12,0},{1,13},{5,9},{9,5},{13,1},{2,14},{6,10},... | collective-permute-start | bytes 393224 | tf_op jit(solution)/shard_map/ppermute | solution.py:50
  10.0 9.2 %collective-permute-start.3 = (bf16[16,32,128]{2,1,0:T(8,128)(2,1)S(1)}, bf16[16,32,128]{2,1,0:T(8,128)(2,1)S(1)}, u32[]{:S(2)}, u32[]{:S(2)}) collective-permute-start(bf16[16,32,128]{2,1,0:T(8,128)(2,1)S(1)} %collective-permute-done.2.refs_2_), channel_id=1, source_target_pairs={{0,4},{4,0},{8,12},{12,8},{1,5},{5,1},{9,13},{13,9},{2,6},{6,2},{1... | collective-permute-start | bytes 393224 | tf_op jit(solution)/shard_map/ppermute | solution.py:50
  12.1 10.6 %collective-permute-start.4 = (bf16[16,32,128]{2,1,0:T(8,128)(2,1)S(1)}, bf16[16,32,128]{2,1,0:T(8,128)(2,1)S(1)}, u32[]{:S(2)}, u32[]{:S(2)}) collective-permute-start(bf16[16,32,128]{2,1,0:T(8,128)(2,1)S(1)} %copy-done.4), channel_id=1, source_target_pairs={{0,4},{4,0},{8,12},{12,8},{1,5},{5,1},{9,13},{13,9},{2,6},{6,2},{1... | collective-permute-start | bytes 393224 | tf_op jit(solution)/shard_map/ppermute | solution.py:50
  12.1 16.0 %collective-permute-start.5 = (bf16[16,32,128]{2,1,0:T(8,128)(2,1)S(1)}, bf16[16,32,128]{2,1,0:T(8,128)(2,1)S(1)}, u32[]{:S(2)}, u32[]{:S(2)}) collective-permute-start(bf16[16,32,128]{2,1,0:T(8,128)(2,1)S(1)} %copy-done.4), channel_id=1, source_target_pairs={{0,1},{1,0},{2,3},{3,2},{4,5},{5,4},{6,7},{7,6},{8,9},{9,8},{10,11... | collective-permute-start | bytes 393224 | tf_op jit(solution)/shard_map/ppermute | solution.py:50
  15.3 12.2 %copy-start.5 = (s32[16]{0:T(128)S(1)}, s32[16]{0:T(128)}, u32[]{:S(2)}) copy-start(s32[16]{0:T(128)} %refs_1_.3) | copy-start | bytes 196
  15.3 12.2 %copy-start.6 = (s32[16]{0:T(128)S(1)}, s32[16]{0:T(128)}, u32[]{:S(2)}) copy-start(s32[16]{0:T(128)} %refs_2_.1) | copy-start | bytes 196
  15.3 12.8 %copy-start = (bf16[2,1024,4,128]{3,2,1,0:T(4,128)(2,1)S(1)}, bf16[2,1024,4,128]{3,2,1,0:T(4,128)(2,1)}, u32[]{:S(2)}) copy-start(bf16[2,1024,4,128]{3,2,1,0:T(4,128)(2,1)} %param.10) | copy-start | bytes 6291460
  15.4 12.8 %copy-start.1 = (bf16[2,1024,4,128]{3,2,1,0:T(4,128)(2,1)S(1)}, bf16[2,1024,4,128]{3,2,1,0:T(4,128)(2,1)}, u32[]{:S(2)}) copy-start(bf16[2,1024,4,128]{3,2,1,0:T(4,128)(2,1)} %param.11) | copy-start | bytes 6291460
  15.4 22.6 %collective-permute-start.7 = (bf16[528,128]{1,0:T(8,128)(2,1)S(1)}, bf16[528,128]{1,0:T(8,128)(2,1)S(1)}, u32[]{:S(2)}, u32[]{:S(2)}) collective-permute-start(bf16[528,128]{1,0:T(8,128)(2,1)S(1)} %root_blocks.3.refs_0_), channel_id=1, source_target_pairs={{0,12},{4,8},{8,4},{12,0},{1,13},{5,9},{9,5},{13,1},{2,14},{6,10},... | collective-permute-start | bytes 405512 | tf_op jit(solution)/shard_map/ppermute | solution.py:50
  22.4 16.5 %collective-permute-start.9 = (bf16[528,128]{1,0:T(8,128)(2,1)S(1)}, bf16[528,128]{1,0:T(8,128)(2,1)S(1)}, u32[]{:S(2)}, u32[]{:S(2)}) collective-permute-start(bf16[528,128]{1,0:T(8,128)(2,1)S(1)} %root_blocks.4.refs_0_), channel_id=1, source_target_pairs={{0,8},{4,12},{8,0},{12,4},{1,9},{5,13},{9,1},{13,5},{2,10},{6,14},... | collective-permute-start | bytes 405512 | tf_op jit(solution)/shard_map/ppermute | solution.py:50
  26.1 11.9 %collective-permute-start.8 = (bf16[528,128]{1,0:T(8,128)(2,1)S(1)}, bf16[528,128]{1,0:T(8,128)(2,1)S(1)}, u32[]{:S(2)}, u32[]{:S(2)}) collective-permute-start(bf16[528,128]{1,0:T(8,128)(2,1)S(1)} %root_blocks.5.refs_0_), channel_id=1, source_target_pairs={{0,4},{4,0},{8,12},{12,8},{1,5},{5,1},{9,13},{13,9},{2,6},{6,2},{1... | collective-permute-start | bytes 405512 | tf_op jit(solution)/shard_map/ppermute | solution.py:50
  33.4 4.6 %collective-permute-start.6 = (bf16[528,128]{1,0:T(8,128)(2,1)S(1)}, bf16[528,128]{1,0:T(8,128)(2,1)S(1)}, u32[]{:S(2)}, u32[]{:S(2)}) collective-permute-start(bf16[528,128]{1,0:T(8,128)(2,1)S(1)} %get-tuple-element.22), channel_id=1, source_target_pairs={{0,1},{1,0},{2,3},{3,2},{4,5},{5,4},{6,7},{7,6},{8,9},{9,8},{10,11... | collective-permute-start | bytes 405512 | tf_op jit(solution)/shard_map/ppermute | solution.py:50
